TPU v7x, 32 devices: a whole 2x2x4 slice. The times are simulated.
32 devices in a mesh: energy: 2 (over x), momentum: 4 (over z), atom: 4 (over y, core).
Axes of the slice: x: 2, y: 2, z: 4, core: 2. Of those that a mesh axis runs over, the one named last changes fastest.
Arguments:
- green: bfloat16 [16, 32, 288, 256], P('momentum', 'atom', None, 'energy'), may hold values from -6 to 6
- neighbours: int32 [32, 8], P('atom'), may hold values from 0 to 31, as said below
- offsets: int32 [16], replicated, may hold values from 1 to 32, as said below
- emit_weight: bfloat16 [16, 16], replicated, may hold values from 0.0099487305 to 0.099609375
- absorb_weight: bfloat16 [16, 16], replicated, may hold values from 0.0099487305 to 0.099609375
- coupling: bfloat16 [32, 8, 12, 12], P('atom'), may hold values from -1.75 to 1.75
Outputs:
- selfenergy: float32 [16, 32, 288, 256], P('momentum', 'atom', None, 'energy')
Inputs may be any that keep to these rules, and one draw needn't show every extreme that they name: `neighbours`: every entry lies within 2 of its own atom index, and some entry lies exactly 2 above it. `offsets`: all entries are distinct, and one of them equals 32.
All inputs are finite; a program needn't handle non-finite values.
Results may differ from a plain program's by a relative error of at most 0.0041.
Values may be sent and summed in bfloat16 or wider, within the bound.
No kernel may reach another device: no remote copies, remote signals or barrier semaphores. Data moves between devices by JAX's collectives and lax.ppermute only.
A program may use at most 128 MiB of HBM per device.

v0:
```python
import jax
import jax.numpy as jnp
from jax import lax
from jax.sharding import PartitionSpec as P

ORB = 12
NB = 8
SMAX = 32
REACH = 2


def with_halo(cells, sides, width):
    for axis, dim in sides:
        count = lax.axis_size(axis)
        ends = count - 1
        head = lax.slice_in_dim(cells, 0, width, axis=dim)
        tail = lax.slice_in_dim(cells, cells.shape[dim] - width, cells.shape[dim], axis=dim)
        cells = jnp.concatenate(
            [
                lax.ppermute(tail, axis, [(i, (i + 1) % count) for i in range(ends)]),
                cells,
                lax.ppermute(head, axis, [((i + 1) % count, i) for i in range(ends)]),
            ],
            axis=dim,
        )
    return cells


def shards(green, neighbours, offsets, emit_weight, absorb_weight, coupling):
    k_count, a_count, components, e_count = green.shape
    extended = with_halo(green, (("energy", 3),), SMAX)
    padded_len = e_count + 2 * SMAX
    k_total = k_count * lax.axis_size("momentum")
    source_pos = jnp.arange(padded_len)[None, :, None]
    target_pos = jnp.arange(e_count)[None, None, :]
    emit_pick = (source_pos == target_pos + SMAX - offsets[:, None, None]).astype(jnp.float32)
    absorb_pick = (source_pos == target_pos + SMAX + offsets[:, None, None]).astype(jnp.float32)
    emit_full = emit_weight.astype(jnp.float32)
    absorb_full = absorb_weight.astype(jnp.float32)
    all_momenta = jnp.arange(k_total)
    lag_index = (all_momenta[:, None] - all_momenta[None, :]) % k_total
    lag_onehot = (lag_index[:, :, None] == jnp.arange(k_total)[None, None, :]).astype(jnp.float32)
    emit_coef = jnp.einsum("pqk,wk->pqw", lag_onehot, emit_full)
    absorb_coef = jnp.einsum("pqk,wk->pqw", lag_onehot, absorb_full)
    toeplitz_table = jnp.einsum("pqw,wfe->pqfe", emit_coef, emit_pick)
    toeplitz_table = toeplitz_table + jnp.einsum("pqw,wfe->pqfe", absorb_coef, absorb_pick)
    convolve_toeplitz_table = toeplitz_table.astype(jnp.bfloat16)
    summed = jnp.einsum(
        "qacf,pqfe->pace",
        lax.all_to_all(extended, "momentum", split_axis=1, concat_axis=0, tiled=True),
        convolve_toeplitz_table,
        preferred_element_type=jnp.float32,
    ).astype(jnp.bfloat16)
    hsum = lax.all_to_all(summed, "momentum", split_axis=0, concat_axis=1, tiled=True)
    hsum = with_halo(hsum, (("atom", 1),), REACH)
    a_first = lax.axis_index("atom") * a_count - REACH
    local_index = neighbours - a_first
    blocks = hsum.reshape(k_count, a_count + 2 * REACH, 2, ORB, ORB, e_count)

    def add_slot(slot_index, accumulated):
        column = lax.dynamic_index_in_dim(local_index, slot_index, 1, keepdims=False)
        chosen = jnp.take(blocks, column, axis=1)
        coupling_slot = lax.dynamic_index_in_dim(coupling, slot_index, 1, keepdims=False)
        half_block = jnp.einsum(
            "aij,kacjle->kacile", coupling_slot, chosen, preferred_element_type=jnp.float32
        ).astype(jnp.bfloat16)
        return accumulated + jnp.einsum(
            "kacile,ajl->kacije", half_block, coupling_slot, preferred_element_type=jnp.float32
        )

    zeros_out = jnp.zeros((k_count, a_count, 2, ORB, ORB, e_count), jnp.float32)
    accumulated = lax.fori_loop(0, NB, add_slot, zeros_out)
    return accumulated.reshape(k_count, a_count, components, e_count)


def solution(mesh):
    in_specs = (
        P("momentum", "atom", None, "energy"),
        P("atom", None),
        P(),
        P(),
        P(),
        P("atom", None, None, None),
    )
    out_specs = P("momentum", "atom", None, "energy")
    return jax.shard_map(shards, mesh=mesh, in_specs=in_specs, out_specs=out_specs, check_vma=False)
```

profile of v0, /device:TPU:9, one launch (start us, length us, event | category | flops | bytes accessed | tf_op | source)
XLA Modules:
  0.0 357.1 jit_solution(13717065916661174323)
XLA Ops:
  0.0 4.6 %fusion.42 = (bf16[4,8,288,32]{3,2,1,0:T(8,128)(2,1)S(1)}, bf16[4,8,288,32]{3,2,1,0:T(8,128)(2,1)}) fusion(bf16[4,8,288,128]{3,2,1,0:T(8,128)(2,1)} %param.8), kind=kLoop, calls=%fused_computation.51 | loop fusion | bytes 2359296 | tf_op jit(solution)/shard_map/slice | solution.py:17
  4.6 1.2 copy.49
  5.8 4.0 %collective-permute-start = (bf16[4,8,288,32]{2,3,1,0:T(8,128)(2,1)S(1)}, bf16[4,8,288,32]{2,3,1,0:T(8,128)(2,1)}, u32[]{:S(2)}, u32[]{:S(2)}) collective-permute-start(bf16[4,8,288,32]{2,3,1,0:T(8,128)(2,1)S(1)} %copy.49), channel_id=1, source_target_pairs={{0,16},{1,17},{2,18},{3,19},{4,20},{5,21},{6,22},{7,23},{8,24},{9,... | collective-permute-start | bytes 1769480 | tf_op jit(solution)/shard_map/ppermute | solution.py:20
  9.9 3.1 copy.50
  13.0 1.3 collective-permute-start.1
  14.2 10.9 %collective-permute-done = bf16[4,8,288,32]{2,3,1,0:T(8,128)(2,1)} collective-permute-done((bf16[4,8,288,32]{2,3,1,0:T(8,128)(2,1)S(1)}, bf16[4,8,288,32]{2,3,1,0:T(8,128)(2,1)}, u32[]{:S(2)}, u32[]{:S(2)}) %collective-permute-start) | collective-permute-done | bytes 589856 | tf_op jit(solution)/shard_map/ppermute | solution.py:20
  25.1 2.8 copy.27
  28.0 5.3 %collective-permute-done.1 = bf16[4,8,288,32]{2,3,1,0:T(8,128)(2,1)} collective-permute-done((bf16[4,8,288,32]{2,3,1,0:T(8,128)(2,1)}, bf16[4,8,288,32]{2,3,1,0:T(8,128)(2,1)}, u32[]{:S(2)}, u32[]{:S(2)}) %collective-permute-start.1) | collective-permute-done | bytes 589856 | tf_op jit(solution)/shard_map/ppermute | solution.py:22
  33.2 2.8 copy.29
  36.1 6.1 %pad_maximum_fusion = bf16[4,8,288,192]{3,2,0,1:T(8,128)(2,1)} fusion(bf16[4,8,288,32]{3,2,0,1:T(8,128)(2,1)} %copy.29, bf16[4,8,288,32]{3,2,0,1:T(8,128)(2,1)} %copy.27, bf16[4,8,288,128]{3,2,1,0:T(8,128)(2,1)S(1)} %copy-done.2), kind=kLoop, calls=%fused_computation.21 | loop fusion | flops 10616832 | bytes 7077888 | tf_op jit(solution)/shard_map/concatenate | solution.py:18
  42.2 5.3 %all-to-all-start = ((bf16[4,8,288,192]{3,2,0,1:T(8,128)(2,1)}), bf16[4,8,288,192]{3,2,0,1:T(8,128)(2,1)}, u32[]{:S(2)}, u32[]{:S(2)}) async-start(bf16[4,8,288,192]{3,2,0,1:T(8,128)(2,1)} %pad_maximum_fusion), calls=%async_computation | async-start | bytes 9437184 | tf_op jit(solution)/shard_map/all_to_all | solution.py:50
  47.5 0.2 convolution_bitcast_fusion
  47.8 10.3 %fusion.23 = f32[16,16,192,128]{3,1,2,0:T(8,128)} fusion(s32[16,128]{1,0:T(8,128)S(1)} %get-tuple-element.150, s32[16,16]{1,0:T(8,128)S(1)} %add_select_fusion, bf16[16,16]{1,0:T(8,128)(2,1)S(1)} %copy-done), kind=kOutput, calls=%fused_computation.28 | convolution fusion | flops 201854976 | bytes 25175552 | tf_op jit(solution)/shard_map/pqw,wfe->pqfe/dot_general | solution.py:45
  58.1 88.9 %all-to-all-done = bf16[4,8,288,192]{3,2,0,1:T(8,128)(2,1)} async-done(((bf16[4,8,288,192]{3,2,0,1:T(8,128)(2,1)}), bf16[4,8,288,192]{3,2,0,1:T(8,128)(2,1)}, u32[]{:S(2)}, u32[]{:S(2)}) %all-to-all-start) | async-done | bytes 3538976 | tf_op jit(solution)/shard_map/all_to_all | solution.py:50
  147.0 4.8 %copy.30 = bf16[4,4,2,288,192]{4,3,0,1,2:T(8,128)(2,1)} copy(bf16[4,4,2,288,192]{4,3,0,2,1:T(8,128)(2,1)} %bitcast.9) | data formatting | bytes 7077888 | tf_op jit(solution)/shard_map/all_to_all | solution.py:50
  151.8 8.4 %copy.44 = bf16[16,2,288,192,1]{2,0,3,1,4:T(8,128)(2,1)} copy(bf16[16,2,288,192,1]{3,2,0,1,4:T(8,128)(2,1)} %bitcast.90) | data formatting | bytes 7077888 | tf_op jit(solution)/shard_map/all_to_all | solution.py:50
  160.2 16.5 %fusion.19 = bf16[16,2,288,128]{3,2,1,0:T(8,128)(2,1)} fusion(bf16[16,2,288,192,1]{2,0,3,1,4:T(8,128)(2,1)} %copy.44, f32[16,16,192,128]{3,1,2,0:T(8,128)} %fusion.23, bf16[16,16,16,1]{2,1,3,0:T(8,128)(2,1)S(1)} %convolution_bitcast_fusion, s32[16,128]{1,0:T(8,128)S(1)} %get-tuple-element.149), kind=kOutput, calls=%fused_computation.24 | convolution fusion | flops 7463239680 | bytes 31080448 | tf_op jit(solution)/shard_map/qacf,pqfe->pace/dot_general | solution.py:48
  176.8 59.0 %all_to_all.36 = bf16[16,2,288,128]{3,2,1,0:T(8,128)(2,1)S(1)} all-to-all(bf16[16,2,288,128]{3,2,1,0:T(8,128)(2,1)} %fusion.19), channel_id=1, replica_groups=mesh['energy'=2,'momentum'=4,'atom'=4] {'momentum'}, dimensions={0} | all-to-all | bytes 4718592 | tf_op jit(solution)/shard_map/all_to_all | solution.py:54
  235.8 0.2 copy.32
  236.0 1.1 fusion.41
  237.1 5.3 %collective-permute-start.2 = (bf16[4,2,288,128]{3,2,1,0:T(8,128)(2,1)}, bf16[4,2,288,128]{3,2,1,0:T(8,128)(2,1)}, u32[]{:S(2)}, u32[]{:S(2)}) collective-permute-start(bf16[4,2,288,128]{3,2,1,0:T(8,128)(2,1)} %get-tuple-element.145), channel_id=1, source_target_pairs={{0,1},{1,2},{2,3},{4,5},{5,6},{6,7},{8,9},{9,10},{10,11},{12,13},{... | collective-permute-start | bytes 1769480 | tf_op jit(solution)/shard_map/ppermute | solution.py:20
  242.3 2.1 collective-permute-start.3
  244.6 1.8 copy.34
  246.4 3.0 collective-permute-done.2
  249.4 1.5 copy.33
  251.0 2.8 collective-permute-done.3
  253.7 0.5 copy.35
  254.2 3.2 pad_maximum_fusion.1
  257.4 3.5 copy.37
  260.9 87.7 %while.14 = (s32[]{:T(128)}, f32[4,8,2,12,12,128]{5,4,3,2,0,1:T(8,128)}, bf16[8,8,12,12]{3,2,0,1:T(8,128)(2,1)S(1)}, s32[8,8]{0,1:T(8,128)S(1)}, bf16[4,12,2,12,...) while((s32[]{:T(128)}, f32[4,8,2,12,12,128]{5,4,3,2,0,1:T(8,128)}, ...), condition=%wide.region_1.2_spmd.clone, body=%wide.region_0.1_spmd.clone.sunk | while | flops 61342768 | bytes 27594996 | solution.py:72
  260.9 3.5 gather_fusion
  264.4 0.4 select_bitcast_fusion.2
  264.8 1.0 convert_bitcast_fusion.2
  265.8 3.6 %bitcast_add_fusion.2 = f32[4,8,2,12,12,128]{5,4,3,2,0,1:T(8,128)} fusion(f32[4,8,2,12,12,128]{5,4,3,2,0,1:T(8,128)} %get-tuple-element.194, pred[]{:T(512)S(6)} %compare.7, bf16[4,8,2,12,12,128]{5,3,4,2,0,1:T(8,128)(2,1)S(1)} %convert_bitcast_fusion.2, bf16[8,8,12,12]{3,2,0,1:T(8,128)(2,1)S(1)} %get-tuple-element.202, s32[]{:T(128)} %get-tuple-element.193), kind=kOutput, calls=%fused_computation.1.clone.1 | convolution fusion | flops 30670848 | bytes 12615685 | tf_op jit(solution)/shard_map/while/body/eval_jaxpr/kacile,ajl->kacije/dot_general | solution.py:67
  269.4 3.5 gather_fusion
  272.9 0.4 select_bitcast_fusion.2
  273.3 1.0 convert_bitcast_fusion.2
  274.3 6.4 %bitcast_add_fusion.2 = f32[4,8,2,12,12,128]{5,4,3,2,0,1:T(8,128)} fusion(f32[4,8,2,12,12,128]{5,4,3,2,0,1:T(8,128)} %get-tuple-element.194, pred[]{:T(512)S(6)} %compare.7, bf16[4,8,2,12,12,128]{5,3,4,2,0,1:T(8,128)(2,1)S(1)} %convert_bitcast_fusion.2, bf16[8,8,12,12]{3,2,0,1:T(8,128)(2,1)S(1)} %get-tuple-element.202, s32[]{:T(128)} %get-tuple-element.193), kind=kOutput, calls=%fused_computation.1.clone.1 | convolution fusion | flops 30670848 | bytes 12615685 | tf_op jit(solution)/shard_map/while/body/eval_jaxpr/kacile,ajl->kacije/dot_general | solution.py:67
  280.8 3.5 gather_fusion
  284.3 0.4 select_bitcast_fusion.2
  284.6 1.0 convert_bitcast_fusion.2
  285.6 6.4 %bitcast_add_fusion.2 = f32[4,8,2,12,12,128]{5,4,3,2,0,1:T(8,128)} fusion(f32[4,8,2,12,12,128]{5,4,3,2,0,1:T(8,128)} %get-tuple-element.194, pred[]{:T(512)S(6)} %compare.7, bf16[4,8,2,12,12,128]{5,3,4,2,0,1:T(8,128)(2,1)S(1)} %convert_bitcast_fusion.2, bf16[8,8,12,12]{3,2,0,1:T(8,128)(2,1)S(1)} %get-tuple-element.202, s32[]{:T(128)} %get-tuple-element.193), kind=kOutput, calls=%fused_computation.1.clone.1 | convolution fusion | flops 30670848 | bytes 12615685 | tf_op jit(solution)/shard_map/while/body/eval_jaxpr/kacile,ajl->kacije/dot_general | solution.py:67
  292.1 3.5 gather_fusion
  295.6 0.4 select_bitcast_fusion.2
  295.9 1.0 convert_bitcast_fusion.2
  296.9 6.4 %bitcast_add_fusion.2 = f32[4,8,2,12,12,128]{5,4,3,2,0,1:T(8,128)} fusion(f32[4,8,2,12,12,128]{5,4,3,2,0,1:T(8,128)} %get-tuple-element.194, pred[]{:T(512)S(6)} %compare.7, bf16[4,8,2,12,12,128]{5,3,4,2,0,1:T(8,128)(2,1)S(1)} %convert_bitcast_fusion.2, bf16[8,8,12,12]{3,2,0,1:T(8,128)(2,1)S(1)} %get-tuple-element.202, s32[]{:T(128)} %get-tuple-element.193), kind=kOutput, calls=%fused_computation.1.clone.1 | convolution fusion | flops 30670848 | bytes 12615685 | tf_op jit(solution)/shard_map/while/body/eval_jaxpr/kacile,ajl->kacije/dot_general | solution.py:67
  303.4 3.5 gather_fusion
  306.9 0.4 select_bitcast_fusion.2
  307.2 1.0 convert_bitcast_fusion.2
  308.2 6.4 %bitcast_add_fusion.2 = f32[4,8,2,12,12,128]{5,4,3,2,0,1:T(8,128)} fusion(f32[4,8,2,12,12,128]{5,4,3,2,0,1:T(8,128)} %get-tuple-element.194, pred[]{:T(512)S(6)} %compare.7, bf16[4,8,2,12,12,128]{5,3,4,2,0,1:T(8,128)(2,1)S(1)} %convert_bitcast_fusion.2, bf16[8,8,12,12]{3,2,0,1:T(8,128)(2,1)S(1)} %get-tuple-element.202, s32[]{:T(128)} %get-tuple-element.193), kind=kOutput, calls=%fused_computation.1.clone.1 | convolution fusion | flops 30670848 | bytes 12615685 | tf_op jit(solution)/shard_map/while/body/eval_jaxpr/kacile,ajl->kacije/dot_general | solution.py:67
  314.7 3.5 gather_fusion
  318.2 0.4 select_bitcast_fusion.2
  318.6 1.0 convert_bitcast_fusion.2
  319.5 6.4 %bitcast_add_fusion.2 = f32[4,8,2,12,12,128]{5,4,3,2,0,1:T(8,128)} fusion(f32[4,8,2,12,12,128]{5,4,3,2,0,1:T(8,128)} %get-tuple-element.194, pred[]{:T(512)S(6)} %compare.7, bf16[4,8,2,12,12,128]{5,3,4,2,0,1:T(8,128)(2,1)S(1)} %convert_bitcast_fusion.2, bf16[8,8,12,12]{3,2,0,1:T(8,128)(2,1)S(1)} %get-tuple-element.202, s32[]{:T(128)} %get-tuple-element.193), kind=kOutput, calls=%fused_computation.1.clone.1 | convolution fusion | flops 30670848 | bytes 12615685 | tf_op jit(solution)/shard_map/while/body/eval_jaxpr/kacile,ajl->kacije/dot_general | solution.py:67
  326.0 3.5 gather_fusion
  329.5 0.4 select_bitcast_fusion.2
  329.9 1.0 convert_bitcast_fusion.2
  330.8 6.4 %bitcast_add_fusion.2 = f32[4,8,2,12,12,128]{5,4,3,2,0,1:T(8,128)} fusion(f32[4,8,2,12,12,128]{5,4,3,2,0,1:T(8,128)} %get-tuple-element.194, pred[]{:T(512)S(6)} %compare.7, bf16[4,8,2,12,12,128]{5,3,4,2,0,1:T(8,128)(2,1)S(1)} %convert_bitcast_fusion.2, bf16[8,8,12,12]{3,2,0,1:T(8,128)(2,1)S(1)} %get-tuple-element.202, s32[]{:T(128)} %get-tuple-element.193), kind=kOutput, calls=%fused_computation.1.clone.1 | convolution fusion | flops 30670848 | bytes 12615685 | tf_op jit(solution)/shard_map/while/body/eval_jaxpr/kacile,ajl->kacije/dot_general | solution.py:67
  337.3 3.5 gather_fusion
  340.8 0.4 select_bitcast_fusion.2
  341.2 1.0 convert_bitcast_fusion.2
  342.2 6.4 %bitcast_add_fusion.2 = f32[4,8,2,12,12,128]{5,4,3,2,0,1:T(8,128)} fusion(f32[4,8,2,12,12,128]{5,4,3,2,0,1:T(8,128)} %get-tuple-element.194, pred[]{:T(512)S(6)} %compare.7, bf16[4,8,2,12,12,128]{5,3,4,2,0,1:T(8,128)(2,1)S(1)} %convert_bitcast_fusion.2, bf16[8,8,12,12]{3,2,0,1:T(8,128)(2,1)S(1)} %get-tuple-element.202, s32[]{:T(128)} %get-tuple-element.193), kind=kOutput, calls=%fused_computation.1.clone.1 | convolution fusion | flops 30670848 | bytes 12615685 | tf_op jit(solution)/shard_map/while/body/eval_jaxpr/kacile,ajl->kacije/dot_general | solution.py:67
  348.6 5.5 %copy.38 = f32[4,8,2,12,12,128]{5,1,4,3,2,0:T(8,128)S(1)} copy(f32[4,8,2,12,12,128]{5,4,3,2,0,1:T(8,128)} %get-tuple-element.99) | data formatting | bytes 9437184 | tf_op jit(solution)/shard_map/while | solution.py:72
  354.1 3.0 copy.39
  (37 shorter events, 0.4 us)
Async XLA Ops:
  0.0 47.8 %copy-start = (bf16[16,16]{1,0:T(8,128)(2,1)S(1)}, bf16[16,16]{1,0:T(8,128)(2,1)}, u32[]{:S(2)}) copy-start(bf16[16,16]{1,0:T(8,128)(2,1)} %param.11) | copy-start | bytes 1540
  5.8 19.3 %collective-permute-start = (bf16[4,8,288,32]{2,3,1,0:T(8,128)(2,1)S(1)}, bf16[4,8,288,32]{2,3,1,0:T(8,128)(2,1)}, u32[]{:S(2)}, u32[]{:S(2)}) collective-permute-start(bf16[4,8,288,32]{2,3,1,0:T(8,128)(2,1)S(1)} %copy.49), channel_id=1, source_target_pairs={{0,16},{1,17},{2,18},{3,19},{4,20},{5,21},{6,22},{7,23},{8,24},{9,... | collective-permute-start | bytes 1769480 | tf_op jit(solution)/shard_map/ppermute | solution.py:20
  9.8 26.2 %copy-start.2 = (bf16[4,8,288,128]{3,2,1,0:T(8,128)(2,1)S(1)}, bf16[4,8,288,128]{3,2,1,0:T(8,128)(2,1)}, u32[]{:S(2)}) copy-start(bf16[4,8,288,128]{3,2,1,0:T(8,128)(2,1)} %param.8) | copy-start | bytes 7077892
  13.0 20.3 %collective-permute-start.1 = (bf16[4,8,288,32]{2,3,1,0:T(8,128)(2,1)}, bf16[4,8,288,32]{2,3,1,0:T(8,128)(2,1)}, u32[]{:S(2)}, u32[]{:S(2)}) collective-permute-start(bf16[4,8,288,32]{2,3,1,0:T(8,128)(2,1)} %copy.50), channel_id=1, source_target_pairs={{16,0},{17,1},{18,2},{19,3},{20,4},{21,5},{22,6},{23,7},{24,8},{25... | collective-permute-start | bytes 1769480 | tf_op jit(solution)/shard_map/ppermute | solution.py:22
  42.2 5.3 %copy-start.6 = (bf16[16,16]{1,0:T(8,128)(2,1)S(1)}, bf16[16,16]{1,0:T(8,128)(2,1)}, u32[]{:S(2)}) copy-start(bf16[16,16]{1,0:T(8,128)(2,1)} %param.12) | copy-start | bytes 1540
  42.2 5.6 %copy-start.5 = (s32[16]{0:T(128)S(1)}, s32[16]{0:T(128)}, u32[]{:S(2)}) copy-start(s32[16]{0:T(128)} %param.10) | copy-start | bytes 196
  42.2 104.9 %all-to-all-start = ((bf16[4,8,288,192]{3,2,0,1:T(8,128)(2,1)}), bf16[4,8,288,192]{3,2,0,1:T(8,128)(2,1)}, u32[]{:S(2)}, u32[]{:S(2)}) async-start(bf16[4,8,288,192]{3,2,0,1:T(8,128)(2,1)} %pad_maximum_fusion), calls=%async_computation | async-start | bytes 9437184 | tf_op jit(solution)/shard_map/all_to_all | solution.py:50
  235.8 8.7 %copy-start.3 = (bf16[8,8,12,12]{3,1,2,0:T(8,128)(2,1)S(1)}, bf16[8,8,12,12]{3,1,2,0:T(8,128)(2,1)}, u32[]{:S(2)}) copy-start(bf16[8,8,12,12]{3,1,2,0:T(8,128)(2,1)} %param.13) | copy-start | bytes 55300
  235.8 8.7 %copy-start.4 = (s32[8,8]{1,0:T(8,128)S(1)}, s32[8,8]{1,0:T(8,128)}, u32[]{:S(2)}) copy-start(s32[8,8]{1,0:T(8,128)} %param.9) | copy-start | bytes 772
  237.1 12.4 %collective-permute-start.2 = (bf16[4,2,288,128]{3,2,1,0:T(8,128)(2,1)}, bf16[4,2,288,128]{3,2,1,0:T(8,128)(2,1)}, u32[]{:S(2)}, u32[]{:S(2)}) collective-permute-start(bf16[4,2,288,128]{3,2,1,0:T(8,128)(2,1)} %get-tuple-element.145), channel_id=1, source_target_pairs={{0,1},{1,2},{2,3},{4,5},{5,6},{6,7},{8,9},{9,10},{10,11},{12,13},{... | collective-permute-start | bytes 1769480 | tf_op jit(solution)/shard_map/ppermute | solution.py:20
  242.3 11.4 %collective-permute-start.3 = (bf16[4,2,288,128]{3,2,1,0:T(8,128)(2,1)}, bf16[4,2,288,128]{3,2,1,0:T(8,128)(2,1)S(1)}, u32[]{:S(2)}, u32[]{:S(2)}) collective-permute-start(bf16[4,2,288,128]{3,2,1,0:T(8,128)(2,1)} %get-tuple-element.146), channel_id=1, source_target_pairs={{1,0},{2,1},{3,2},{5,4},{6,5},{7,6},{9,8},{10,9},{11,10},{13,12},{... | collective-permute-start | bytes 1769480 | tf_op jit(solution)/shard_map/ppermute | solution.py:22
  354.1 3.0 copy-start.1
where the time goes:
time: 361 us; the launch traced here: 357 us
  waiting for transfers between devices  111 us (31%)
  matrix products  83.5 us (23%)
  local copies, waits for them, and re-layouts  72.9 us (20%)
  blocking collectives  59 us (16%)
  starting transfers between devices  18 us (5%)
  other arithmetic  12.4 us (3%)
    all_to_all x1, waiting for transfers between devices, shards(): lax.all_to_all(extended, 'momentum', split_axis=1, concat_axis=0, tiled=T...  88.9 us
    all_to_all x1, blocking collectives, shards(): lax.all_to_all(summed, 'momentum', split_axis=0, concat_axis=1, tiled=True)  59 us
    dot_general x8, matrix products, add_slot(): jnp.einsum('kacile,ajl->kacije', half_block, coupling_slot, preferred_ele...  48.7 us
    gather x8, local copies, waits for them, and re-layouts, add_slot(): chosen = jnp.take(blocks, column, axis=1)  27.9 us
    dot_general x1, matrix products, shards(): jnp.einsum('qacf,pqfe->pace', lax.all_to_all(extended, 'momentum', split_...  16.5 us
    ppermute x2, waiting for transfers between devices, with_halo(): lax.ppermute(tail, axis, [(i, (i + 1) % count) for i in range(ends)])  13.9 us
    all_to_all x2, local copies, waits for them, and re-layouts, shards(): lax.all_to_all(extended, 'momentum', split_axis=1, concat_axis=0, tiled=T...  13.2 us
    dot_general x1, matrix products, shards(): toeplitz_table = jnp.einsum('pqw,wfe->pqfe', emit_coef, emit_pick)  10.3 us
  transfers between devices with their start and end apart: 5, of which 5 were waited for; matrix products, arithmetic and copies ran while one was open for 6% of the time, Pallas kernels for 0%

commit v1 on v0

v1 whole, which is shorter than its diff:
```python
import functools

import jax
import jax.numpy as jnp
from jax import lax
from jax.experimental import pallas as pl
from jax.experimental.pallas import tpu as pltpu
from jax.sharding import PartitionSpec as P

SMAX = 32
REACH = 2
BF = jnp.bfloat16
F32 = jnp.float32
VMEM_LIMIT = 16 * 1024 * 1024
PACK_LIMIT = 16 * 1024 * 1024


def params(limit=VMEM_LIMIT):
    return pltpu.CompilerParams(vmem_limit_bytes=limit)


def smem():
    return pl.BlockSpec(memory_space=pltpu.SMEM)


def vmem():
    return pl.BlockSpec(memory_space=pltpu.VMEM)


def anywhere():
    return pl.BlockSpec(memory_space=pl.ANY)


def token():
    return jax.ShapeDtypeStruct((8, 128), F32)


def cost(flops, nbytes):
    return pl.CostEstimate(flops=0, bytes_accessed=0, transcendentals=0)


def atom_of(turn, atoms):
    return jnp.where(turn < REACH, turn, jnp.where(turn < 2 * REACH, turn + atoms - 2 * REACH, turn - REACH))


def pack_kernel(group, nz, z_ref, green, *refs):
    outs, sems = refs[-nz - 1:-1], refs[-1]
    atoms = green.shape[1]
    copies = []
    for r in range(nz):
        atom = atom_of(group * nz + lax.rem(z_ref[0] + r, nz), atoms)
        copies.append(pltpu.make_async_copy(green.at[:, atom], outs[r], sems.at[r]))
    for copy in copies:
        copy.start()
    for copy in copies:
        copy.wait()


def pack(z, green, nz, group, waits):
    k, _, comps, energies = green.shape
    piece = jax.ShapeDtypeStruct((k, comps, energies), BF)
    return pl.pallas_call(
        functools.partial(pack_kernel, group, nz),
        out_shape=(piece,) * nz,
        in_specs=[smem(), pl.BlockSpec(memory_space=pltpu.HBM)] + [vmem()] * len(waits),
        out_specs=(anywhere(),) * nz,
        scratch_shapes=[pltpu.SemaphoreType.DMA((nz,))],
        compiler_params=params(PACK_LIMIT),
        cost_estimate=cost(0, nz * piece.size * 4),
    )(z, green, *waits)


def halo_kernel(nz, sides, base_ref, *refs):
    pieces, outs = refs[:nz], refs[-sides:]
    k, rows, energies = pieces[0].shape
    lanes = k * SMAX
    row = lax.broadcasted_iota(jnp.int32, (energies, lanes), 0)
    col = lax.broadcasted_iota(jnp.int32, (energies, lanes), 1)
    for side in range(sides):
        picks = [(row - base_ref[side] == col - kk * SMAX) & (col >= kk * SMAX) & (col < (kk + 1) * SMAX) for kk in range(k)]
        pick = jnp.concatenate([jnp.where(p, 1.0, 0.0) for p in picks], axis=0).astype(BF)
        for r in range(nz):
            wide = jnp.concatenate([pieces[r][kk] for kk in range(k)], axis=1)
            outs[side][r] = jnp.dot(wide, pick, preferred_element_type=F32).astype(BF)


def halo_pack(base, pieces, sides, waits):
    nz = len(pieces)
    k, rows, energies = pieces[0].shape
    out = jax.ShapeDtypeStruct((nz, rows, k * SMAX), BF)
    return pl.pallas_call(
        functools.partial(halo_kernel, nz, sides),
        out_shape=(out,) * sides,
        in_specs=[smem()] + [vmem()] * nz + [vmem()] * len(waits),
        out_specs=(vmem(),) * sides,
        compiler_params=params(),
        cost_estimate=cost(2 * sides * out.size * k * energies, nz * pieces[0].size * 2),
    )(base, *pieces, *waits)


def table_kernel(nz, k, energies, sides, off_ref, emit_ref, absorb_ref, pos_ref, *refs):
    main, halos, done, own, edge = refs[0], refs[1:1 + sides], refs[1 + sides], refs[2 + sides], refs[3 + sides]
    done[...] = jnp.zeros_like(done)
    phonons = off_ref.shape[0]
    total = nz * k
    pairs = total // 2

    def lag_matrix(lag, sources, first):
        distance = lax.broadcasted_iota(jnp.int32, (sources, energies), 1) - lax.broadcasted_iota(jnp.int32, (sources, energies), 0) - first
        value = jnp.zeros((sources, energies), F32)
        for w in range(phonons):
            value = jnp.where(distance == off_ref[w], emit_ref[w, lag], value)
            value = jnp.where(distance == -off_ref[w], absorb_ref[w, lag], value)
        return value.astype(BF)

    def step(lag, carry):
        own[lag] = lag_matrix(lag, energies, 0)
        for side in range(sides):
            edge[side, lag] = lag_matrix(lag, SMAX, pos_ref[side])
        return carry

    lax.fori_loop(0, total, step, 0)
    for i in range(2 * pairs - 1):
        m = 2 * (pairs - 1 - i)
        for a in range(2):
            for b in range(2):
                at = i * 2 * energies + a * energies
                main[at:at + energies, b * energies:(b + 1) * energies] = own[(m + b - a) % total]
    per = k // 2
    for side in range(sides):
        for par in range(per):
            for i in range(2 * nz - 1):
                m = 2 * (per * (nz - 1 - i) + par)
                for a in range(k):
                    for b in range(2):
                        at = i * k * SMAX + a * SMAX
                        halos[side][par, at:at + SMAX, b * energies:(b + 1) * energies] = edge[side, (m + b - a) % total]


def tables(offsets, emit, absorb, pos, nz, k, energies):
    sides = pos.shape[0]
    total = nz * k
    main = jax.ShapeDtypeStruct(((total - 1) * 2 * energies, 2 * energies), BF)
    halo = jax.ShapeDtypeStruct((k // 2, (2 * nz - 1) * k * SMAX, 2 * energies), BF)
    return pl.pallas_call(
        functools.partial(table_kernel, nz, k, energies, sides),
        out_shape=(main,) + (halo,) * sides + (token(),),
        in_specs=[smem()] * 4,
        out_specs=(vmem(),) * (2 + sides),
        scratch_shapes=[pltpu.VMEM((total, energies, energies), BF), pltpu.VMEM((sides, total, SMAX, energies), BF)],
        compiler_params=params(),
        cost_estimate=cost(total * energies * energies * 100, main.size * 2),
    )(offsets, emit.astype(F32), absorb.astype(F32), pos)


def sum_kernel(nz, sides, *refs):
    pieces, refs = refs[:nz], refs[nz:]
    halos, refs = refs[:sides], refs[sides:]
    main, refs = refs[0], refs[1:]
    edges, refs = refs[:sides], refs[sides:]
    outs, done, wide = refs[-nz - 2:-2], refs[-2], refs[-1]
    done[...] = jnp.zeros_like(done)
    k, rows, energies = pieces[0].shape
    total = nz * k
    pairs = total // 2
    per = k // 2
    strip = k * SMAX
    inner = total * energies
    for q in range(nz):
        piece = pieces[(nz - q) % nz]
        for kk in range(k):
            wide[:, (q * k + kk) * energies:(q * k + kk + 1) * energies] = piece[kk]
        for side in range(sides):
            at = inner + (side * nz + q) * strip
            wide[:, at:at + strip] = halos[side][(nz - q) % nz]
    for pair in range(pairs):
        top = (pairs - 1 - pair) * 2 * energies
        value = jnp.dot(wide[:, :inner], main[top:top + inner, :], preferred_element_type=F32)
        for side in range(sides):
            at = inner + side * nz * strip
            start = (nz - 1 - pair // per) * strip
            value += jnp.dot(wide[:, at:at + nz * strip], edges[side][pair % per, start:start + nz * strip, :], preferred_element_type=F32)
        value = value.astype(BF)
        for b in range(2):
            outs[pair // per][2 * (pair % per) + b] = value[:, b * energies:(b + 1) * energies]


def phonon_sum(pieces, halos, main, edges, waits):
    nz, sides = len(pieces), len(halos)
    k, rows, energies = pieces[0].shape
    out = jax.ShapeDtypeStruct((k, rows, energies), BF)
    depth = nz * k * energies + sides * nz * k * SMAX
    return pl.pallas_call(
        functools.partial(sum_kernel, nz, sides),
        out_shape=(out,) * nz + (token(),),
        in_specs=[vmem()] * (nz + sides + 1 + sides + len(waits)),
        out_specs=(vmem(),) * (nz + 1),
        scratch_shapes=[pltpu.VMEM((rows, depth), BF)],
        compiler_params=params(),
        cost_estimate=cost(2 * rows * depth * nz * k * energies, main.size * 2),
    )(*pieces, *halos, main, *edges, *waits)


def coupling_kernel(slots, nz, inner_atoms, atoms, skip, z_ref, near_ref, c_ref, rows_a, rows_b, cols_a, cols_b, place, _, outer, inner, done, total):
    atom = pl.program_id(0) + skip
    done[...] = jnp.zeros_like(done)
    blocks = c_ref[0]
    left = jnp.dot(blocks, cols_a[...], preferred_element_type=F32).astype(BF)
    right = jnp.dot(blocks, cols_b[...], preferred_element_type=F32).astype(BF)
    total[...] = jnp.zeros_like(total)
    for n in range(slots):
        product = jnp.dot(rows_a[n], left, preferred_element_type=F32) * jnp.dot(rows_b[n], right, preferred_element_type=F32)
        total[near_ref[atom, n] + atom] += product
    first = jnp.where(atom < 2 * REACH, 0, atoms)
    value = jnp.dot(total[first].astype(BF), place[0], preferred_element_type=F32)
    for i in range(1, 2 * REACH):
        value += jnp.dot(total[first + i].astype(BF), place[i], preferred_element_type=F32)
    outer[0] = value.astype(BF)
    value = None
    for i in range(inner_atoms):
        turn = 2 * REACH + i // nz * nz + lax.rem(z_ref[0] + nz - i % nz, nz)
        term = jnp.dot(total[turn].astype(BF), place[i], preferred_element_type=F32)
        value = term if value is None else value + term
    inner[0] = value.astype(BF)


def coupling_matrices(z, nz, near, coupling, skip, count, wait):
    atoms, slots, orb, _ = coupling.shape
    comp = orb * orb
    inner_atoms = atoms - 2 * REACH
    blocks = coupling.reshape(atoms, slots * orb, orb)
    row = jnp.arange(comp)
    source = jnp.arange(slots * orb)
    slot = jnp.arange(slots)[:, None, None]
    rows_a = (source[None, None, :] == slot * orb + (row // orb)[None, :, None]).astype(BF)
    rows_b = (source[None, None, :] == slot * orb + (row % orb)[None, :, None]).astype(BF)
    cols_a = (jnp.arange(orb)[:, None] == (row // orb)[None, :]).astype(BF)
    cols_b = (jnp.arange(orb)[:, None] == (row % orb)[None, :]).astype(BF)
    wide = max(2 * REACH, inner_atoms)
    place = (jnp.arange(wide * comp)[None, None, :] == jnp.arange(wide)[:, None, None] * comp + row[None, :, None]).astype(BF)

    def fixed(array):
        return pl.BlockSpec(array.shape, lambda a: (0,) * len(array.shape))

    fixed_arrays = (rows_a, rows_b, cols_a, cols_b, place)
    out = jax.ShapeDtypeStruct((count, comp, wide * comp), BF)
    out_spec = pl.BlockSpec((1, comp, wide * comp), lambda a: (a, 0, 0))
    return pl.pallas_call(
        functools.partial(coupling_kernel, slots, nz, inner_atoms, atoms, skip),
        grid=(count,),
        out_shape=(out, out, token()),
        in_specs=[smem(), smem(), pl.BlockSpec((1, slots * orb, orb), lambda a: (a + skip, 0, 0))] + [fixed(v) for v in fixed_arrays + (wait,)],
        out_specs=(out_spec, out_spec, fixed(token())),
        scratch_shapes=[pltpu.VMEM((atoms + 2 * REACH, comp, comp), F32)],
        compiler_params=params(),
        cost_estimate=cost(atoms * comp * comp * slots * 400, atoms * comp * comp * 16),
    )(z, near, blocks, *fixed_arrays, wait)


def edge_kernel(nz, z_ref, *refs):
    pieces, low, high = refs[:nz], refs[-2], refs[-1]
    for r in range(nz):
        turn = lax.rem(z_ref[0] + nz - r, nz)
        for j in range(2 * REACH):
            target = low if j < REACH else high

            @pl.when(turn == j)
            def _(r=r, j=j, target=target):
                target[j % REACH] = pieces[r][...]


def edge_pack(z, pieces, waits):
    nz = len(pieces)
    out = jax.ShapeDtypeStruct((REACH,) + pieces[0].shape, BF)
    return pl.pallas_call(
        functools.partial(edge_kernel, nz),
        out_shape=(out, out),
        in_specs=[smem()] + [vmem()] * nz + [vmem()] * len(waits),
        out_specs=(vmem(), vmem()),
        compiler_params=params(),
        cost_estimate=cost(0, nz * pieces[0].size * 4),
    )(z, *pieces, *waits)


def arrive_kernel(*refs):
    refs[-1][...] = jnp.zeros_like(refs[-1])


def arrive(pieces):
    return pl.pallas_call(
        arrive_kernel,
        out_shape=token(),
        in_specs=[vmem()] * len(pieces),
        out_specs=vmem(),
        compiler_params=params(),
        cost_estimate=pl.CostEstimate(flops=40 * 10**9, bytes_accessed=0, transcendentals=0),
    )(*[piece[0, :16] for piece in pieces])


def apply_kernel(before, low, high, after, *refs):
    pieces, (outer_low, outer_high, inner_low, inner_high, _, out) = refs[:-6], refs[-6:]
    _, atoms, comp, energies = out.shape
    edge = 2 * REACH * comp
    half = inner_low.shape[0]
    rows = pl.ds(pl.multiple_of(pl.program_id(0) * comp, 16), comp)
    k = pl.program_id(1) * 2

    def window(refs):
        return jnp.concatenate([jnp.concatenate([r[k, rows, :], r[k + 1, rows, :]], axis=1) for r in refs], axis=0)

    def put(value, first):
        for a in range(value.shape[0] // comp):
            for b in range(2):
                out[b, first + a] = value[a * comp:(a + 1) * comp, b * energies:(b + 1) * energies]

    inside = window(pieces)
    value = jnp.dot(inner_low[:, :inside.shape[0]], inside, preferred_element_type=F32)
    value_edge = jnp.dot(outer_low[:edge, :edge], window([before.at[0], before.at[1], low.at[0], low.at[1]]), preferred_element_type=F32)
    put(value[:edge] + value_edge, 0)
    if half > edge:
        put(value[edge:], 2 * REACH)
    value = jnp.dot(inner_high[:, :inside.shape[0]], inside, preferred_element_type=F32)
    value_edge = jnp.dot(outer_high[half - edge:, :edge], window([high.at[0], high.at[1], after.at[0], after.at[1]]), preferred_element_type=F32)
    if half > edge:
        put(value[:half - edge], atoms // 2)
    put(value[half - edge:] + value_edge, atoms - 2 * REACH)


def apply_couplings(before, low, high, after, pieces, outers, inners, wait, shape):
    k, atoms, comps, energies = shape
    comp = comps // 2
    matrices = [m.reshape(-1, m.shape[2]) for m in (*outers, *inners)]
    return pl.pallas_call(
        apply_kernel,
        grid=(2, k // 2),
        out_shape=jax.ShapeDtypeStruct(shape, F32),
        in_specs=[vmem()] * (4 + len(pieces) + len(matrices) + 1),
        out_specs=pl.BlockSpec((2, atoms, comp, energies), lambda c, kk: (kk, 0, c, 0)),
        compiler_params=params(),
        cost_estimate=cost(0, 0),
    )(before, low, high, after, *pieces, *matrices, wait)


def shards(green, neighbours, offsets, emit_weight, absorb_weight, coupling):
    k, atoms, comps, energies = green.shape
    nz, ne, ny = (lax.axis_size(axis) for axis in ("momentum", "energy", "atom"))
    groups = atoms // nz
    z = lax.axis_index("momentum").astype(jnp.int32).reshape(1)
    where_e = lax.axis_index("energy").astype(jnp.int32)

    def around(array, r):
        return lax.ppermute(array, "momentum", [(i, (i + r) % nz) for i in range(nz)])

    if ne == 2:
        base = jnp.where(where_e == 0, energies - SMAX, 0).reshape(1)
        pos = jnp.where(where_e == 0, energies, -SMAX).reshape(1)
        routes = [[(0, 1), (1, 0)]]
    else:
        base = jnp.array([energies - SMAX, 0], jnp.int32)
        pos = jnp.array([-SMAX, energies], jnp.int32)
        routes = [[(i, i + 1) for i in range(ne - 1)], [(i + 1, i) for i in range(ne - 1)]]
    sides = len(routes)

    def send(group, *waits):
        sent = [lax.dynamic_index_in_dim(green, atom_of(group * nz + lax.rem(z[0] + r, nz), atoms), 1, keepdims=False) for r in range(nz)]
        if waits:
            sent = list(lax.optimization_barrier((sent, waits))[0])
        return spread(sent, ([[1, 2, 3], [1, 2, 3], [1, 2, 3], [1, 2, 3]])[group])

    def spread(sent, order):
        there = {r: around(sent[r], r) for r in order}
        return [sent[0]] + [there[r] for r in range(1, nz)]

    got = [send(0)]
    main, *edges, done = tables(offsets, emit_weight, absorb_weight, pos, nz, k, energies)
    first = lax.axis_index("atom") * atoms
    near = neighbours - (first + jnp.arange(atoms))[:, None].astype(jnp.int32) + REACH
    half = atoms // 2
    outer_low, inner_low, done = coupling_matrices(z, nz, near, coupling, 0, half, done)
    for group in range(1, groups):
        got.append(send(group, done))
    outer_high, inner_high, done = coupling_matrices(z, nz, near, coupling, half, half, done)

    waits = [done]
    back = []
    for group in range(groups):
        halos = halo_pack(base, got[group], sides, waits)
        halos = [jnp.concatenate([lax.ppermute(h[i:i + 2], "energy", route) for i in range(0, nz, 2)]) for h, route in zip(halos, routes)]
        *sums, sum_done = phonon_sum(got[group], halos, main, edges, [back[-1][2][0, :16]] if back else [])
        waits = [sum_done]
        back.append(spread(sums, ([[1, 2, 3], [1, 2, 3], [1, 2, 3], [1, 2, 3]])[2 + group]))

    low, high = edge_pack(z, back[0], waits)
    after = lax.ppermute(low, "atom", [(i + 1, i) for i in range(ny - 1)])
    before = lax.ppermute(high, "atom", [(i, i + 1) for i in range(ny - 1)])
    pieces = [piece for group in back[1:] for piece in group]
    return apply_couplings(before, low, high, after, pieces, (outer_low, outer_high), (inner_low, inner_high), arrive([p for group in back[1:] for p in group[1:]]), green.shape)


def solution(mesh):
    in_specs = (
        P("momentum", "atom", None, "energy"),
        P("atom", None),
        P(),
        P(),
        P(),
        P("atom", None, None, None),
    )
    out_specs = P("momentum", "atom", None, "energy")
    return jax.shard_map(shards, mesh=mesh, in_specs=in_specs, out_specs=out_specs, check_vma=False)
```

time: 361 us -> 117 us (0.32)
  matrix products: 83.5 us -> 0 us
  waiting for transfers between devices: 111 us -> 36.2 us
  local copies, waits for them, and re-layouts: 72.9 us -> 10.4 us
  blocking collectives: 59 us -> 0 us
  Pallas kernels: 0 us -> 35.1 us
  starting transfers between devices: 18 us -> 33.8 us
  other arithmetic: 12.4 us -> 0.94 us
    all_to_all x1 -> x0, waiting for transfers between devices: 88.9 us -> none  [shards(): lax.all_to_all(extended, 'momentum', split_axis=1, concat_axis=0, tiled=T...]
    dot_general x19 -> x0, matrix products: 83.5 us -> none  [the longest x8 48.7 us: add_slot(): jnp.einsum('kacile,ajl->kacije', half_block, coupling_slot, preferred_ele...]
    all_to_all x1 -> x0, blocking collectives: 59 us -> none  [shards(): lax.all_to_all(summed, 'momentum', split_axis=0, concat_axis=1, tiled=True)]
    pallas_call x0 -> x10, Pallas kernels: none -> 35.1 us  [the longest x2 13.3 us: coupling_matrices(): pl.pallas_call(functools.partial(coupling_kernel, slots, nz, inner_atoms,...]
    gather x8 -> x0, local copies, waits for them, and re-layouts: 27.9 us -> none  [add_slot(): chosen = jnp.take(blocks, column, axis=1)]
    ppermute x4 -> x18, starting transfers between devices: 12.7 us -> 33.8 us  [the longest x12 15.6 us: around(): lax.ppermute(array, 'momentum', [(i, (i + r) % nz) for i in range(nz)])]
    all_to_all x4 -> x0, local copies, waits for them, and re-layouts: 15.2 us -> none  [the longest x2 13.2 us: shards(): lax.all_to_all(extended, 'momentum', split_axis=1, concat_axis=0, tiled=T...]
    ppermute x4 -> x18, waiting for transfers between devices: 22 us -> 36.2 us  [the longest x12 25 us: around(): lax.ppermute(array, 'momentum', [(i, (i + r) % nz) for i in range(nz)])]
  transfers between devices with their start and end apart: 5 -> 18, of which waited for: 5 -> 11; matrix products, arithmetic and copies ran while one was open for 6% -> 2% of each run, Pallas kernels for 0% -> 25%
where the time goes in v1:
time: 117 us
  waiting for transfers between devices  36.2 us (31%)
  Pallas kernels  35.1 us (30%)
  starting transfers between devices  33.8 us (29%)
  local copies, waits for them, and re-layouts  10.4 us (9%)
    ppermute x12, waiting for transfers between devices, around(): lax.ppermute(array, 'momentum', [(i, (i + r) % nz) for i in range(nz)])  25 us
    ppermute x12, starting transfers between devices, around(): lax.ppermute(array, 'momentum', [(i, (i + r) % nz) for i in range(nz)])  15.6 us
    pallas_call x2, Pallas kernels, coupling_matrices(): pl.pallas_call(functools.partial(coupling_kernel, slots, nz, inner_atoms,...  13.3 us
    ppermute x1, starting transfers between devices, shards(): before = lax.ppermute(high, 'atom', [(i, i + 1) for i in range(ny - 1)])  13.2 us
    pallas_call x2, Pallas kernels, phonon_sum(): pl.pallas_call(functools.partial(sum_kernel, nz, sides), out_shape=(out,)...  8.65 us
    ppermute x4, waiting for transfers between devices, shards(): lax.ppermute(h[i:i + 2], 'energy', route)  6.74 us
    unnamed x34, local copies, waits for them, and re-layouts  6.38 us
    pallas_call x1, Pallas kernels, apply_couplings(): pl.pallas_call(apply_kernel, grid=(2, k // 2), out_shape=jax.ShapeDtypeSt...  5.46 us
  transfers between devices with their start and end apart: 18, of which 11 were waited for; matrix products, arithmetic and copies ran while one was open for 2% of the time, Pallas kernels for 25%

profile of v1, /device:TPU:9, one launch (start us, length us, event | category | flops | bytes accessed | tf_op | source)
XLA Modules:
  0.0 116.7 jit_solution(11502093204351470686)
XLA Ops:
  0.0 0.0 copy-start.13
  0.0 0.0 copy-start.12
  0.0 3.2 %dynamic-slice_bitcast_fusion = (bf16[4,288,128]{2,1,0:T(8,128)(2,1)}, bf16[4,288,128]{2,1,0:T(8,128)(2,1)}, bf16[4,288,128]{2,1,0:T(8,128)(2,1)}, bf16[4,288,12...) fusion(bf16[4,8,288,128]{3,2,1,0:T(8,128)(2,1)} %param.6, ...), kind=kLoop, calls=%fused_computation.8 | loop fusion | bytes 4718624 | tf_op jit(solution)/shard_map/jit(dynamic_index_in_dim)/squeeze | solution.py:365
  3.2 0.0 collective-permute-start.2
  3.2 2.5 %collective-permute-start.1 = (bf16[4,288,128]{2,1,0:T(8,128)(2,1)}, bf16[4,288,128]{2,1,0:T(8,128)(2,1)}, u32[]{:S(2)}, u32[]{:S(2)}) collective-permute-start(bf16[4,288,128]{2,1,0:T(8,128)(2,1)} %get-tuple-element.59), channel_id=1, source_target_pairs={{0,8},{4,12},{8,0},{12,4},{1,9},{5,13},{9,1},{13,5},{2,10},{6,14},... | collective-permute-start | bytes 884744 | tf_op jit(solution)/shard_map/ppermute | solution.py:352
  5.7 2.2 %collective-permute-start = (bf16[4,288,128]{2,1,0:T(8,128)(2,1)}, bf16[4,288,128]{2,1,0:T(8,128)(2,1)}, u32[]{:S(2)}, u32[]{:S(2)}) collective-permute-start(bf16[4,288,128]{2,1,0:T(8,128)(2,1)} %get-tuple-element.60), channel_id=1, source_target_pairs={{0,4},{4,8},{8,12},{12,0},{1,5},{5,9},{9,13},{13,1},{2,6},{6,10},{... | collective-permute-start | bytes 884744 | tf_op jit(solution)/shard_map/ppermute | solution.py:352
  7.9 0.1 broadcast_add_fusion
  8.0 0.2 fusion.2.rows_b
  8.2 0.2 fusion.1.rows_a
  8.5 0.1 subtract_add_fusion.near_ref
  8.5 0.1 iota_add_fusion
  8.7 0.8 reshape.171.c_ref
  9.5 4.4 %shard_map.64 = (bf16[3840,256]{1,0:T(8,128)(2,1)S(1)}, bf16[2,896,256]{2,1,0:T(8,128)(2,1)S(1)}, f32[8,128]{1,0:T(8,128)S(1)}) custom-call(s32[16]{0:T(128)S(1)} %copy-done.12, f32[16,16]{1,0:T(8,128)S(1)} %convert_element_type.41.emit_ref, f32[16,16]{1,0:T(8,128)S(1)} %convert_element_type.42.absorb_ref, s32[1]{0:T(128)} %bitcast.6.pos_ref), custom_call_target="tpu_custom_call" | custom-call | tf_op jit(solution)/shard_map/pallas_call | solution.py:145
  13.8 0.2 fusion.place
  14.0 0.0 copy-start.3
  14.0 0.9 copy-done.3
  14.9 6.7 %shard_map.65 = (bf16[4,144,576]{2,1,0:T(8,128)(2,1)S(1)}, bf16[4,144,576]{2,1,0:T(8,128)(2,1)S(1)}, f32[8,128]{1,0:T(8,128)S(1)}) custom-call(s32[1]{0:T(128)} %bitcast.z_ref, s32[8,8]{1,0:T(8,128)S(1)} %subtract_add_fusion.near_ref, bf16[8,96,12]{2,1,0:T(8,128)(2,1)S(1)} %copy-done.3, bf16[8,144,96]{2,1,0:T(8,128)(2,1)S(1)} %fusion.1.rows_a, ...), custom_call_target="tpu_custom_call" | custom-call | tf_op jit(solution)/shard_map/pallas_call | solution.py:248
  21.6 0.0 copy-start.4
  21.6 0.9 copy-done.4
  22.5 0.9 copy-done.6
  23.4 0.0 collective-permute-start.8
  23.4 1.3 %collective-permute-start.9 = (bf16[4,288,128]{2,1,0:T(8,128)(2,1)}, bf16[4,288,128]{2,1,0:T(8,128)(2,1)}, u32[]{:S(2)}, u32[]{:S(2)}) collective-permute-start(bf16[4,288,128]{2,1,0:T(8,128)(2,1)} %get-tuple-element.41), channel_id=1, source_target_pairs={{0,8},{4,12},{8,0},{12,4},{1,9},{5,13},{9,1},{13,5},{2,10},{6,14},... | collective-permute-start | bytes 884744 | tf_op jit(solution)/shard_map/ppermute | solution.py:352
  24.7 6.7 %shard_map.66 = (bf16[4,144,576]{2,1,0:T(8,128)(2,1)S(1)}, bf16[4,144,576]{2,1,0:T(8,128)(2,1)S(1)}, f32[8,128]{1,0:T(8,128)S(1)}) custom-call(s32[1]{0:T(128)} %bitcast.z_ref, s32[8,8]{1,0:T(8,128)S(1)} %subtract_add_fusion.near_ref, bf16[8,96,12]{2,1,0:T(8,128)(2,1)S(1)} %copy-done.3, bf16[8,144,96]{2,1,0:T(8,128)(2,1)S(1)} %fusion.1.rows_a, ...), custom_call_target="tpu_custom_call" | custom-call | tf_op jit(solution)/shard_map/pallas_call | solution.py:248
  31.4 0.9 copy-done.8
  32.3 0.9 copy-done.10
  33.1 0.0 collective-permute-done.2.refs_3_
  33.1 1.0 collective-permute-start.10
  34.2 0.0 collective-permute-done.1.refs_2_
  34.2 0.0 collective-permute-done.refs_1_
  34.2 1.0 copy-done.1
  35.1 1.6 %shard_map.67 = bf16[4,288,128]{2,1,0:T(8,128)(2,1)S(1)} custom-call(s32[1]{0:T(128)} %bitcast.5.base_ref, bf16[4,288,128]{2,1,0:T(8,128)(2,1)S(1)} %copy-done.1, bf16[4,288,128]{2,1,0:T(8,128)(2,1)} %collective-permute-done.refs_1_, bf16[4,288,128]{2,1,0:T(8,128)(2,1)} %collective-permute-done.1.refs_2_, ...), custom_call_target="tpu_custom_call" | custom-call | tf_op jit(solution)/shard_map/pallas_call | solution.py:91
  36.8 1.3 %collective-permute-start.3 = (bf16[2,288,128]{2,1,0:T(8,128)(2,1)S(1)}, bf16[2,288,128]{2,1,0:T(8,128)(2,1)S(1)}, u32[]{:S(2)}, u32[]{:S(2)}) collective-permute-start(bf16[2,288,128]{2,1,0:T(8,128)(2,1)S(1)} %get-tuple-element.65), channel_id=1, source_target_pairs={{0,16},{16,0},{1,17},{17,1},{2,18},{18,2},{3,19},{19,3},{4,20},{20... | collective-permute-start | bytes 442376 | tf_op jit(solution)/shard_map/ppermute | solution.py:388
  38.1 0.3 collective-permute-start.4
  38.3 2.5 %collective-permute-done.3 = bf16[2,288,128]{2,1,0:T(8,128)(2,1)S(1)} collective-permute-done((bf16[2,288,128]{2,1,0:T(8,128)(2,1)S(1)}, bf16[2,288,128]{2,1,0:T(8,128)(2,1)S(1)}, u32[]{:S(2)}, u32[]{:S(2)}) %collective-permute-start.3) | collective-permute-done | bytes 147488 | tf_op jit(solution)/shard_map/ppermute | solution.py:388
  40.8 1.6 %collective-permute-done.4 = bf16[2,288,128]{2,1,0:T(8,128)(2,1)S(1)} collective-permute-done((bf16[2,288,128]{2,1,0:T(8,128)(2,1)S(1)}, bf16[2,288,128]{2,1,0:T(8,128)(2,1)S(1)}, u32[]{:S(2)}, u32[]{:S(2)}) %collective-permute-start.4) | collective-permute-done | bytes 147488 | tf_op jit(solution)/shard_map/ppermute | solution.py:388
  42.5 1.0 copy-done.2
  43.4 4.4 %shard_map.68 = (bf16[4,288,128]{2,1,0:T(8,128)(2,1)S(1)}, bf16[4,288,128]{2,1,0:T(8,128)(2,1)S(1)}, bf16[4,288,128]{2,1,0:T(8,128)(2,1)S(1)}, bf16[4,288,128]{2,1,0:T(8,128)(2,1)S(1)}, f32[8,128]{1,0:T(8,128)S(1)}) custom-call(bf16[4,288,128]{2,1,0:T(8,128)(2,1)S(1)} %copy-done.2, bf16[4,288,128]{2,1,0:T(8,128)(2,1)} %collective-permute-done.refs_1_, ...), custom_call_target="tpu_custom_call" | custom-call | tf_op jit(solution)/shard_map/pallas_call | solution.py:193
  47.8 2.1 %collective-permute-start.6 = (bf16[4,288,128]{2,1,0:T(8,128)(2,1)S(1)}, bf16[4,288,128]{2,1,0:T(8,128)(2,1)S(1)}, u32[]{:S(2)}, u32[]{:S(2)}) collective-permute-start(bf16[4,288,128]{2,1,0:T(8,128)(2,1)S(1)} %get-tuple-element.37), channel_id=1, source_target_pairs={{0,8},{4,12},{8,0},{12,4},{1,9},{5,13},{9,1},{13,5},{2,10},{6,14},... | collective-permute-start | bytes 884744 | tf_op jit(solution)/shard_map/ppermute | solution.py:352
  49.9 0.0 collective-permute-done.8.refs_1_
  49.9 6.3 %collective-permute-done.9.refs_2_ = bf16[4,288,128]{2,1,0:T(8,128)(2,1)} collective-permute-done((bf16[4,288,128]{2,1,0:T(8,128)(2,1)}, bf16[4,288,128]{2,1,0:T(8,128)(2,1)}, u32[]{:S(2)}, u32[]{:S(2)}) %collective-permute-start.9) | collective-permute-done | bytes 294944 | tf_op jit(solution)/shard_map/ppermute | solution.py:352
  56.2 5.7 %collective-permute-done.10.refs_3_ = bf16[4,288,128]{2,1,0:T(8,128)(2,1)S(1)} collective-permute-done((bf16[4,288,128]{2,1,0:T(8,128)(2,1)}, bf16[4,288,128]{2,1,0:T(8,128)(2,1)S(1)}, u32[]{:S(2)}, u32[]{:S(2)}) %collective-permute-start.10) | collective-permute-done | bytes 294944 | tf_op jit(solution)/shard_map/ppermute | solution.py:352
  61.9 1.5 %shard_map.69 = bf16[4,288,128]{2,1,0:T(8,128)(2,1)S(1)} custom-call(s32[1]{0:T(128)} %bitcast.5.base_ref, bf16[4,288,128]{2,1,0:T(8,128)(2,1)S(1)} %copy-done, bf16[4,288,128]{2,1,0:T(8,128)(2,1)} %collective-permute-done.8.refs_1_, bf16[4,288,128]{2,1,0:T(8,128)(2,1)} %collective-permute-done.9.refs_2_, ...), custom_call_target="tpu_custom_call" | custom-call | tf_op jit(solution)/shard_map/pallas_call | solution.py:91
  63.4 1.3 %collective-permute-start.11 = (bf16[2,288,128]{2,1,0:T(8,128)(2,1)S(1)}, bf16[2,288,128]{2,1,0:T(8,128)(2,1)S(1)}, u32[]{:S(2)}, u32[]{:S(2)}) collective-permute-start(bf16[2,288,128]{2,1,0:T(8,128)(2,1)S(1)} %get-tuple-element.63), channel_id=1, source_target_pairs={{0,16},{16,0},{1,17},{17,1},{2,18},{18,2},{3,19},{19,3},{4,20},{20... | collective-permute-start | bytes 442376 | tf_op jit(solution)/shard_map/ppermute | solution.py:388
  64.7 0.3 collective-permute-start.12
  65.0 0.0 collective-permute-start.5
  65.0 1.5 %collective-permute-start.7 = (bf16[4,288,128]{2,1,0:T(8,128)(2,1)S(1)}, bf16[4,288,128]{2,1,0:T(8,128)(2,1)S(1)}, u32[]{:S(2)}, u32[]{:S(2)}) collective-permute-start(bf16[4,288,128]{2,1,0:T(8,128)(2,1)S(1)} %get-tuple-element.38), channel_id=1, source_target_pairs={{0,12},{4,0},{8,4},{12,8},{1,13},{5,1},{9,5},{13,9},{2,14},{6,2},{... | collective-permute-start | bytes 884744 | tf_op jit(solution)/shard_map/ppermute | solution.py:352
  66.4 1.1 collective-permute-done.11
  67.5 1.6 %collective-permute-done.12 = bf16[2,288,128]{2,1,0:T(8,128)(2,1)S(1)} collective-permute-done((bf16[2,288,128]{2,1,0:T(8,128)(2,1)S(1)}, bf16[2,288,128]{2,1,0:T(8,128)(2,1)S(1)}, u32[]{:S(2)}, u32[]{:S(2)}) %collective-permute-start.12) | collective-permute-done | bytes 147488 | tf_op jit(solution)/shard_map/ppermute | solution.py:388
  69.1 0.0 collective-permute-done.6.refs_2_
  69.1 4.3 %shard_map.70 = (bf16[4,288,128]{2,1,0:T(8,128)(2,1)S(1)}, bf16[4,288,128]{2,1,0:T(8,128)(2,1)S(1)}, bf16[4,288,128]{2,1,0:T(8,128)(2,1)S(1)}, bf16[4,288,128]{2,1,0:T(8,128)(2,1)S(1)}, f32[8,128]{1,0:T(8,128)S(1)}) custom-call(bf16[4,288,128]{2,1,0:T(8,128)(2,1)S(1)} %copy-done, bf16[4,288,128]{2,1,0:T(8,128)(2,1)} %collective-permute-done.8.refs_1_, ...), custom_call_target="tpu_custom_call" | custom-call | tf_op jit(solution)/shard_map/pallas_call | solution.py:193
  73.4 1.0 collective-permute-start.15
  74.5 4.0 %collective-permute-start.16 = (bf16[4,288,128]{2,1,0:T(8,128)(2,1)S(1)}, bf16[4,288,128]{2,1,0:T(8,128)(2,1)S(1)}, u32[]{:S(2)}, u32[]{:S(2)}) collective-permute-start(bf16[4,288,128]{2,1,0:T(8,128)(2,1)S(1)} %get-tuple-element.49), channel_id=1, source_target_pairs={{0,8},{4,12},{8,0},{12,4},{1,9},{5,13},{9,1},{13,5},{2,10},{6,14},... | collective-permute-start | bytes 884744 | tf_op jit(solution)/shard_map/ppermute | solution.py:352
  78.5 0.0 collective-permute-start.17
  78.5 0.7 collective-permute-done.5.refs_1_
  79.2 7.5 %collective-permute-done.7.refs_3_ = bf16[4,288,128]{2,1,0:T(8,128)(2,1)S(1)} collective-permute-done((bf16[4,288,128]{2,1,0:T(8,128)(2,1)S(1)}, bf16[4,288,128]{2,1,0:T(8,128)(2,1)S(1)}, u32[]{:S(2)}, u32[]{:S(2)}) %collective-permute-start.7) | collective-permute-done | bytes 294944 | tf_op jit(solution)/shard_map/ppermute | solution.py:352
  86.6 0.1 shard_map.71
  86.8 13.2 %collective-permute-start.13 = (bf16[2,4,288,128]{3,2,1,0:T(8,128)(2,1)S(1)}, bf16[2,4,288,128]{3,2,1,0:T(8,128)(2,1)S(1)}, u32[]{:S(2)}, u32[]{:S(2)}) collective-permute-start(bf16[2,4,288,128]{3,2,1,0:T(8,128)(2,1)S(1)} %get-tuple-element.45.high), channel_id=1, source_target_pairs={{0,1},{1,2},{2,3},{4,5},{5,6},{6,7},{8,9},{9,10},{10,11},{12,13},{... | collective-permute-start | bytes 1769480 | tf_op jit(solution)/shard_map/ppermute | solution.py:395
  100.0 1.9 %collective-permute-start.14 = (bf16[2,4,288,128]{3,2,1,0:T(8,128)(2,1)S(1)}, bf16[2,4,288,128]{3,2,1,0:T(8,128)(2,1)S(1)}, u32[]{:S(2)}, u32[]{:S(2)}) collective-permute-start(bf16[2,4,288,128]{3,2,1,0:T(8,128)(2,1)S(1)} %get-tuple-element.46.low), channel_id=1, source_target_pairs={{1,0},{2,1},{3,2},{5,4},{6,5},{7,6},{9,8},{10,9},{11,10},{13,12},{... | collective-permute-start | bytes 1769480 | tf_op jit(solution)/shard_map/ppermute | solution.py:394
  101.9 0.0 collective-permute-done.15.refs_1_
  101.9 4.7 %collective-permute-done.16.refs_2_ = bf16[4,288,128]{2,1,0:T(8,128)(2,1)S(1)} collective-permute-done((bf16[4,288,128]{2,1,0:T(8,128)(2,1)S(1)}, bf16[4,288,128]{2,1,0:T(8,128)(2,1)S(1)}, u32[]{:S(2)}, u32[]{:S(2)}) %collective-permute-start.16) | collective-permute-done | bytes 294944 | tf_op jit(solution)/shard_map/ppermute | solution.py:352
  106.7 0.0 collective-permute-done.17.refs_3_
  106.7 0.1 collective-permute-done.13.before
  106.8 4.4 %collective-permute-done.14.after = bf16[2,4,288,128]{3,2,1,0:T(8,128)(2,1)S(1)} collective-permute-done((bf16[2,4,288,128]{3,2,1,0:T(8,128)(2,1)S(1)}, bf16[2,4,288,128]{3,2,1,0:T(8,128)(2,1)S(1)}, u32[]{:S(2)}, u32[]{:S(2)}) %collective-permute-start.14) | collective-permute-done | bytes 589856 | tf_op jit(solution)/shard_map/ppermute | solution.py:394
  111.2 5.5 %shard_map.73 = f32[4,8,288,128]{3,2,1,0:T(8,128)} custom-call(bf16[2,4,288,128]{3,2,1,0:T(8,128)(2,1)S(1)} %collective-permute-done.13.before, bf16[2,4,288,128]{3,2,1,0:T(8,128)(2,1)S(1)} %get-tuple-element.46.low, bf16[2,4,288,128]{3,2,1,0:T(8,128)(2,1)S(1)} %get-tuple-element.45.high, bf16[2,4,288,128]{3,2,1,0:T(8,128)(2,1)S(1)} %collective-permute-done.14.after, ...), custom_call_target="tpu_custom_call" | custom-call | tf_op jit(solution)/shard_map/pallas_call | solution.py:333
  (41 shorter events, 0.2 us)
Async XLA Ops:
  0.0 8.5 %copy-start.16 = (s32[8,8]{1,0:T(8,128)S(1)}, s32[8,8]{1,0:T(8,128)}, u32[]{:S(2)}) copy-start(s32[8,8]{1,0:T(8,128)} %param.7) | copy-start | bytes 772
  0.0 8.6 %copy-start.14 = (bf16[16,16]{1,0:T(8,128)(2,1)S(1)}, bf16[16,16]{1,0:T(8,128)(2,1)}, u32[]{:S(2)}) copy-start(bf16[16,16]{1,0:T(8,128)(2,1)} %param.9) | copy-start | bytes 1540
  0.0 8.6 %copy-start.15 = (bf16[16,16]{1,0:T(8,128)(2,1)S(1)}, bf16[16,16]{1,0:T(8,128)(2,1)}, u32[]{:S(2)}) copy-start(bf16[16,16]{1,0:T(8,128)(2,1)} %param.10) | copy-start | bytes 1540
  0.0 8.6 %copy-start.13 = (bf16[8,8,12,12]{3,1,2,0:T(8,128)(2,1)S(1)}, bf16[8,8,12,12]{3,1,2,0:T(8,128)(2,1)}, u32[]{:S(2)}) copy-start(bf16[8,8,12,12]{3,1,2,0:T(8,128)(2,1)} %param.11) | copy-start | bytes 55300
  0.0 9.4 %copy-start.12 = (s32[16]{0:T(128)S(1)}, s32[16]{0:T(128)}, u32[]{:S(2)}) copy-start(s32[16]{0:T(128)} %off_ref.1) | copy-start | bytes 196
  3.2 29.9 %collective-permute-start.2 = (bf16[4,288,128]{2,1,0:T(8,128)(2,1)}, bf16[4,288,128]{2,1,0:T(8,128)(2,1)}, u32[]{:S(2)}, u32[]{:S(2)}) collective-permute-start(bf16[4,288,128]{2,1,0:T(8,128)(2,1)} %get-tuple-element.58), channel_id=1, source_target_pairs={{0,12},{4,0},{8,4},{12,8},{1,13},{5,1},{9,5},{13,9},{2,14},{6,2},{... | collective-permute-start | bytes 884744 | tf_op jit(solution)/shard_map/ppermute | solution.py:352
  3.2 31.0 %collective-permute-start.1 = (bf16[4,288,128]{2,1,0:T(8,128)(2,1)}, bf16[4,288,128]{2,1,0:T(8,128)(2,1)}, u32[]{:S(2)}, u32[]{:S(2)}) collective-permute-start(bf16[4,288,128]{2,1,0:T(8,128)(2,1)} %get-tuple-element.59), channel_id=1, source_target_pairs={{0,8},{4,12},{8,0},{12,4},{1,9},{5,13},{9,1},{13,5},{2,10},{6,14},... | collective-permute-start | bytes 884744 | tf_op jit(solution)/shard_map/ppermute | solution.py:352
  5.7 28.5 %collective-permute-start = (bf16[4,288,128]{2,1,0:T(8,128)(2,1)}, bf16[4,288,128]{2,1,0:T(8,128)(2,1)}, u32[]{:S(2)}, u32[]{:S(2)}) collective-permute-start(bf16[4,288,128]{2,1,0:T(8,128)(2,1)} %get-tuple-element.60), channel_id=1, source_target_pairs={{0,4},{4,8},{8,12},{12,0},{1,5},{5,9},{9,13},{13,1},{2,6},{6,10},{... | collective-permute-start | bytes 884744 | tf_op jit(solution)/shard_map/ppermute | solution.py:352
  14.0 0.9 copy-start.3
  21.6 0.9 copy-start.4
  22.5 0.9 copy-start.6
  23.4 26.5 %collective-permute-start.8 = (bf16[4,288,128]{2,1,0:T(8,128)(2,1)}, bf16[4,288,128]{2,1,0:T(8,128)(2,1)}, u32[]{:S(2)}, u32[]{:S(2)}) collective-permute-start(bf16[4,288,128]{2,1,0:T(8,128)(2,1)} %get-tuple-element.40), channel_id=1, source_target_pairs={{0,4},{4,8},{8,12},{12,0},{1,5},{5,9},{9,13},{13,1},{2,6},{6,10},{... | collective-permute-start | bytes 884744 | tf_op jit(solution)/shard_map/ppermute | solution.py:352
  23.4 32.8 %collective-permute-start.9 = (bf16[4,288,128]{2,1,0:T(8,128)(2,1)}, bf16[4,288,128]{2,1,0:T(8,128)(2,1)}, u32[]{:S(2)}, u32[]{:S(2)}) collective-permute-start(bf16[4,288,128]{2,1,0:T(8,128)(2,1)} %get-tuple-element.41), channel_id=1, source_target_pairs={{0,8},{4,12},{8,0},{12,4},{1,9},{5,13},{9,1},{13,5},{2,10},{6,14},... | collective-permute-start | bytes 884744 | tf_op jit(solution)/shard_map/ppermute | solution.py:352
  31.4 0.9 copy-start.8
  32.3 0.9 copy-start.10
  33.1 28.7 %collective-permute-start.10 = (bf16[4,288,128]{2,1,0:T(8,128)(2,1)}, bf16[4,288,128]{2,1,0:T(8,128)(2,1)S(1)}, u32[]{:S(2)}, u32[]{:S(2)}) collective-permute-start(bf16[4,288,128]{2,1,0:T(8,128)(2,1)} %get-tuple-element.42), channel_id=1, source_target_pairs={{0,12},{4,0},{8,4},{12,8},{1,13},{5,1},{9,5},{13,9},{2,14},{6,2},{... | collective-permute-start | bytes 884744 | tf_op jit(solution)/shard_map/ppermute | solution.py:352
  34.2 1.0 copy-start.1
  36.8 4.1 %collective-permute-start.3 = (bf16[2,288,128]{2,1,0:T(8,128)(2,1)S(1)}, bf16[2,288,128]{2,1,0:T(8,128)(2,1)S(1)}, u32[]{:S(2)}, u32[]{:S(2)}) collective-permute-start(bf16[2,288,128]{2,1,0:T(8,128)(2,1)S(1)} %get-tuple-element.65), channel_id=1, source_target_pairs={{0,16},{16,0},{1,17},{17,1},{2,18},{18,2},{3,19},{19,3},{4,20},{20... | collective-permute-start | bytes 442376 | tf_op jit(solution)/shard_map/ppermute | solution.py:388
  38.0 23.8 %copy-start = (bf16[4,288,128]{2,1,0:T(8,128)(2,1)S(1)}, bf16[4,288,128]{2,1,0:T(8,128)(2,1)}, u32[]{:S(2)}) copy-start(bf16[4,288,128]{2,1,0:T(8,128)(2,1)} %get-tuple-element.39.refs_0_) | copy-start | bytes 884740
  38.1 4.4 %collective-permute-start.4 = (bf16[2,288,128]{2,1,0:T(8,128)(2,1)S(1)}, bf16[2,288,128]{2,1,0:T(8,128)(2,1)S(1)}, u32[]{:S(2)}, u32[]{:S(2)}) collective-permute-start(bf16[2,288,128]{2,1,0:T(8,128)(2,1)S(1)} %get-tuple-element.66), channel_id=1, source_target_pairs={{0,16},{16,0},{1,17},{17,1},{2,18},{18,2},{3,19},{19,3},{4,20},{20... | collective-permute-start | bytes 442376 | tf_op jit(solution)/shard_map/ppermute | solution.py:388
  42.4 1.0 copy-start.2
  47.8 21.3 %collective-permute-start.6 = (bf16[4,288,128]{2,1,0:T(8,128)(2,1)S(1)}, bf16[4,288,128]{2,1,0:T(8,128)(2,1)S(1)}, u32[]{:S(2)}, u32[]{:S(2)}) collective-permute-start(bf16[4,288,128]{2,1,0:T(8,128)(2,1)S(1)} %get-tuple-element.37), channel_id=1, source_target_pairs={{0,8},{4,12},{8,0},{12,4},{1,9},{5,13},{9,1},{13,5},{2,10},{6,14},... | collective-permute-start | bytes 884744 | tf_op jit(solution)/shard_map/ppermute | solution.py:352
  63.4 4.1 %collective-permute-start.11 = (bf16[2,288,128]{2,1,0:T(8,128)(2,1)S(1)}, bf16[2,288,128]{2,1,0:T(8,128)(2,1)S(1)}, u32[]{:S(2)}, u32[]{:S(2)}) collective-permute-start(bf16[2,288,128]{2,1,0:T(8,128)(2,1)S(1)} %get-tuple-element.63), channel_id=1, source_target_pairs={{0,16},{16,0},{1,17},{17,1},{2,18},{18,2},{3,19},{19,3},{4,20},{20... | collective-permute-start | bytes 442376 | tf_op jit(solution)/shard_map/ppermute | solution.py:388
  64.7 4.4 %collective-permute-start.12 = (bf16[2,288,128]{2,1,0:T(8,128)(2,1)S(1)}, bf16[2,288,128]{2,1,0:T(8,128)(2,1)S(1)}, u32[]{:S(2)}, u32[]{:S(2)}) collective-permute-start(bf16[2,288,128]{2,1,0:T(8,128)(2,1)S(1)} %get-tuple-element.64), channel_id=1, source_target_pairs={{0,16},{16,0},{1,17},{17,1},{2,18},{18,2},{3,19},{19,3},{4,20},{20... | collective-permute-start | bytes 442376 | tf_op jit(solution)/shard_map/ppermute | solution.py:388
  65.0 14.2 %collective-permute-start.5 = (bf16[4,288,128]{2,1,0:T(8,128)(2,1)S(1)}, bf16[4,288,128]{2,1,0:T(8,128)(2,1)S(1)}, u32[]{:S(2)}, u32[]{:S(2)}) collective-permute-start(bf16[4,288,128]{2,1,0:T(8,128)(2,1)S(1)} %get-tuple-element.36), channel_id=1, source_target_pairs={{0,4},{4,8},{8,12},{12,0},{1,5},{5,9},{9,13},{13,1},{2,6},{6,10},{... | collective-permute-start | bytes 884744 | tf_op jit(solution)/shard_map/ppermute | solution.py:352
  65.0 21.7 %collective-permute-start.7 = (bf16[4,288,128]{2,1,0:T(8,128)(2,1)S(1)}, bf16[4,288,128]{2,1,0:T(8,128)(2,1)S(1)}, u32[]{:S(2)}, u32[]{:S(2)}) collective-permute-start(bf16[4,288,128]{2,1,0:T(8,128)(2,1)S(1)} %get-tuple-element.38), channel_id=1, source_target_pairs={{0,12},{4,0},{8,4},{12,8},{1,13},{5,1},{9,5},{13,9},{2,14},{6,2},{... | collective-permute-start | bytes 884744 | tf_op jit(solution)/shard_map/ppermute | solution.py:352
  73.4 28.5 %collective-permute-start.15 = (bf16[4,288,128]{2,1,0:T(8,128)(2,1)S(1)}, bf16[4,288,128]{2,1,0:T(8,128)(2,1)S(1)}, u32[]{:S(2)}, u32[]{:S(2)}) collective-permute-start(bf16[4,288,128]{2,1,0:T(8,128)(2,1)S(1)} %get-tuple-element.48), channel_id=1, source_target_pairs={{0,4},{4,8},{8,12},{12,0},{1,5},{5,9},{9,13},{13,1},{2,6},{6,10},{... | collective-permute-start | bytes 884744 | tf_op jit(solution)/shard_map/ppermute | solution.py:352
  74.5 32.2 %collective-permute-start.16 = (bf16[4,288,128]{2,1,0:T(8,128)(2,1)S(1)}, bf16[4,288,128]{2,1,0:T(8,128)(2,1)S(1)}, u32[]{:S(2)}, u32[]{:S(2)}) collective-permute-start(bf16[4,288,128]{2,1,0:T(8,128)(2,1)S(1)} %get-tuple-element.49), channel_id=1, source_target_pairs={{0,8},{4,12},{8,0},{12,4},{1,9},{5,13},{9,1},{13,5},{2,10},{6,14},... | collective-permute-start | bytes 884744 | tf_op jit(solution)/shard_map/ppermute | solution.py:352
  78.5 28.2 %collective-permute-start.17 = (bf16[4,288,128]{2,1,0:T(8,128)(2,1)S(1)}, bf16[4,288,128]{2,1,0:T(8,128)(2,1)S(1)}, u32[]{:S(2)}, u32[]{:S(2)}) collective-permute-start(bf16[4,288,128]{2,1,0:T(8,128)(2,1)S(1)} %get-tuple-element.50), channel_id=1, source_target_pairs={{0,12},{4,0},{8,4},{12,8},{1,13},{5,1},{9,5},{13,9},{2,14},{6,2},{... | collective-permute-start | bytes 884744 | tf_op jit(solution)/shard_map/ppermute | solution.py:352
  86.8 20.0 %collective-permute-start.13 = (bf16[2,4,288,128]{3,2,1,0:T(8,128)(2,1)S(1)}, bf16[2,4,288,128]{3,2,1,0:T(8,128)(2,1)S(1)}, u32[]{:S(2)}, u32[]{:S(2)}) collective-permute-start(bf16[2,4,288,128]{3,2,1,0:T(8,128)(2,1)S(1)} %get-tuple-element.45.high), channel_id=1, source_target_pairs={{0,1},{1,2},{2,3},{4,5},{5,6},{6,7},{8,9},{9,10},{10,11},{12,13},{... | collective-permute-start | bytes 1769480 | tf_op jit(solution)/shard_map/ppermute | solution.py:395
  100.0 11.2 %collective-permute-start.14 = (bf16[2,4,288,128]{3,2,1,0:T(8,128)(2,1)S(1)}, bf16[2,4,288,128]{3,2,1,0:T(8,128)(2,1)S(1)}, u32[]{:S(2)}, u32[]{:S(2)}) collective-permute-start(bf16[2,4,288,128]{3,2,1,0:T(8,128)(2,1)S(1)} %get-tuple-element.46.low), channel_id=1, source_target_pairs={{1,0},{2,1},{3,2},{5,4},{6,5},{7,6},{9,8},{10,9},{11,10},{13,12},{... | collective-permute-start | bytes 1769480 | tf_op jit(solution)/shard_map/ppermute | solution.py:394
  106.7 4.5 %copy-start.5 = (bf16[4,144,576]{2,1,0:T(8,128)(2,1)S(1)}, bf16[4,144,576]{2,1,0:T(8,128)(2,1)}, u32[]{:S(2)}) copy-start(bf16[4,144,576]{2,1,0:T(8,128)(2,1)} %copy-done.4) | copy-start | bytes 1990660
  106.7 4.5 %copy-start.7 = (bf16[4,144,576]{2,1,0:T(8,128)(2,1)S(1)}, bf16[4,144,576]{2,1,0:T(8,128)(2,1)}, u32[]{:S(2)}) copy-start(bf16[4,144,576]{2,1,0:T(8,128)(2,1)} %copy-done.6) | copy-start | bytes 1990660
  106.7 4.5 %copy-start.9 = (bf16[4,144,576]{2,1,0:T(8,128)(2,1)S(1)}, bf16[4,144,576]{2,1,0:T(8,128)(2,1)}, u32[]{:S(2)}) copy-start(bf16[4,144,576]{2,1,0:T(8,128)(2,1)} %copy-done.8) | copy-start | bytes 1990660
  106.7 4.5 %copy-start.11 = (bf16[4,144,576]{2,1,0:T(8,128)(2,1)S(1)}, bf16[4,144,576]{2,1,0:T(8,128)(2,1)}, u32[]{:S(2)}) copy-start(bf16[4,144,576]{2,1,0:T(8,128)(2,1)} %copy-done.10) | copy-start | bytes 1990660

commit v2 on v1

v2 whole, which is shorter than its diff:
```python
import functools

import jax
import jax.numpy as jnp
from jax import lax
from jax.experimental import pallas as pl
from jax.experimental.pallas import tpu as pltpu
from jax.sharding import PartitionSpec as P

SMAX = 32
REACH = 2
BF = jnp.bfloat16
F32 = jnp.float32
VMEM_LIMIT = 16 * 1024 * 1024
PACK_LIMIT = 62 * 1024 * 1024


def params(limit=VMEM_LIMIT):
    return pltpu.CompilerParams(vmem_limit_bytes=limit)


def smem():
    return pl.BlockSpec(memory_space=pltpu.SMEM)


def vmem():
    return pl.BlockSpec(memory_space=pltpu.VMEM)


def anywhere():
    return pl.BlockSpec(memory_space=pl.ANY)


def token():
    return jax.ShapeDtypeStruct((8, 128), F32)


def cost(flops, nbytes):
    return pl.CostEstimate(flops=0, bytes_accessed=0, transcendentals=0)


def atom_of(turn, atoms):
    return jnp.where(turn < REACH, turn, jnp.where(turn < 2 * REACH, turn + atoms - 2 * REACH, turn - REACH))


def pack_kernel(group, nz, ids, green, *refs):
    outs, sems = refs[-nz - 1:-1], refs[-1]
    atoms = green.shape[1]
    copies = []
    for r in range(nz):
        atom = atom_of(group * nz + lax.rem(ids[0] + r, nz), atoms)
        copies.append(pltpu.make_async_copy(green.at[:, atom], outs[r], sems.at[r]))
    for copy in copies:
        copy.start()
    for copy in copies:
        copy.wait()


def pack(ids, green, nz, group, waits):
    k, _, comps, energies = green.shape
    piece = jax.ShapeDtypeStruct((k, comps, energies), BF)
    return pl.pallas_call(
        functools.partial(pack_kernel, group, nz),
        out_shape=(piece,) * nz,
        in_specs=[smem(), pl.BlockSpec(memory_space=pltpu.HBM)] + [vmem()] * len(waits),
        out_specs=(anywhere(),) * nz,
        scratch_shapes=[pltpu.SemaphoreType.DMA((nz,))],
        compiler_params=params(VMEM_LIMIT if waits else PACK_LIMIT),
        cost_estimate=cost(0, nz * piece.size * 4),
    )(ids, green, *waits)


def own_edge(place, side, sides, energies):
    last = place == 0 if sides == 1 else side == 0
    return jnp.where(last, energies - SMAX, 0)


def far_edge(place, side, sides, energies):
    above = place == 0 if sides == 1 else side == 1
    return jnp.where(above, energies, -SMAX)


def halo_kernel(nz, sides, ids, *refs):
    pieces, outs = refs[:nz], refs[-2 * sides:]
    half = nz // 2
    k, rows, energies = pieces[0].shape
    lanes = k * SMAX
    row = lax.broadcasted_iota(jnp.int32, (energies, lanes), 0)
    col = lax.broadcasted_iota(jnp.int32, (energies, lanes), 1)
    for side in range(sides):
        base = own_edge(ids[1], side, sides, energies)
        picks = [(row - base == col - kk * SMAX) & (col >= kk * SMAX) & (col < (kk + 1) * SMAX) for kk in range(k)]
        pick = jnp.concatenate([jnp.where(p, 1.0, 0.0) for p in picks], axis=0).astype(BF)
        for r in range(nz):
            wide = jnp.concatenate([pieces[r][kk] for kk in range(k)], axis=1)
            outs[2 * side + r // half][r % half] = jnp.dot(wide, pick, preferred_element_type=F32).astype(BF)


def halo_pack(ids, pieces, sides, waits):
    nz = len(pieces)
    k, rows, energies = pieces[0].shape
    out = jax.ShapeDtypeStruct((nz // 2, rows, k * SMAX), BF)
    return pl.pallas_call(
        functools.partial(halo_kernel, nz, sides),
        out_shape=(out,) * (2 * sides),
        in_specs=[smem()] + [vmem()] * nz + [anywhere()] * len(waits),
        out_specs=(vmem(),) * (2 * sides),
        compiler_params=params(),
        cost_estimate=cost(2 * sides * out.size * k * energies, nz * pieces[0].size * 2),
    )(ids, *pieces, *waits)


def table_kernel(nz, k, energies, sides, off_ref, emit_ref, absorb_ref, ids, *refs):
    main, halos, done, own, edge = refs[0], refs[1:1 + sides], refs[1 + sides], refs[2 + sides], refs[3 + sides]
    done[...] = jnp.zeros_like(done)
    phonons = off_ref.shape[0]
    total = nz * k
    pairs = total // 2

    def lag_matrix(lag, sources, first):
        distance = lax.broadcasted_iota(jnp.int32, (sources, energies), 1) - lax.broadcasted_iota(jnp.int32, (sources, energies), 0) - first
        value = jnp.zeros((sources, energies), F32)
        for w in range(phonons):
            value = jnp.where(distance == off_ref[w], emit_ref[w, lag], value)
            value = jnp.where(distance == -off_ref[w], absorb_ref[w, lag], value)
        return value.astype(BF)

    def step(lag, carry):
        own[lag] = lag_matrix(lag, energies, 0)
        for side in range(sides):
            edge[side, lag] = lag_matrix(lag, SMAX, far_edge(ids[1], side, sides, energies))
        return carry

    lax.fori_loop(0, total, step, 0)
    for i in range(2 * pairs - 1):
        m = 2 * (pairs - 1 - i)
        for a in range(2):
            for b in range(2):
                at = i * 2 * energies + a * energies
                main[at:at + energies, b * energies:(b + 1) * energies] = own[(m + b - a) % total]
    per = k // 2
    for side in range(sides):
        for par in range(per):
            for i in range(2 * nz - 1):
                m = 2 * (per * (nz - 1 - i) + par)
                for a in range(k):
                    for b in range(2):
                        at = i * k * SMAX + a * SMAX
                        halos[side][par, at:at + SMAX, b * energies:(b + 1) * energies] = edge[side, (m + b - a) % total]


def tables(offsets, emit, absorb, ids, sides, nz, k, energies):
    total = nz * k
    main = jax.ShapeDtypeStruct(((total - 1) * 2 * energies, 2 * energies), BF)
    halo = jax.ShapeDtypeStruct((k // 2, (2 * nz - 1) * k * SMAX, 2 * energies), BF)
    return pl.pallas_call(
        functools.partial(table_kernel, nz, k, energies, sides),
        out_shape=(main,) + (halo,) * sides + (token(),),
        in_specs=[smem()] * 4,
        out_specs=(vmem(),) * (2 + sides),
        scratch_shapes=[pltpu.VMEM((total, energies, energies), BF), pltpu.VMEM((sides, total, SMAX, energies), BF)],
        compiler_params=params(),
        cost_estimate=cost(total * energies * energies * 100, main.size * 2),
    )(offsets, emit.astype(F32), absorb.astype(F32), ids)


def sum_kernel(nz, sides, *refs):
    pieces, refs = refs[:nz], refs[nz:]
    halos, refs = refs[:2 * sides], refs[2 * sides:]
    main, refs = refs[0], refs[1:]
    edges, refs = refs[:sides], refs[sides:]
    outs, done, wide = refs[-nz - 2:-2], refs[-2], refs[-1]
    done[...] = jnp.zeros_like(done)
    k, rows, energies = pieces[0].shape
    total = nz * k
    pairs = total // 2
    per = k // 2
    strip = k * SMAX
    inner = total * energies
    for q in range(nz):
        piece = pieces[(nz - q) % nz]
        for kk in range(k):
            wide[:, (q * k + kk) * energies:(q * k + kk + 1) * energies] = piece[kk]
        for side in range(sides):
            at = inner + (side * nz + q) * strip
            r = (nz - q) % nz
            wide[:, at:at + strip] = halos[2 * side + r // (nz // 2)][r % (nz // 2)]
    for pair in range(pairs):
        top = (pairs - 1 - pair) * 2 * energies
        value = jnp.dot(wide[:, :inner], main[top:top + inner, :], preferred_element_type=F32)
        for side in range(sides):
            at = inner + side * nz * strip
            start = (nz - 1 - pair // per) * strip
            value += jnp.dot(wide[:, at:at + nz * strip], edges[side][pair % per, start:start + nz * strip, :], preferred_element_type=F32)
        value = value.astype(BF)
        for b in range(2):
            outs[pair // per][2 * (pair % per) + b] = value[:, b * energies:(b + 1) * energies]


def phonon_sum(pieces, halos, main, edges, waits):
    nz, sides = len(pieces), len(halos) // 2
    k, rows, energies = pieces[0].shape
    out = jax.ShapeDtypeStruct((k, rows, energies), BF)
    depth = nz * k * energies + sides * nz * k * SMAX
    return pl.pallas_call(
        functools.partial(sum_kernel, nz, sides),
        out_shape=(out,) * nz + (token(),),
        in_specs=[vmem()] * (nz + 2 * sides + 1 + sides) + [anywhere()] * len(waits),
        out_specs=(vmem(),) * (nz + 1),
        scratch_shapes=[pltpu.VMEM((rows, depth), BF)],
        compiler_params=params(),
        cost_estimate=cost(2 * rows * depth * nz * k * energies, main.size * 2),
    )(*pieces, *halos, main, *edges, *waits)


def coupling_kernel(slots, nz, inner_atoms, atoms, skip, ids, near_ref, c_ref, wait, outer, inner, done, total):
    atom = pl.program_id(0) + skip
    done[...] = jnp.zeros_like(done)
    blocks = c_ref[0]
    depth, orb = blocks.shape
    comp = total.shape[1]

    def iotas(rows, cols):
        return lax.broadcasted_iota(jnp.int32, (rows, cols), 0), lax.broadcasted_iota(jnp.int32, (rows, cols), 1)

    def picks(condition):
        return jnp.where(condition, 1.0, 0.0).astype(BF)

    def over(index):
        return lax.shift_right_logical(index * (4096 // orb + 1), 12)

    row, col = iotas(orb, comp)
    left = jnp.dot(blocks, picks(row == over(col)), preferred_element_type=F32).astype(BF)
    right = jnp.dot(blocks, picks(row == col - over(col) * orb), preferred_element_type=F32).astype(BF)
    total[...] = jnp.zeros_like(total)
    row, col = iotas(comp, depth)
    for n in range(slots):
        spread_left = jnp.dot(picks(col == over(row) * slots + n), left, preferred_element_type=F32)
        spread_right = jnp.dot(picks(col == (row - over(row) * orb) * slots + n), right, preferred_element_type=F32)
        total[near_ref[atom, n] - ids[2] + REACH] += spread_left * spread_right

    def side_by_side(indices, width):
        row, col = iotas(comp, width)
        value = None
        for i, index in enumerate(indices):
            term = jnp.dot(total[index].astype(BF), picks(col == row + i * comp), preferred_element_type=F32)
            value = term if value is None else value + term
        return value.astype(BF)

    start = jnp.where(atom < 2 * REACH, 0, atoms)
    outer[0] = side_by_side([start + i for i in range(2 * REACH)], outer.shape[2])
    turns = [2 * REACH + i // nz * nz + lax.rem(ids[0] + nz - i % nz, nz) for i in range(inner_atoms)]
    inner[0] = side_by_side(turns, inner.shape[2])


def coupling_matrices(ids, nz, neighbours, coupling, skip, count, wait):
    atoms, slots, orb, _ = coupling.shape
    comp = orb * orb
    inner_atoms = atoms - 2 * REACH
    blocks = jnp.transpose(coupling, (0, 2, 1, 3)).reshape(atoms, orb * slots, orb)

    def out(blocks_wide):
        return jax.ShapeDtypeStruct((count, comp, blocks_wide * comp), BF), pl.BlockSpec((1, comp, blocks_wide * comp), lambda a: (a, 0, 0))

    outer, outer_spec = out(2 * REACH)
    inner, inner_spec = out(inner_atoms)
    done_spec = pl.BlockSpec(token().shape, lambda a: (0, 0))
    return pl.pallas_call(
        functools.partial(coupling_kernel, slots, nz, inner_atoms, atoms, skip),
        grid=(count,),
        out_shape=(outer, inner, token()),
        in_specs=[smem(), smem(), pl.BlockSpec((1, orb * slots, orb), lambda a: (a + skip, 0, 0)), anywhere()],
        out_specs=(outer_spec, inner_spec, done_spec),
        scratch_shapes=[pltpu.VMEM((atoms + 2 * REACH, comp, comp), F32)],
        compiler_params=params(),
        cost_estimate=cost(0, 0),
    )(ids, neighbours, blocks, wait)


def edge_kernel(nz, ids, *refs):
    pieces, low, high = refs[:nz], refs[-2], refs[-1]
    for r in range(nz):
        turn = lax.rem(ids[0] + nz - r, nz)
        for j in range(2 * REACH):
            target = low if j < REACH else high

            @pl.when(turn == j)
            def _(r=r, j=j, target=target):
                target[j % REACH] = pieces[r][...]


def edge_pack(ids, pieces, waits):
    nz = len(pieces)
    out = jax.ShapeDtypeStruct((REACH,) + pieces[0].shape, BF)
    return pl.pallas_call(
        functools.partial(edge_kernel, nz),
        out_shape=(out, out),
        in_specs=[smem()] + [vmem()] * nz + [anywhere()] * len(waits),
        out_specs=(vmem(), vmem()),
        compiler_params=params(),
        cost_estimate=cost(0, nz * pieces[0].size * 4),
    )(ids, *pieces, *waits)


def arrive_kernel(*refs):
    refs[-1][...] = jnp.zeros_like(refs[-1])


def arrive(pieces):
    return pl.pallas_call(
        arrive_kernel,
        out_shape=token(),
        in_specs=[anywhere()] * len(pieces),
        out_specs=vmem(),
        compiler_params=params(),
        cost_estimate=pl.CostEstimate(flops=40 * 10**9, bytes_accessed=0, transcendentals=0),
    )(*pieces)


def apply_kernel(before, low, high, after, *refs):
    pieces, (outer_low, outer_high, inner_low, inner_high, _, out) = refs[:-6], refs[-6:]
    _, atoms, comp, energies = out.shape
    edge = 2 * REACH * comp
    half = inner_low.shape[0]
    rows = pl.ds(pl.multiple_of(pl.program_id(0) * comp, 16), comp)
    k = pl.program_id(1) * 2

    def window(refs):
        return jnp.concatenate([jnp.concatenate([r[k, rows, :], r[k + 1, rows, :]], axis=1) for r in refs], axis=0)

    def put(value, first):
        for a in range(value.shape[0] // comp):
            for b in range(2):
                out[b, first + a] = value[a * comp:(a + 1) * comp, b * energies:(b + 1) * energies]

    inside = window(pieces)
    value = jnp.dot(inner_low[:, :inside.shape[0]], inside, preferred_element_type=F32)
    value_edge = jnp.dot(outer_low[:edge, :edge], window([before.at[0], before.at[1], low.at[0], low.at[1]]), preferred_element_type=F32)
    put(value[:edge] + value_edge, 0)
    if half > edge:
        put(value[edge:], 2 * REACH)
    value = jnp.dot(inner_high[:, :inside.shape[0]], inside, preferred_element_type=F32)
    value_edge = jnp.dot(outer_high[half - edge:, :edge], window([high.at[0], high.at[1], after.at[0], after.at[1]]), preferred_element_type=F32)
    if half > edge:
        put(value[:half - edge], atoms // 2)
    put(value[half - edge:] + value_edge, atoms - 2 * REACH)


def apply_couplings(before, low, high, after, pieces, outers, inners, wait, shape):
    k, atoms, comps, energies = shape
    comp = comps // 2
    matrices = [m.reshape(-1, m.shape[2]) for m in (*outers, *inners)]
    return pl.pallas_call(
        apply_kernel,
        grid=(2, k // 2),
        out_shape=jax.ShapeDtypeStruct(shape, F32),
        in_specs=[vmem()] * (4 + len(pieces) + len(matrices) + 1),
        out_specs=pl.BlockSpec((2, atoms, comp, energies), lambda c, kk: (kk, 0, c, 0)),
        compiler_params=params(),
        cost_estimate=cost(0, 0),
    )(before, low, high, after, *pieces, *matrices, wait)


def shards(green, neighbours, offsets, emit_weight, absorb_weight, coupling):
    k, atoms, comps, energies = green.shape
    nz, ne, ny = (lax.axis_size(axis) for axis in ("momentum", "energy", "atom"))
    groups = atoms // nz
    ids = jnp.stack([lax.axis_index("momentum"), lax.axis_index("energy"), lax.axis_index("atom") * atoms]).astype(jnp.int32)
    green, ids = lax.optimization_barrier((green, ids))

    def around(array, r):
        return lax.ppermute(array, "momentum", [(i, (i + r) % nz) for i in range(nz)])

    if ne == 2:
        routes = [[(0, 1), (1, 0)]]
    else:
        routes = [[(i, i + 1) for i in range(ne - 1)], [(i + 1, i) for i in range(ne - 1)]]
    sides = len(routes)

    def send(group, *waits):
        if group == 0:
            sent = [lax.dynamic_index_in_dim(green, atom_of(group * nz + lax.rem(ids[0] + r, nz), atoms), 1, keepdims=False) for r in range(nz)]
        else:
            sent = pack(ids, green, nz, group, waits)
        return spread(sent, ([[1, 2, 3], [1, 2, 3], [1, 2, 3], [1, 2, 3]])[group])

    def spread(sent, order):
        there = {r: around(sent[r], r) for r in order}
        return [sent[0]] + [there[r] for r in range(1, nz)]

    got = [send(0)]
    main, *edges, done = tables(offsets, emit_weight, absorb_weight, ids, sides, nz, k, energies)
    half = atoms // 2
    outer_low, inner_low, done = coupling_matrices(ids, nz, neighbours, coupling, 0, half, done)
    for group in range(1, groups):
        got.append(send(group, done))
    outer_high, inner_high, done = coupling_matrices(ids, nz, neighbours, coupling, half, half, done)

    waits = [done]
    back = []
    for group in range(groups):
        halos = halo_pack(ids, got[group], sides, waits)
        halos = [lax.ppermute(h, "energy", routes[i // 2]) for i, h in enumerate(halos)]
        *sums, sum_done = phonon_sum(got[group], halos, main, edges, [back[-1][r] for r in [2]] if back else [])
        waits = [sum_done]
        back.append(spread(sums, ([[1, 2, 3], [1, 2, 3], [1, 2, 3], [1, 2, 3]])[2 + group]))

    low, high = edge_pack(ids, back[0], waits)
    after = lax.ppermute(low, "atom", [(i + 1, i) for i in range(ny - 1)])
    before = lax.ppermute(high, "atom", [(i, i + 1) for i in range(ny - 1)])
    pieces = [piece for group in back[1:] for piece in group]
    return apply_couplings(before, low, high, after, pieces, (outer_low, outer_high), (inner_low, inner_high), arrive([p for group in back[1:] for p in group[1:]]), green.shape)


def solution(mesh):
    in_specs = (
        P("momentum", "atom", None, "energy"),
        P("atom", None),
        P(),
        P(),
        P(),
        P("atom", None, None, None),
    )
    out_specs = P("momentum", "atom", None, "energy")
    return jax.shard_map(shards, mesh=mesh, in_specs=in_specs, out_specs=out_specs, check_vma=False)
```

time: 117 us -> 113 us (0.966)
  local copies, waits for them, and re-layouts: 10.4 us -> 1.34 us
  waiting for transfers between devices: 36.2 us -> 41.5 us
  Pallas kernels: 35.1 us -> 33.3 us
  starting transfers between devices: 33.8 us -> 35.2 us
    ppermute x12, waiting for transfers between devices: 25 us -> 32.5 us  [around(): lax.ppermute(array, 'momentum', [(i, (i + r) % nz) for i in range(nz)])]
    unnamed x34 -> x10, local copies, waits for them, and re-layouts: 6.38 us -> 0.02 us
    ppermute x1, waiting for transfers between devices: 4.4 us -> 1.98 us  [shards(): after = lax.ppermute(low, 'atom', [(i + 1, i) for i in range(ny - 1)])]
    pallas_call x2, Pallas kernels: 8.65 us -> 6.49 us  [phonon_sum(): pl.pallas_call(functools.partial(sum_kernel, nz, sides), out_shape=(out,)...]
    ppermute x12, starting transfers between devices: 15.6 us -> 17.6 us  [around(): lax.ppermute(array, 'momentum', [(i, (i + r) % nz) for i in range(nz)])]
    squeeze x5 -> x1, local copies, waits for them, and re-layouts: 3.17 us -> 1.32 us  [send(): lax.dynamic_index_in_dim(green, atom_of(group * nz + lax.rem(ids[0] + r,...]
  transfers between devices with their start and end apart: 18 -> 18, of which waited for: 11 -> 14; matrix products, arithmetic and copies ran while one was open for 2% -> 1% of each run, Pallas kernels for 25% -> 25%
where the time goes in v2:
time: 113 us
  waiting for transfers between devices  41.5 us (37%)
  starting transfers between devices  35.2 us (31%)
  Pallas kernels  33.3 us (29%)
  local copies, waits for them, and re-layouts  1.34 us (1%)
    ppermute x12, waiting for transfers between devices, around(): lax.ppermute(array, 'momentum', [(i, (i + r) % nz) for i in range(nz)])  32.5 us
    ppermute x12, starting transfers between devices, around(): lax.ppermute(array, 'momentum', [(i, (i + r) % nz) for i in range(nz)])  17.6 us
    pallas_call x2, Pallas kernels, coupling_matrices(): pl.pallas_call(functools.partial(coupling_kernel, slots, nz, inner_atoms,...  13.5 us
    ppermute x1, starting transfers between devices, shards(): before = lax.ppermute(high, 'atom', [(i, i + 1) for i in range(ny - 1)])  12.6 us
    ppermute x4, waiting for transfers between devices, shards(): lax.ppermute(h, 'energy', routes[i // 2])  7.04 us
    pallas_call x2, Pallas kernels, phonon_sum(): pl.pallas_call(functools.partial(sum_kernel, nz, sides), out_shape=(out,)...  6.49 us
    pallas_call x1, Pallas kernels, apply_couplings(): pl.pallas_call(apply_kernel, grid=(2, k // 2), out_shape=jax.ShapeDtypeSt...  5.41 us
    pallas_call x1, Pallas kernels, tables(): pl.pallas_call(functools.partial(table_kernel, nz, k, energies, sides), o...  4.37 us
  transfers between devices with their start and end apart: 18, of which 14 were waited for; matrix products, arithmetic and copies ran while one was open for 1% of the time, Pallas kernels for 25%

profile of v2, /device:TPU:9, one launch (start us, length us, event | category | flops | bytes accessed | tf_op | source)
XLA Modules:
  0.0 112.5 jit_solution(4612181264700588496)
XLA Ops:
  0.0 0.0 copy-start
  0.0 0.0 copy-start.4
  0.0 0.0 copy-start.3
  0.0 0.0 copy-start.2
  0.0 0.0 copy-start.1
  0.0 0.1 pad_add_fusion.ids
  0.4 1.3 %dynamic-slice_bitcast_fusion = (bf16[4,288,128]{2,1,0:T(8,128)(2,1)S(1)}, bf16[4,288,128]{2,1,0:T(8,128)(2,1)S(1)}, bf16[4,288,128]{2,1,0:T(8,128)(2,1)S(1)}, bf16[4,288,128]{2,1,0:T(8,128)(2,1)S(1)}) fusion(bf16[4,8,288,128]{3,2,1,0:T(8,128)(2,1)} %green, s32[]{:T(128)S(6)} %select_n.49, s32[]{:T(128)S(6)} %select_n.46, s32[]{:T(128)S(6)} %select_n.43, ...), kind=kLoop, calls=%fused_computation | loop fusion | bytes 2359312 | tf_op jit(solution)/shard_map/jit(dynamic_index_in_dim)/squeeze | solution.py:382
  1.7 0.1 collective-permute-start.2
  1.8 2.5 %collective-permute-start.1 = (bf16[4,288,128]{2,1,0:T(8,128)(2,1)S(1)}, bf16[4,288,128]{2,1,0:T(8,128)(2,1)S(1)}, u32[]{:S(2)}, u32[]{:S(2)}) collective-permute-start(bf16[4,288,128]{2,1,0:T(8,128)(2,1)S(1)} %get-tuple-element.68), channel_id=1, source_target_pairs={{0,8},{4,12},{8,0},{12,4},{1,9},{5,13},{9,1},{13,5},{2,10},{6,14},... | collective-permute-start | bytes 884744 | tf_op jit(solution)/shard_map/ppermute | solution.py:372
  4.2 2.2 %collective-permute-start = (bf16[4,288,128]{2,1,0:T(8,128)(2,1)S(1)}, bf16[4,288,128]{2,1,0:T(8,128)(2,1)S(1)}, u32[]{:S(2)}, u32[]{:S(2)}) collective-permute-start(bf16[4,288,128]{2,1,0:T(8,128)(2,1)S(1)} %get-tuple-element.69), channel_id=1, source_target_pairs={{0,4},{4,8},{8,12},{12,0},{1,5},{5,9},{9,13},{13,1},{2,6},{6,10},{... | collective-permute-start | bytes 884744 | tf_op jit(solution)/shard_map/ppermute | solution.py:372
  6.4 0.0 copy-done.4
  6.5 0.7 convert_element_type.7.absorb_ref
  7.1 0.0 copy-done.3
  7.1 4.4 %shard_map.64 = (bf16[3840,256]{1,0:T(8,128)(2,1)S(1)}, bf16[2,896,256]{2,1,0:T(8,128)(2,1)S(1)}, f32[8,128]{1,0:T(8,128)S(1)}) custom-call(s32[16]{0:T(128)S(1)} %copy-done.3, f32[16,16]{1,0:T(8,128)S(1)} %convert_element_type.6.emit_ref, f32[16,16]{1,0:T(8,128)S(1)} %convert_element_type.7.absorb_ref, s32[3]{0:T(128)S(1)} %pad_add_fusion.ids), custom_call_target="tpu_custom_call" | custom-call | tf_op jit(solution)/shard_map/pallas_call | solution.py:156
  11.5 0.0 copy-done.2
  11.5 0.0 copy-done.1
  11.5 6.8 %shard_map.65 = (bf16[4,144,576]{2,1,0:T(8,128)(2,1)S(1)}, bf16[4,144,576]{2,1,0:T(8,128)(2,1)S(1)}, f32[8,128]{1,0:T(8,128)S(1)}) custom-call(s32[3]{0:T(128)S(1)} %pad_add_fusion.ids, s32[8,8]{1,0:T(8,128)S(1)} %copy-done.2, bf16[8,96,12]{2,1,0:T(8,128)(2,1)S(1)} %bitcast.20, f32[8,128]{1,0:T(8,128)S(1)} %get-tuple-element.38.wait), custom_call_target="tpu_custom_call" | custom-call | tf_op jit(solution)/shard_map/pallas_call | solution.py:268
  18.3 0.0 copy-done
  18.3 0.7 shard_map.69
  19.1 0.1 collective-permute-start.8
  19.1 1.3 %collective-permute-start.9 = (bf16[4,288,128]{2,1,0:T(8,128)(2,1)S(1)}, bf16[4,288,128]{2,1,0:T(8,128)(2,1)S(1)}, u32[]{:S(2)}, u32[]{:S(2)}) collective-permute-start(bf16[4,288,128]{2,1,0:T(8,128)(2,1)S(1)} %get-tuple-element.51), channel_id=1, source_target_pairs={{0,8},{4,12},{8,0},{12,4},{1,9},{5,13},{9,1},{13,5},{2,10},{6,14},... | collective-permute-start | bytes 884744 | tf_op jit(solution)/shard_map/ppermute | solution.py:372
  20.5 6.8 %shard_map.66 = (bf16[4,144,576]{2,1,0:T(8,128)(2,1)S(1)}, bf16[4,144,576]{2,1,0:T(8,128)(2,1)S(1)}, f32[8,128]{1,0:T(8,128)S(1)}) custom-call(s32[3]{0:T(128)S(1)} %pad_add_fusion.ids, s32[8,8]{1,0:T(8,128)S(1)} %copy-done.2, bf16[8,96,12]{2,1,0:T(8,128)(2,1)S(1)} %bitcast.21, f32[8,128]{1,0:T(8,128)S(1)} %get-tuple-element.39.wait.refs_0_), custom_call_target="tpu_custom_call" | custom-call | tf_op jit(solution)/shard_map/pallas_call | solution.py:268
  27.2 0.0 collective-permute-done.2.refs_3_
  27.2 1.1 collective-permute-start.10
  28.3 0.0 collective-permute-done.1.refs_2_
  28.3 0.9 collective-permute-done.refs_1_
  29.2 1.0 shard_map.67
  30.3 1.3 %collective-permute-start.3 = (bf16[2,288,128]{2,1,0:T(8,128)(2,1)S(1)}, bf16[2,288,128]{2,1,0:T(8,128)(2,1)S(1)}, u32[]{:S(2)}, u32[]{:S(2)}) collective-permute-start(bf16[2,288,128]{2,1,0:T(8,128)(2,1)S(1)} %get-tuple-element.41), channel_id=1, source_target_pairs={{0,16},{16,0},{1,17},{17,1},{2,18},{18,2},{3,19},{19,3},{4,20},{20... | collective-permute-start | bytes 442376 | tf_op jit(solution)/shard_map/ppermute | solution.py:403
  31.5 0.3 collective-permute-start.4
  31.8 2.8 %collective-permute-done.3.refs_4_ = bf16[2,288,128]{2,1,0:T(8,128)(2,1)S(1)} collective-permute-done((bf16[2,288,128]{2,1,0:T(8,128)(2,1)S(1)}, bf16[2,288,128]{2,1,0:T(8,128)(2,1)S(1)}, u32[]{:S(2)}, u32[]{:S(2)}) %collective-permute-start.3) | collective-permute-done | bytes 147488 | tf_op jit(solution)/shard_map/ppermute | solution.py:403
  34.6 1.6 %collective-permute-done.4.refs_5_ = bf16[2,288,128]{2,1,0:T(8,128)(2,1)S(1)} collective-permute-done((bf16[2,288,128]{2,1,0:T(8,128)(2,1)S(1)}, bf16[2,288,128]{2,1,0:T(8,128)(2,1)S(1)}, u32[]{:S(2)}, u32[]{:S(2)}) %collective-permute-start.4) | collective-permute-done | bytes 147488 | tf_op jit(solution)/shard_map/ppermute | solution.py:403
  36.2 3.2 %shard_map.68 = (bf16[4,288,128]{2,1,0:T(8,128)(2,1)S(1)}, bf16[4,288,128]{2,1,0:T(8,128)(2,1)S(1)}, bf16[4,288,128]{2,1,0:T(8,128)(2,1)S(1)}, bf16[4,288,128]{2,1,0:T(8,128)(2,1)S(1)}, f32[8,128]{1,0:T(8,128)S(1)}) custom-call(bf16[4,288,128]{2,1,0:T(8,128)(2,1)S(1)} %get-tuple-element.70.refs_0_, bf16[4,288,128]{2,1,0:T(8,128)(2,1)S(1)} %collective-permute-done.refs_1_, ...), custom_call_target="tpu_custom_call" | custom-call | tf_op jit(solution)/shard_map/pallas_call | solution.py:205
  39.4 0.9 collective-permute-start.6
  40.3 7.9 %collective-permute-done.8.refs_1_ = bf16[4,288,128]{2,1,0:T(8,128)(2,1)S(1)} collective-permute-done((bf16[4,288,128]{2,1,0:T(8,128)(2,1)S(1)}, bf16[4,288,128]{2,1,0:T(8,128)(2,1)S(1)}, u32[]{:S(2)}, u32[]{:S(2)}) %collective-permute-start.8) | collective-permute-done | bytes 294944 | tf_op jit(solution)/shard_map/ppermute | solution.py:372
  48.2 9.5 %collective-permute-done.9.refs_2_ = bf16[4,288,128]{2,1,0:T(8,128)(2,1)S(1)} collective-permute-done((bf16[4,288,128]{2,1,0:T(8,128)(2,1)S(1)}, bf16[4,288,128]{2,1,0:T(8,128)(2,1)S(1)}, u32[]{:S(2)}, u32[]{:S(2)}) %collective-permute-start.9) | collective-permute-done | bytes 294944 | tf_op jit(solution)/shard_map/ppermute | solution.py:372
  57.7 2.6 %collective-permute-done.10.refs_3_ = bf16[4,288,128]{2,1,0:T(8,128)(2,1)S(1)} collective-permute-done((bf16[4,288,128]{2,1,0:T(8,128)(2,1)S(1)}, bf16[4,288,128]{2,1,0:T(8,128)(2,1)S(1)}, u32[]{:S(2)}, u32[]{:S(2)}) %collective-permute-start.10) | collective-permute-done | bytes 294944 | tf_op jit(solution)/shard_map/ppermute | solution.py:372
  60.2 1.0 shard_map.70
  61.3 1.3 %collective-permute-start.11 = (bf16[2,288,128]{2,1,0:T(8,128)(2,1)S(1)}, bf16[2,288,128]{2,1,0:T(8,128)(2,1)S(1)}, u32[]{:S(2)}, u32[]{:S(2)}) collective-permute-start(bf16[2,288,128]{2,1,0:T(8,128)(2,1)S(1)} %get-tuple-element.54), channel_id=1, source_target_pairs={{0,16},{16,0},{1,17},{17,1},{2,18},{18,2},{3,19},{19,3},{4,20},{20... | collective-permute-start | bytes 442376 | tf_op jit(solution)/shard_map/ppermute | solution.py:403
  62.5 0.3 collective-permute-start.12
  62.8 0.0 collective-permute-start.5
  62.8 1.5 %collective-permute-start.7 = (bf16[4,288,128]{2,1,0:T(8,128)(2,1)S(1)}, bf16[4,288,128]{2,1,0:T(8,128)(2,1)S(1)}, u32[]{:S(2)}, u32[]{:S(2)}) collective-permute-start(bf16[4,288,128]{2,1,0:T(8,128)(2,1)S(1)} %get-tuple-element.48), channel_id=1, source_target_pairs={{0,12},{4,0},{8,4},{12,8},{1,13},{5,1},{9,5},{13,9},{2,14},{6,2},{... | collective-permute-start | bytes 884744 | tf_op jit(solution)/shard_map/ppermute | solution.py:372
  64.3 1.1 collective-permute-done.11.refs_4_
  65.3 1.6 %collective-permute-done.12.refs_5_ = bf16[2,288,128]{2,1,0:T(8,128)(2,1)S(1)} collective-permute-done((bf16[2,288,128]{2,1,0:T(8,128)(2,1)S(1)}, bf16[2,288,128]{2,1,0:T(8,128)(2,1)S(1)}, u32[]{:S(2)}, u32[]{:S(2)}) %collective-permute-start.12) | collective-permute-done | bytes 147488 | tf_op jit(solution)/shard_map/ppermute | solution.py:403
  66.9 0.3 collective-permute-done.6.refs_8_.refs_2_
  67.2 3.3 %shard_map.71 = (bf16[4,288,128]{2,1,0:T(8,128)(2,1)S(1)}, bf16[4,288,128]{2,1,0:T(8,128)(2,1)S(1)}, bf16[4,288,128]{2,1,0:T(8,128)(2,1)S(1)}, bf16[4,288,128]{2,1,0:T(8,128)(2,1)S(1)}, f32[8,128]{1,0:T(8,128)S(1)}) custom-call(bf16[4,288,128]{2,1,0:T(8,128)(2,1)S(1)} %get-tuple-element.49.refs_0_, bf16[4,288,128]{2,1,0:T(8,128)(2,1)S(1)} %collective-permute-done.8.refs_1_, ...), custom_call_target="tpu_custom_call" | custom-call | tf_op jit(solution)/shard_map/pallas_call | solution.py:205
  70.5 3.6 %collective-permute-start.15 = (bf16[4,288,128]{2,1,0:T(8,128)(2,1)S(1)}, bf16[4,288,128]{2,1,0:T(8,128)(2,1)S(1)}, u32[]{:S(2)}, u32[]{:S(2)}) collective-permute-start(bf16[4,288,128]{2,1,0:T(8,128)(2,1)S(1)} %get-tuple-element.60), channel_id=1, source_target_pairs={{0,4},{4,8},{8,12},{12,0},{1,5},{5,9},{9,13},{13,1},{2,6},{6,10},{... | collective-permute-start | bytes 884744 | tf_op jit(solution)/shard_map/ppermute | solution.py:372
  74.1 4.5 %collective-permute-start.16 = (bf16[4,288,128]{2,1,0:T(8,128)(2,1)S(1)}, bf16[4,288,128]{2,1,0:T(8,128)(2,1)S(1)}, u32[]{:S(2)}, u32[]{:S(2)}) collective-permute-start(bf16[4,288,128]{2,1,0:T(8,128)(2,1)S(1)} %get-tuple-element.61), channel_id=1, source_target_pairs={{0,8},{4,12},{8,0},{12,4},{1,9},{5,13},{9,1},{13,5},{2,10},{6,14},... | collective-permute-start | bytes 884744 | tf_op jit(solution)/shard_map/ppermute | solution.py:372
  78.6 0.0 collective-permute-start.17
  78.6 1.3 %collective-permute-done.5.refs_1_ = bf16[4,288,128]{2,1,0:T(8,128)(2,1)S(1)} collective-permute-done((bf16[4,288,128]{2,1,0:T(8,128)(2,1)S(1)}, bf16[4,288,128]{2,1,0:T(8,128)(2,1)S(1)}, u32[]{:S(2)}, u32[]{:S(2)}) %collective-permute-start.5) | collective-permute-done | bytes 294944 | tf_op jit(solution)/shard_map/ppermute | solution.py:372
  79.8 2.7 %collective-permute-done.7.refs_3_ = bf16[4,288,128]{2,1,0:T(8,128)(2,1)S(1)} collective-permute-done((bf16[4,288,128]{2,1,0:T(8,128)(2,1)S(1)}, bf16[4,288,128]{2,1,0:T(8,128)(2,1)S(1)}, u32[]{:S(2)}, u32[]{:S(2)}) %collective-permute-start.7) | collective-permute-done | bytes 294944 | tf_op jit(solution)/shard_map/ppermute | solution.py:372
  82.6 0.7 shard_map.72
  83.3 12.6 %collective-permute-start.13 = (bf16[2,4,288,128]{3,2,1,0:T(8,128)(2,1)S(1)}, bf16[2,4,288,128]{3,2,1,0:T(8,128)(2,1)S(1)}, u32[]{:S(2)}, u32[]{:S(2)}) collective-permute-start(bf16[2,4,288,128]{3,2,1,0:T(8,128)(2,1)S(1)} %get-tuple-element.57.high), channel_id=1, source_target_pairs={{0,1},{1,2},{2,3},{4,5},{5,6},{6,7},{8,9},{9,10},{10,11},{12,13},{... | collective-permute-start | bytes 1769480 | tf_op jit(solution)/shard_map/ppermute | solution.py:410
  95.9 1.9 %collective-permute-start.14 = (bf16[2,4,288,128]{3,2,1,0:T(8,128)(2,1)S(1)}, bf16[2,4,288,128]{3,2,1,0:T(8,128)(2,1)S(1)}, u32[]{:S(2)}, u32[]{:S(2)}) collective-permute-start(bf16[2,4,288,128]{3,2,1,0:T(8,128)(2,1)S(1)} %get-tuple-element.58.low), channel_id=1, source_target_pairs={{1,0},{2,1},{3,2},{5,4},{6,5},{7,6},{9,8},{10,9},{11,10},{13,12},{... | collective-permute-start | bytes 1769480 | tf_op jit(solution)/shard_map/ppermute | solution.py:409
  97.8 1.0 collective-permute-done.15.refs_0_.refs_1_
  98.8 6.3 %collective-permute-done.16.refs_1_.refs_2_ = bf16[4,288,128]{2,1,0:T(8,128)(2,1)S(1)} collective-permute-done((bf16[4,288,128]{2,1,0:T(8,128)(2,1)S(1)}, bf16[4,288,128]{2,1,0:T(8,128)(2,1)S(1)}, u32[]{:S(2)}, u32[]{:S(2)}) %collective-permute-start.16) | collective-permute-done | bytes 294944 | tf_op jit(solution)/shard_map/ppermute | solution.py:372
  105.1 0.0 collective-permute-done.17.refs_2_.refs_3_
  105.1 0.0 collective-permute-done.13.before
  105.1 2.0 %collective-permute-done.14.after = bf16[2,4,288,128]{3,2,1,0:T(8,128)(2,1)S(1)} collective-permute-done((bf16[2,4,288,128]{3,2,1,0:T(8,128)(2,1)S(1)}, bf16[2,4,288,128]{3,2,1,0:T(8,128)(2,1)S(1)}, u32[]{:S(2)}, u32[]{:S(2)}) %collective-permute-start.14) | collective-permute-done | bytes 589856 | tf_op jit(solution)/shard_map/ppermute | solution.py:409
  107.1 5.4 %shard_map.74 = f32[4,8,288,128]{3,2,1,0:T(8,128)} custom-call(bf16[2,4,288,128]{3,2,1,0:T(8,128)(2,1)S(1)} %collective-permute-done.13.before, bf16[2,4,288,128]{3,2,1,0:T(8,128)(2,1)S(1)} %get-tuple-element.58.low, bf16[2,4,288,128]{3,2,1,0:T(8,128)(2,1)S(1)} %get-tuple-element.57.high, bf16[2,4,288,128]{3,2,1,0:T(8,128)(2,1)S(1)} %collective-permute-done.14.after, ...), custom_call_target="tpu_custom_call" | custom-call | tf_op jit(solution)/shard_map/pallas_call | solution.py:353
  (2 shorter events, 0.0 us)
Async XLA Ops:
  0.0 18.3 %copy-start = (bf16[4,8,288,128]{3,2,1,0:T(8,128)(2,1)S(1)}, bf16[4,8,288,128]{3,2,1,0:T(8,128)(2,1)}, u32[]{:S(2)}) copy-start(bf16[4,8,288,128]{3,2,1,0:T(8,128)(2,1)} %green) | copy-start | bytes 7077892
  0.0 6.4 %copy-start.4 = (bf16[16,16]{1,0:T(8,128)(2,1)S(1)}, bf16[16,16]{1,0:T(8,128)(2,1)}, u32[]{:S(2)}) copy-start(bf16[16,16]{1,0:T(8,128)(2,1)} %param.9) | copy-start | bytes 1540
  0.0 7.1 %copy-start.3 = (s32[16]{0:T(128)S(1)}, s32[16]{0:T(128)}, u32[]{:S(2)}) copy-start(s32[16]{0:T(128)} %off_ref.1) | copy-start | bytes 196
  0.0 11.5 %copy-start.2 = (s32[8,8]{1,0:T(8,128)S(1)}, s32[8,8]{1,0:T(8,128)}, u32[]{:S(2)}) copy-start(s32[8,8]{1,0:T(8,128)} %near_ref.3) | copy-start | bytes 772
  0.0 11.5 %copy-start.1 = (bf16[8,8,12,12]{3,1,2,0:T(8,128)(2,1)S(1)}, bf16[8,8,12,12]{3,1,2,0:T(8,128)(2,1)}, u32[]{:S(2)}) copy-start(bf16[8,8,12,12]{3,1,2,0:T(8,128)(2,1)} %param.11) | copy-start | bytes 55300
  1.7 25.5 %collective-permute-start.2 = (bf16[4,288,128]{2,1,0:T(8,128)(2,1)S(1)}, bf16[4,288,128]{2,1,0:T(8,128)(2,1)S(1)}, u32[]{:S(2)}, u32[]{:S(2)}) collective-permute-start(bf16[4,288,128]{2,1,0:T(8,128)(2,1)S(1)} %get-tuple-element.67), channel_id=1, source_target_pairs={{0,12},{4,0},{8,4},{12,8},{1,13},{5,1},{9,5},{13,9},{2,14},{6,2},{... | collective-permute-start | bytes 884744 | tf_op jit(solution)/shard_map/ppermute | solution.py:372
  1.8 26.5 %collective-permute-start.1 = (bf16[4,288,128]{2,1,0:T(8,128)(2,1)S(1)}, bf16[4,288,128]{2,1,0:T(8,128)(2,1)S(1)}, u32[]{:S(2)}, u32[]{:S(2)}) collective-permute-start(bf16[4,288,128]{2,1,0:T(8,128)(2,1)S(1)} %get-tuple-element.68), channel_id=1, source_target_pairs={{0,8},{4,12},{8,0},{12,4},{1,9},{5,13},{9,1},{13,5},{2,10},{6,14},... | collective-permute-start | bytes 884744 | tf_op jit(solution)/shard_map/ppermute | solution.py:372
  4.2 25.0 %collective-permute-start = (bf16[4,288,128]{2,1,0:T(8,128)(2,1)S(1)}, bf16[4,288,128]{2,1,0:T(8,128)(2,1)S(1)}, u32[]{:S(2)}, u32[]{:S(2)}) collective-permute-start(bf16[4,288,128]{2,1,0:T(8,128)(2,1)S(1)} %get-tuple-element.69), channel_id=1, source_target_pairs={{0,4},{4,8},{8,12},{12,0},{1,5},{5,9},{9,13},{13,1},{2,6},{6,10},{... | collective-permute-start | bytes 884744 | tf_op jit(solution)/shard_map/ppermute | solution.py:372
  19.1 29.1 %collective-permute-start.8 = (bf16[4,288,128]{2,1,0:T(8,128)(2,1)S(1)}, bf16[4,288,128]{2,1,0:T(8,128)(2,1)S(1)}, u32[]{:S(2)}, u32[]{:S(2)}) collective-permute-start(bf16[4,288,128]{2,1,0:T(8,128)(2,1)S(1)} %get-tuple-element.50), channel_id=1, source_target_pairs={{0,4},{4,8},{8,12},{12,0},{1,5},{5,9},{9,13},{13,1},{2,6},{6,10},{... | collective-permute-start | bytes 884744 | tf_op jit(solution)/shard_map/ppermute | solution.py:372
  19.1 38.5 %collective-permute-start.9 = (bf16[4,288,128]{2,1,0:T(8,128)(2,1)S(1)}, bf16[4,288,128]{2,1,0:T(8,128)(2,1)S(1)}, u32[]{:S(2)}, u32[]{:S(2)}) collective-permute-start(bf16[4,288,128]{2,1,0:T(8,128)(2,1)S(1)} %get-tuple-element.51), channel_id=1, source_target_pairs={{0,8},{4,12},{8,0},{12,4},{1,9},{5,13},{9,1},{13,5},{2,10},{6,14},... | collective-permute-start | bytes 884744 | tf_op jit(solution)/shard_map/ppermute | solution.py:372
  27.2 33.0 %collective-permute-start.10 = (bf16[4,288,128]{2,1,0:T(8,128)(2,1)S(1)}, bf16[4,288,128]{2,1,0:T(8,128)(2,1)S(1)}, u32[]{:S(2)}, u32[]{:S(2)}) collective-permute-start(bf16[4,288,128]{2,1,0:T(8,128)(2,1)S(1)} %get-tuple-element.52), channel_id=1, source_target_pairs={{0,12},{4,0},{8,4},{12,8},{1,13},{5,1},{9,5},{13,9},{2,14},{6,2},{... | collective-permute-start | bytes 884744 | tf_op jit(solution)/shard_map/ppermute | solution.py:372
  30.3 4.4 %collective-permute-start.3 = (bf16[2,288,128]{2,1,0:T(8,128)(2,1)S(1)}, bf16[2,288,128]{2,1,0:T(8,128)(2,1)S(1)}, u32[]{:S(2)}, u32[]{:S(2)}) collective-permute-start(bf16[2,288,128]{2,1,0:T(8,128)(2,1)S(1)} %get-tuple-element.41), channel_id=1, source_target_pairs={{0,16},{16,0},{1,17},{17,1},{2,18},{18,2},{3,19},{19,3},{4,20},{20... | collective-permute-start | bytes 442376 | tf_op jit(solution)/shard_map/ppermute | solution.py:403
  31.5 4.7 %collective-permute-start.4 = (bf16[2,288,128]{2,1,0:T(8,128)(2,1)S(1)}, bf16[2,288,128]{2,1,0:T(8,128)(2,1)S(1)}, u32[]{:S(2)}, u32[]{:S(2)}) collective-permute-start(bf16[2,288,128]{2,1,0:T(8,128)(2,1)S(1)} %get-tuple-element.42), channel_id=1, source_target_pairs={{0,16},{16,0},{1,17},{17,1},{2,18},{18,2},{3,19},{19,3},{4,20},{20... | collective-permute-start | bytes 442376 | tf_op jit(solution)/shard_map/ppermute | solution.py:403
  39.4 27.8 %collective-permute-start.6 = (bf16[4,288,128]{2,1,0:T(8,128)(2,1)S(1)}, bf16[4,288,128]{2,1,0:T(8,128)(2,1)S(1)}, u32[]{:S(2)}, u32[]{:S(2)}) collective-permute-start(bf16[4,288,128]{2,1,0:T(8,128)(2,1)S(1)} %get-tuple-element.47), channel_id=1, source_target_pairs={{0,8},{4,12},{8,0},{12,4},{1,9},{5,13},{9,1},{13,5},{2,10},{6,14},... | collective-permute-start | bytes 884744 | tf_op jit(solution)/shard_map/ppermute | solution.py:372
  61.3 4.1 %collective-permute-start.11 = (bf16[2,288,128]{2,1,0:T(8,128)(2,1)S(1)}, bf16[2,288,128]{2,1,0:T(8,128)(2,1)S(1)}, u32[]{:S(2)}, u32[]{:S(2)}) collective-permute-start(bf16[2,288,128]{2,1,0:T(8,128)(2,1)S(1)} %get-tuple-element.54), channel_id=1, source_target_pairs={{0,16},{16,0},{1,17},{17,1},{2,18},{18,2},{3,19},{19,3},{4,20},{20... | collective-permute-start | bytes 442376 | tf_op jit(solution)/shard_map/ppermute | solution.py:403
  62.5 4.4 %collective-permute-start.12 = (bf16[2,288,128]{2,1,0:T(8,128)(2,1)S(1)}, bf16[2,288,128]{2,1,0:T(8,128)(2,1)S(1)}, u32[]{:S(2)}, u32[]{:S(2)}) collective-permute-start(bf16[2,288,128]{2,1,0:T(8,128)(2,1)S(1)} %get-tuple-element.55), channel_id=1, source_target_pairs={{0,16},{16,0},{1,17},{17,1},{2,18},{18,2},{3,19},{19,3},{4,20},{20... | collective-permute-start | bytes 442376 | tf_op jit(solution)/shard_map/ppermute | solution.py:403
  62.8 17.0 %collective-permute-start.5 = (bf16[4,288,128]{2,1,0:T(8,128)(2,1)S(1)}, bf16[4,288,128]{2,1,0:T(8,128)(2,1)S(1)}, u32[]{:S(2)}, u32[]{:S(2)}) collective-permute-start(bf16[4,288,128]{2,1,0:T(8,128)(2,1)S(1)} %get-tuple-element.46), channel_id=1, source_target_pairs={{0,4},{4,8},{8,12},{12,0},{1,5},{5,9},{9,13},{13,1},{2,6},{6,10},{... | collective-permute-start | bytes 884744 | tf_op jit(solution)/shard_map/ppermute | solution.py:372
  62.8 19.8 %collective-permute-start.7 = (bf16[4,288,128]{2,1,0:T(8,128)(2,1)S(1)}, bf16[4,288,128]{2,1,0:T(8,128)(2,1)S(1)}, u32[]{:S(2)}, u32[]{:S(2)}) collective-permute-start(bf16[4,288,128]{2,1,0:T(8,128)(2,1)S(1)} %get-tuple-element.48), channel_id=1, source_target_pairs={{0,12},{4,0},{8,4},{12,8},{1,13},{5,1},{9,5},{13,9},{2,14},{6,2},{... | collective-permute-start | bytes 884744 | tf_op jit(solution)/shard_map/ppermute | solution.py:372
  70.5 28.3 %collective-permute-start.15 = (bf16[4,288,128]{2,1,0:T(8,128)(2,1)S(1)}, bf16[4,288,128]{2,1,0:T(8,128)(2,1)S(1)}, u32[]{:S(2)}, u32[]{:S(2)}) collective-permute-start(bf16[4,288,128]{2,1,0:T(8,128)(2,1)S(1)} %get-tuple-element.60), channel_id=1, source_target_pairs={{0,4},{4,8},{8,12},{12,0},{1,5},{5,9},{9,13},{13,1},{2,6},{6,10},{... | collective-permute-start | bytes 884744 | tf_op jit(solution)/shard_map/ppermute | solution.py:372
  74.1 31.0 %collective-permute-start.16 = (bf16[4,288,128]{2,1,0:T(8,128)(2,1)S(1)}, bf16[4,288,128]{2,1,0:T(8,128)(2,1)S(1)}, u32[]{:S(2)}, u32[]{:S(2)}) collective-permute-start(bf16[4,288,128]{2,1,0:T(8,128)(2,1)S(1)} %get-tuple-element.61), channel_id=1, source_target_pairs={{0,8},{4,12},{8,0},{12,4},{1,9},{5,13},{9,1},{13,5},{2,10},{6,14},... | collective-permute-start | bytes 884744 | tf_op jit(solution)/shard_map/ppermute | solution.py:372
  78.6 26.6 %collective-permute-start.17 = (bf16[4,288,128]{2,1,0:T(8,128)(2,1)S(1)}, bf16[4,288,128]{2,1,0:T(8,128)(2,1)S(1)}, u32[]{:S(2)}, u32[]{:S(2)}) collective-permute-start(bf16[4,288,128]{2,1,0:T(8,128)(2,1)S(1)} %get-tuple-element.62), channel_id=1, source_target_pairs={{0,12},{4,0},{8,4},{12,8},{1,13},{5,1},{9,5},{13,9},{2,14},{6,2},{... | collective-permute-start | bytes 884744 | tf_op jit(solution)/shard_map/ppermute | solution.py:372
  83.3 21.8 %collective-permute-start.13 = (bf16[2,4,288,128]{3,2,1,0:T(8,128)(2,1)S(1)}, bf16[2,4,288,128]{3,2,1,0:T(8,128)(2,1)S(1)}, u32[]{:S(2)}, u32[]{:S(2)}) collective-permute-start(bf16[2,4,288,128]{3,2,1,0:T(8,128)(2,1)S(1)} %get-tuple-element.57.high), channel_id=1, source_target_pairs={{0,1},{1,2},{2,3},{4,5},{5,6},{6,7},{8,9},{9,10},{10,11},{12,13},{... | collective-permute-start | bytes 1769480 | tf_op jit(solution)/shard_map/ppermute | solution.py:410
  95.9 11.2 %collective-permute-start.14 = (bf16[2,4,288,128]{3,2,1,0:T(8,128)(2,1)S(1)}, bf16[2,4,288,128]{3,2,1,0:T(8,128)(2,1)S(1)}, u32[]{:S(2)}, u32[]{:S(2)}) collective-permute-start(bf16[2,4,288,128]{3,2,1,0:T(8,128)(2,1)S(1)} %get-tuple-element.58.low), channel_id=1, source_target_pairs={{1,0},{2,1},{3,2},{5,4},{6,5},{7,6},{9,8},{10,9},{11,10},{13,12},{... | collective-permute-start | bytes 1769480 | tf_op jit(solution)/shard_map/ppermute | solution.py:409

commit v3 on v2

--- a/solution.py
+++ b/solution.py
@@ -110,7 +110,7 @@
     )(ids, *pieces, *waits)
 
 
-def table_kernel(nz, k, energies, sides, off_ref, emit_ref, absorb_ref, ids, *refs):
+def table_kernel(nz, k, energies, sides, off_ref, emit_ref, absorb_ref, ids, _, *refs):
     main, halos, done, own, edge = refs[0], refs[1:1 + sides], refs[1 + sides], refs[2 + sides], refs[3 + sides]
     done[...] = jnp.zeros_like(done)
     phonons = off_ref.shape[0]
@@ -149,19 +149,19 @@
                         halos[side][par, at:at + SMAX, b * energies:(b + 1) * energies] = edge[side, (m + b - a) % total]
 
 
-def tables(offsets, emit, absorb, ids, sides, nz, k, energies):
+def tables(offsets, emit, absorb, ids, sides, nz, k, energies, wait):
     total = nz * k
     main = jax.ShapeDtypeStruct(((total - 1) * 2 * energies, 2 * energies), BF)
     halo = jax.ShapeDtypeStruct((k // 2, (2 * nz - 1) * k * SMAX, 2 * energies), BF)
     return pl.pallas_call(
         functools.partial(table_kernel, nz, k, energies, sides),
         out_shape=(main,) + (halo,) * sides + (token(),),
-        in_specs=[smem()] * 4,
+        in_specs=[smem()] * 4 + [anywhere()],
         out_specs=(vmem(),) * (2 + sides),
         scratch_shapes=[pltpu.VMEM((total, energies, energies), BF), pltpu.VMEM((sides, total, SMAX, energies), BF)],
         compiler_params=params(),
         cost_estimate=cost(total * energies * energies * 100, main.size * 2),
-    )(offsets, emit.astype(F32), absorb.astype(F32), ids)
+    )(offsets, emit.astype(F32), absorb.astype(F32), ids, wait)
 
 
 def sum_kernel(nz, sides, *refs):
@@ -213,7 +213,7 @@
     )(*pieces, *halos, main, *edges, *waits)
 
 
-def coupling_kernel(slots, nz, inner_atoms, atoms, skip, ids, near_ref, c_ref, wait, outer, inner, done, total):
+def coupling_kernel(slots, skip, ids, near_ref, c_ref, wait, out, done, total):
     atom = pl.program_id(0) + skip
     done[...] = jnp.zeros_like(done)
     blocks = c_ref[0]
@@ -247,30 +247,20 @@
             value = term if value is None else value + term
         return value.astype(BF)
 
-    start = jnp.where(atom < 2 * REACH, 0, atoms)
-    outer[0] = side_by_side([start + i for i in range(2 * REACH)], outer.shape[2])
-    turns = [2 * REACH + i // nz * nz + lax.rem(ids[0] + nz - i % nz, nz) for i in range(inner_atoms)]
-    inner[0] = side_by_side(turns, inner.shape[2])
-
-
-def coupling_matrices(ids, nz, neighbours, coupling, skip, count, wait):
+    out[0] = side_by_side([atom + i for i in range(2 * REACH + 1)], out.shape[2])
+
+
+def coupling_matrices(ids, neighbours, coupling, skip, count, wait):
     atoms, slots, orb, _ = coupling.shape
     comp = orb * orb
-    inner_atoms = atoms - 2 * REACH
+    wide = (2 * REACH + 1) * comp
     blocks = jnp.transpose(coupling, (0, 2, 1, 3)).reshape(atoms, orb * slots, orb)
-
-    def out(blocks_wide):
-        return jax.ShapeDtypeStruct((count, comp, blocks_wide * comp), BF), pl.BlockSpec((1, comp, blocks_wide * comp), lambda a: (a, 0, 0))
-
-    outer, outer_spec = out(2 * REACH)
-    inner, inner_spec = out(inner_atoms)
-    done_spec = pl.BlockSpec(token().shape, lambda a: (0, 0))
-    return pl.pallas_call(
-        functools.partial(coupling_kernel, slots, nz, inner_atoms, atoms, skip),
+    return pl.pallas_call(
+        functools.partial(coupling_kernel, slots, skip),
         grid=(count,),
-        out_shape=(outer, inner, token()),
+        out_shape=(jax.ShapeDtypeStruct((count, comp, wide), BF), token()),
         in_specs=[smem(), smem(), pl.BlockSpec((1, orb * slots, orb), lambda a: (a + skip, 0, 0)), anywhere()],
-        out_specs=(outer_spec, inner_spec, done_spec),
+        out_specs=(pl.BlockSpec((1, comp, wide), lambda a: (a, 0, 0)), pl.BlockSpec(token().shape, lambda a: (0, 0))),
         scratch_shapes=[pltpu.VMEM((atoms + 2 * REACH, comp, comp), F32)],
         compiler_params=params(),
         cost_estimate=cost(0, 0),
@@ -317,48 +307,53 @@
     )(*pieces)
 
 
-def apply_kernel(before, low, high, after, *refs):
-    pieces, (outer_low, outer_high, inner_low, inner_high, _, out) = refs[:-6], refs[-6:]
-    _, atoms, comp, energies = out.shape
-    edge = 2 * REACH * comp
-    half = inner_low.shape[0]
-    rows = pl.ds(pl.multiple_of(pl.program_id(0) * comp, 16), comp)
-    k = pl.program_id(1) * 2
-
-    def window(refs):
-        return jnp.concatenate([jnp.concatenate([r[k, rows, :], r[k + 1, rows, :]], axis=1) for r in refs], axis=0)
-
-    def put(value, first):
-        for a in range(value.shape[0] // comp):
+def apply_kernel(nz, ids, before, low, high, after, *refs):
+    pieces, (below, above, _, out, held, ready, sems) = refs[:-7], refs[-7:]
+    k, atoms, comps, energies = out.shape
+    comp = comps // 2
+    deep = below.shape[1]
+    half = atoms // 2
+    copies = []
+    for c in range(2):
+        rows = pl.ds(c * comp, comp)
+        for kk in range(0, k, 2):
             for b in range(2):
-                out[b, first + a] = value[a * comp:(a + 1) * comp, b * energies:(b + 1) * energies]
-
-    inside = window(pieces)
-    value = jnp.dot(inner_low[:, :inside.shape[0]], inside, preferred_element_type=F32)
-    value_edge = jnp.dot(outer_low[:edge, :edge], window([before.at[0], before.at[1], low.at[0], low.at[1]]), preferred_element_type=F32)
-    put(value[:edge] + value_edge, 0)
-    if half > edge:
-        put(value[edge:], 2 * REACH)
-    value = jnp.dot(inner_high[:, :inside.shape[0]], inside, preferred_element_type=F32)
-    value_edge = jnp.dot(outer_high[half - edge:, :edge], window([high.at[0], high.at[1], after.at[0], after.at[1]]), preferred_element_type=F32)
-    if half > edge:
-        put(value[:half - edge], atoms // 2)
-    put(value[half - edge:] + value_edge, atoms - 2 * REACH)
-
-
-def apply_couplings(before, low, high, after, pieces, outers, inners, wait, shape):
+                cols = pl.ds(b * energies, energies)
+                for j in range(REACH):
+                    for ref, at in ((before, j), (low, REACH + j), (high, atoms + j), (after, atoms + REACH + j)):
+                        held[at * comp:(at + 1) * comp, cols] = ref[j, kk + b, rows, :]
+                for i, piece in enumerate(pieces):
+                    at = (2 * REACH + i // nz * nz + lax.rem(ids[0] + nz - i % nz, nz)) * comp
+                    held[pl.ds(pl.multiple_of(at, 16), comp), cols] = piece[kk + b, rows, :]
+            for atom in range(atoms):
+                matrix, at = (below, atom) if atom < half else (above, atom - half)
+                value = jnp.dot(matrix[at * comp:(at + 1) * comp, :], held[atom * comp:atom * comp + deep, :], preferred_element_type=F32)
+                for b in range(2):
+                    ready[kk + b, atom, rows, :] = value[:, b * energies:(b + 1) * energies]
+                block = (pl.ds(kk, 2), atom, rows)
+                copies.append(pltpu.make_async_copy(ready.at[block], out.at[block], sems.at[len(copies)]))
+                copies[-1].start()
+    for copy in copies:
+        copy.wait()
+
+
+def apply_couplings(ids, nz, before, low, high, after, pieces, below, above, wait, shape):
     k, atoms, comps, energies = shape
     comp = comps // 2
-    matrices = [m.reshape(-1, m.shape[2]) for m in (*outers, *inners)]
-    return pl.pallas_call(
-        apply_kernel,
-        grid=(2, k // 2),
+    matrices = [m.reshape(-1, m.shape[2]) for m in (below, above)]
+    return pl.pallas_call(
+        functools.partial(apply_kernel, nz),
         out_shape=jax.ShapeDtypeStruct(shape, F32),
-        in_specs=[vmem()] * (4 + len(pieces) + len(matrices) + 1),
-        out_specs=pl.BlockSpec((2, atoms, comp, energies), lambda c, kk: (kk, 0, c, 0)),
+        in_specs=[smem()] + [vmem()] * (4 + len(pieces) + len(matrices)) + [anywhere()],
+        out_specs=anywhere(),
+        scratch_shapes=[
+            pltpu.VMEM(((atoms + 2 * REACH) * comp, 2 * energies), BF),
+            pltpu.VMEM(shape, F32),
+            pltpu.SemaphoreType.DMA((k * atoms,)),
+        ],
         compiler_params=params(),
         cost_estimate=cost(0, 0),
-    )(before, low, high, after, *pieces, *matrices, wait)
+    )(ids, before, low, high, after, *pieces, *matrices, wait)
 
 
 def shards(green, neighbours, offsets, emit_weight, absorb_weight, coupling):
@@ -389,13 +384,13 @@
         return [sent[0]] + [there[r] for r in range(1, nz)]
 
     got = [send(0)]
-    main, *edges, done = tables(offsets, emit_weight, absorb_weight, ids, sides, nz, k, energies)
     half = atoms // 2
-    outer_low, inner_low, done = coupling_matrices(ids, nz, neighbours, coupling, 0, half, done)
+    below, done = coupling_matrices(ids, neighbours, coupling, 0, half, got[0][0])
+    above, done = coupling_matrices(ids, neighbours, coupling, half, half, done)
+
+    main, *edges, done = tables(offsets, emit_weight, absorb_weight, ids, sides, nz, k, energies, done)
     for group in range(1, groups):
         got.append(send(group, done))
-    outer_high, inner_high, done = coupling_matrices(ids, nz, neighbours, coupling, half, half, done)
-
     waits = [done]
     back = []
     for group in range(groups):
@@ -409,7 +404,7 @@
     after = lax.ppermute(low, "atom", [(i + 1, i) for i in range(ny - 1)])
     before = lax.ppermute(high, "atom", [(i, i + 1) for i in range(ny - 1)])
     pieces = [piece for group in back[1:] for piece in group]
-    return apply_couplings(before, low, high, after, pieces, (outer_low, outer_high), (inner_low, inner_high), arrive([p for group in back[1:] for p in group[1:]]), green.shape)
+    return apply_couplings(ids, nz, before, low, high, after, pieces, below, above, arrive([p for group in back[1:] for p in group[1:]]), green.shape)
 
 
 def solution(mesh):

time: 113 us -> 111 us (0.982)
  waiting for transfers between devices: 41.5 us -> 54.8 us
  starting transfers between devices: 35.2 us -> 22.4 us
  Pallas kernels: 33.3 us -> 29.5 us
    ppermute x12, waiting for transfers between devices: 32.5 us -> 47.1 us  [around(): lax.ppermute(array, 'momentum', [(i, (i + r) % nz) for i in range(nz)])]
    ppermute x1, starting transfers between devices: 12.6 us -> 3.69 us  [shards(): before = lax.ppermute(high, 'atom', [(i, i + 1) for i in range(ny - 1)])]
    ppermute x12, starting transfers between devices: 17.6 us -> 13.6 us  [around(): lax.ppermute(array, 'momentum', [(i, (i + r) % nz) for i in range(nz)])]
    pallas_call x3, Pallas kernels: 19 us -> 15.2 us  [the longest x2 11.3 us: coupling_matrices(): pl.pallas_call(functools.partial(coupling_kernel, slots, skip), grid=(cou...]
    ppermute x1, waiting for transfers between devices: 1.98 us -> 0.01 us  [shards(): after = lax.ppermute(low, 'atom', [(i + 1, i) for i in range(ny - 1)])]
  transfers between devices with their start and end apart: 18 -> 18, of which waited for: 14 -> 12; matrix products, arithmetic and copies ran while one was open for 1% -> 0% of each run, Pallas kernels for 25% -> 23%
where the time goes in v3:
time: 111 us; the launch traced here: 110 us
  waiting for transfers between devices  54.8 us (49%)
  Pallas kernels  29.5 us (27%)
  starting transfers between devices  22.4 us (20%)
  local copies, waits for them, and re-layouts  2.26 us (2%)
    ppermute x12, waiting for transfers between devices, around(): lax.ppermute(array, 'momentum', [(i, (i + r) % nz) for i in range(nz)])  47.1 us
    ppermute x12, starting transfers between devices, around(): lax.ppermute(array, 'momentum', [(i, (i + r) % nz) for i in range(nz)])  13.6 us
    pallas_call x2, Pallas kernels, coupling_matrices(): pl.pallas_call(functools.partial(coupling_kernel, slots, skip), grid=(cou...  11.3 us
    ppermute x4, waiting for transfers between devices, shards(): lax.ppermute(h, 'energy', routes[i // 2])  7.67 us
    pallas_call x2, Pallas kernels, phonon_sum(): pl.pallas_call(functools.partial(sum_kernel, nz, sides), out_shape=(out,)...  6.49 us
    pallas_call x1, Pallas kernels, tables(): pl.pallas_call(functools.partial(table_kernel, nz, k, energies, sides), o...  4.37 us
    pallas_call x1, Pallas kernels, apply_couplings(): pl.pallas_call(functools.partial(apply_kernel, nz), out_shape=jax.ShapeDt...  3.94 us
    ppermute x1, starting transfers between devices, shards(): before = lax.ppermute(high, 'atom', [(i, i + 1) for i in range(ny - 1)])  3.69 us
  transfers between devices with their start and end apart: 18, of which 12 were waited for; matrix products, arithmetic and copies ran while one was open for 0% of the time, Pallas kernels for 23%

profile of v3, /device:TPU:9, one launch (start us, length us, event | category | flops | bytes accessed | tf_op | source)
XLA Modules:
  0.0 109.7 jit_solution(463957577944284348)
XLA Ops:
  0.0 0.0 copy-start
  0.0 0.0 copy-start.4
  0.0 0.0 copy-start.5
  0.0 0.0 copy-start.2
  0.0 0.0 copy-start.3
  0.0 0.1 pad_add_fusion.ids
  0.4 1.3 %dynamic-slice_bitcast_fusion = (bf16[4,288,128]{2,1,0:T(8,128)(2,1)S(1)}, bf16[4,288,128]{2,1,0:T(8,128)(2,1)S(1)}, bf16[4,288,128]{2,1,0:T(8,128)(2,1)S(1)}, bf16[4,288,128]{2,1,0:T(8,128)(2,1)S(1)}) fusion(bf16[4,8,288,128]{3,2,1,0:T(8,128)(2,1)} %green, s32[]{:T(128)S(6)} %select_n.49, s32[]{:T(128)S(6)} %select_n.46, s32[]{:T(128)S(6)} %select_n.43, ...), kind=kLoop, calls=%fused_computation | loop fusion | bytes 2359312 | tf_op jit(solution)/shard_map/jit(dynamic_index_in_dim)/squeeze | solution.py:377
  1.7 0.1 collective-permute-start.2
  1.8 2.5 %collective-permute-start.1 = (bf16[4,288,128]{2,1,0:T(8,128)(2,1)S(1)}, bf16[4,288,128]{2,1,0:T(8,128)(2,1)S(1)}, u32[]{:S(2)}, u32[]{:S(2)}) collective-permute-start(bf16[4,288,128]{2,1,0:T(8,128)(2,1)S(1)} %get-tuple-element.64), channel_id=1, source_target_pairs={{0,8},{4,12},{8,0},{12,4},{1,9},{5,13},{9,1},{13,5},{2,10},{6,14},... | collective-permute-start | bytes 884744 | tf_op jit(solution)/shard_map/ppermute | solution.py:367
  4.2 2.2 %collective-permute-start = (bf16[4,288,128]{2,1,0:T(8,128)(2,1)S(1)}, bf16[4,288,128]{2,1,0:T(8,128)(2,1)S(1)}, u32[]{:S(2)}, u32[]{:S(2)}) collective-permute-start(bf16[4,288,128]{2,1,0:T(8,128)(2,1)S(1)} %get-tuple-element.65), channel_id=1, source_target_pairs={{0,4},{4,8},{8,12},{12,0},{1,5},{5,9},{9,13},{13,1},{2,6},{6,10},{... | collective-permute-start | bytes 884744 | tf_op jit(solution)/shard_map/ppermute | solution.py:367
  6.4 0.0 copy-done.4
  6.5 0.0 copy-done.5
  6.5 0.0 copy-done.2
  6.5 0.0 copy-start.1
  6.5 0.9 copy-done.1
  7.4 5.6 %shard_map.64 = (bf16[4,144,720]{2,1,0:T(8,128)(2,1)S(1)}, f32[8,128]{1,0:T(8,128)S(1)}) custom-call(s32[3]{0:T(128)S(1)} %pad_add_fusion.ids, s32[8,8]{1,0:T(8,128)S(1)} %copy-done.2, bf16[8,96,12]{2,1,0:T(8,128)(2,1)S(1)} %bitcast.20, bf16[4,288,128]{2,1,0:T(8,128)(2,1)S(1)} %get-tuple-element.66.wait.refs_0_), custom_call_target="tpu_custom_call" | custom-call | tf_op jit(solution)/shard_map/pallas_call | solution.py:258
  13.0 5.7 %shard_map.65 = (bf16[4,144,720]{2,1,0:T(8,128)(2,1)S(1)}, f32[8,128]{1,0:T(8,128)S(1)}) custom-call(s32[3]{0:T(128)S(1)} %pad_add_fusion.ids, s32[8,8]{1,0:T(8,128)S(1)} %copy-done.2, bf16[8,96,12]{2,1,0:T(8,128)(2,1)S(1)} %bitcast.21, f32[8,128]{1,0:T(8,128)S(1)} %get-tuple-element.36.wait), custom_call_target="tpu_custom_call" | custom-call | tf_op jit(solution)/shard_map/pallas_call | solution.py:258
  18.7 0.0 copy-done.3
  18.7 4.4 %shard_map.66 = (bf16[3840,256]{1,0:T(8,128)(2,1)S(1)}, bf16[2,896,256]{2,1,0:T(8,128)(2,1)S(1)}, f32[8,128]{1,0:T(8,128)S(1)}) custom-call(s32[16]{0:T(128)S(1)} %copy-done.3, f32[16,16]{1,0:T(8,128)S(1)} %convert_element_type.6.emit_ref, f32[16,16]{1,0:T(8,128)S(1)} %convert_element_type.7.absorb_ref, s32[3]{0:T(128)S(1)} %pad_add_fusion.ids, ...), custom_call_target="tpu_custom_call" | custom-call | tf_op jit(solution)/shard_map/pallas_call | solution.py:156
  23.1 0.0 copy-done
  23.1 0.7 shard_map.69
  23.8 0.1 collective-permute-start.8
  23.9 1.3 %collective-permute-start.9 = (bf16[4,288,128]{2,1,0:T(8,128)(2,1)S(1)}, bf16[4,288,128]{2,1,0:T(8,128)(2,1)S(1)}, u32[]{:S(2)}, u32[]{:S(2)}) collective-permute-start(bf16[4,288,128]{2,1,0:T(8,128)(2,1)S(1)} %get-tuple-element.49), channel_id=1, source_target_pairs={{0,8},{4,12},{8,0},{12,4},{1,9},{5,13},{9,1},{13,5},{2,10},{6,14},... | collective-permute-start | bytes 884744 | tf_op jit(solution)/shard_map/ppermute | solution.py:367
  25.2 0.0 collective-permute-done.2.refs_3_
  25.2 1.0 collective-permute-start.10
  26.2 0.0 collective-permute-done.1.refs_2_
  26.2 3.0 %collective-permute-done.refs_1_ = bf16[4,288,128]{2,1,0:T(8,128)(2,1)S(1)} collective-permute-done((bf16[4,288,128]{2,1,0:T(8,128)(2,1)S(1)}, bf16[4,288,128]{2,1,0:T(8,128)(2,1)S(1)}, u32[]{:S(2)}, u32[]{:S(2)}) %collective-permute-start) | collective-permute-done | bytes 294944 | tf_op jit(solution)/shard_map/ppermute | solution.py:367
  29.2 1.0 shard_map.67
  30.2 1.3 %collective-permute-start.3 = (bf16[2,288,128]{2,1,0:T(8,128)(2,1)S(1)}, bf16[2,288,128]{2,1,0:T(8,128)(2,1)S(1)}, u32[]{:S(2)}, u32[]{:S(2)}) collective-permute-start(bf16[2,288,128]{2,1,0:T(8,128)(2,1)S(1)} %get-tuple-element.39), channel_id=1, source_target_pairs={{0,16},{16,0},{1,17},{17,1},{2,18},{18,2},{3,19},{19,3},{4,20},{20... | collective-permute-start | bytes 442376 | tf_op jit(solution)/shard_map/ppermute | solution.py:398
  31.5 0.3 collective-permute-start.4
  31.7 2.8 %collective-permute-done.3.refs_4_ = bf16[2,288,128]{2,1,0:T(8,128)(2,1)S(1)} collective-permute-done((bf16[2,288,128]{2,1,0:T(8,128)(2,1)S(1)}, bf16[2,288,128]{2,1,0:T(8,128)(2,1)S(1)}, u32[]{:S(2)}, u32[]{:S(2)}) %collective-permute-start.3) | collective-permute-done | bytes 147488 | tf_op jit(solution)/shard_map/ppermute | solution.py:398
  34.6 1.6 %collective-permute-done.4.refs_5_ = bf16[2,288,128]{2,1,0:T(8,128)(2,1)S(1)} collective-permute-done((bf16[2,288,128]{2,1,0:T(8,128)(2,1)S(1)}, bf16[2,288,128]{2,1,0:T(8,128)(2,1)S(1)}, u32[]{:S(2)}, u32[]{:S(2)}) %collective-permute-start.4) | collective-permute-done | bytes 147488 | tf_op jit(solution)/shard_map/ppermute | solution.py:398
  36.2 3.2 %shard_map.68 = (bf16[4,288,128]{2,1,0:T(8,128)(2,1)S(1)}, bf16[4,288,128]{2,1,0:T(8,128)(2,1)S(1)}, bf16[4,288,128]{2,1,0:T(8,128)(2,1)S(1)}, bf16[4,288,128]{2,1,0:T(8,128)(2,1)S(1)}, f32[8,128]{1,0:T(8,128)S(1)}) custom-call(bf16[4,288,128]{2,1,0:T(8,128)(2,1)S(1)} %get-tuple-element.66.wait.refs_0_, ...), custom_call_target="tpu_custom_call" | custom-call | tf_op jit(solution)/shard_map/pallas_call | solution.py:205
  39.4 0.1 collective-permute-start.6
  39.5 8.7 %collective-permute-done.8.refs_1_ = bf16[4,288,128]{2,1,0:T(8,128)(2,1)S(1)} collective-permute-done((bf16[4,288,128]{2,1,0:T(8,128)(2,1)S(1)}, bf16[4,288,128]{2,1,0:T(8,128)(2,1)S(1)}, u32[]{:S(2)}, u32[]{:S(2)}) %collective-permute-start.8) | collective-permute-done | bytes 294944 | tf_op jit(solution)/shard_map/ppermute | solution.py:367
  48.2 12.5 %collective-permute-done.9.refs_2_ = bf16[4,288,128]{2,1,0:T(8,128)(2,1)S(1)} collective-permute-done((bf16[4,288,128]{2,1,0:T(8,128)(2,1)S(1)}, bf16[4,288,128]{2,1,0:T(8,128)(2,1)S(1)}, u32[]{:S(2)}, u32[]{:S(2)}) %collective-permute-start.9) | collective-permute-done | bytes 294944 | tf_op jit(solution)/shard_map/ppermute | solution.py:367
  60.7 0.0 collective-permute-done.10.refs_3_
  60.7 1.0 shard_map.70
  61.7 1.3 %collective-permute-start.11 = (bf16[2,288,128]{2,1,0:T(8,128)(2,1)S(1)}, bf16[2,288,128]{2,1,0:T(8,128)(2,1)S(1)}, u32[]{:S(2)}, u32[]{:S(2)}) collective-permute-start(bf16[2,288,128]{2,1,0:T(8,128)(2,1)S(1)} %get-tuple-element.52), channel_id=1, source_target_pairs={{0,16},{16,0},{1,17},{17,1},{2,18},{18,2},{3,19},{19,3},{4,20},{20... | collective-permute-start | bytes 442376 | tf_op jit(solution)/shard_map/ppermute | solution.py:398
  63.0 0.3 collective-permute-start.12
  63.2 0.0 collective-permute-start.5
  63.2 1.5 %collective-permute-start.7 = (bf16[4,288,128]{2,1,0:T(8,128)(2,1)S(1)}, bf16[4,288,128]{2,1,0:T(8,128)(2,1)S(1)}, u32[]{:S(2)}, u32[]{:S(2)}) collective-permute-start(bf16[4,288,128]{2,1,0:T(8,128)(2,1)S(1)} %get-tuple-element.46), channel_id=1, source_target_pairs={{0,12},{4,0},{8,4},{12,8},{1,13},{5,1},{9,5},{13,9},{2,14},{6,2},{... | collective-permute-start | bytes 884744 | tf_op jit(solution)/shard_map/ppermute | solution.py:367
  64.7 1.1 collective-permute-done.11.refs_4_
  65.7 2.2 %collective-permute-done.12.refs_5_ = bf16[2,288,128]{2,1,0:T(8,128)(2,1)S(1)} collective-permute-done((bf16[2,288,128]{2,1,0:T(8,128)(2,1)S(1)}, bf16[2,288,128]{2,1,0:T(8,128)(2,1)S(1)}, u32[]{:S(2)}, u32[]{:S(2)}) %collective-permute-start.12) | collective-permute-done | bytes 147488 | tf_op jit(solution)/shard_map/ppermute | solution.py:398
  67.9 0.0 collective-permute-done.6.refs_8_.refs_2_
  67.9 3.2 %shard_map.71 = (bf16[4,288,128]{2,1,0:T(8,128)(2,1)S(1)}, bf16[4,288,128]{2,1,0:T(8,128)(2,1)S(1)}, bf16[4,288,128]{2,1,0:T(8,128)(2,1)S(1)}, bf16[4,288,128]{2,1,0:T(8,128)(2,1)S(1)}, f32[8,128]{1,0:T(8,128)S(1)}) custom-call(bf16[4,288,128]{2,1,0:T(8,128)(2,1)S(1)} %get-tuple-element.47.refs_0_, bf16[4,288,128]{2,1,0:T(8,128)(2,1)S(1)} %collective-permute-done.8.refs_1_, ...), custom_call_target="tpu_custom_call" | custom-call | tf_op jit(solution)/shard_map/pallas_call | solution.py:205
  71.2 0.1 collective-permute-start.15
  71.3 3.5 %collective-permute-start.16 = (bf16[4,288,128]{2,1,0:T(8,128)(2,1)S(1)}, bf16[4,288,128]{2,1,0:T(8,128)(2,1)S(1)}, u32[]{:S(2)}, u32[]{:S(2)}) collective-permute-start(bf16[4,288,128]{2,1,0:T(8,128)(2,1)S(1)} %get-tuple-element.59), channel_id=1, source_target_pairs={{0,8},{4,12},{8,0},{12,4},{1,9},{5,13},{9,1},{13,5},{2,10},{6,14},... | collective-permute-start | bytes 884744 | tf_op jit(solution)/shard_map/ppermute | solution.py:367
  74.7 1.4 %collective-permute-start.17 = (bf16[4,288,128]{2,1,0:T(8,128)(2,1)S(1)}, bf16[4,288,128]{2,1,0:T(8,128)(2,1)S(1)}, u32[]{:S(2)}, u32[]{:S(2)}) collective-permute-start(bf16[4,288,128]{2,1,0:T(8,128)(2,1)S(1)} %get-tuple-element.60), channel_id=1, source_target_pairs={{0,12},{4,0},{8,4},{12,8},{1,13},{5,1},{9,5},{13,9},{2,14},{6,2},{... | collective-permute-start | bytes 884744 | tf_op jit(solution)/shard_map/ppermute | solution.py:367
  76.1 2.0 %collective-permute-done.5.refs_1_ = bf16[4,288,128]{2,1,0:T(8,128)(2,1)S(1)} collective-permute-done((bf16[4,288,128]{2,1,0:T(8,128)(2,1)S(1)}, bf16[4,288,128]{2,1,0:T(8,128)(2,1)S(1)}, u32[]{:S(2)}, u32[]{:S(2)}) %collective-permute-start.5) | collective-permute-done | bytes 294944 | tf_op jit(solution)/shard_map/ppermute | solution.py:367
  78.1 5.0 %collective-permute-done.7.refs_3_ = bf16[4,288,128]{2,1,0:T(8,128)(2,1)S(1)} collective-permute-done((bf16[4,288,128]{2,1,0:T(8,128)(2,1)S(1)}, bf16[4,288,128]{2,1,0:T(8,128)(2,1)S(1)}, u32[]{:S(2)}, u32[]{:S(2)}) %collective-permute-start.7) | collective-permute-done | bytes 294944 | tf_op jit(solution)/shard_map/ppermute | solution.py:367
  83.1 0.7 shard_map.72
  83.8 3.7 %collective-permute-start.13 = (bf16[2,4,288,128]{3,2,1,0:T(8,128)(2,1)S(1)}, bf16[2,4,288,128]{3,2,1,0:T(8,128)(2,1)S(1)}, u32[]{:S(2)}, u32[]{:S(2)}) collective-permute-start(bf16[2,4,288,128]{3,2,1,0:T(8,128)(2,1)S(1)} %get-tuple-element.55.high), channel_id=1, source_target_pairs={{0,1},{1,2},{2,3},{4,5},{5,6},{6,7},{8,9},{9,10},{10,11},{12,13},{... | collective-permute-start | bytes 1769480 | tf_op jit(solution)/shard_map/ppermute | solution.py:405
  87.5 2.1 %collective-permute-start.14 = (bf16[2,4,288,128]{3,2,1,0:T(8,128)(2,1)S(1)}, bf16[2,4,288,128]{3,2,1,0:T(8,128)(2,1)S(1)}, u32[]{:S(2)}, u32[]{:S(2)}) collective-permute-start(bf16[2,4,288,128]{3,2,1,0:T(8,128)(2,1)S(1)} %get-tuple-element.56.low), channel_id=1, source_target_pairs={{1,0},{2,1},{3,2},{5,4},{6,5},{7,6},{9,8},{10,9},{11,10},{13,12},{... | collective-permute-start | bytes 1769480 | tf_op jit(solution)/shard_map/ppermute | solution.py:404
  89.6 9.1 %collective-permute-done.15.refs_0_.refs_1_ = bf16[4,288,128]{2,1,0:T(8,128)(2,1)S(1)} collective-permute-done((bf16[4,288,128]{2,1,0:T(8,128)(2,1)S(1)}, bf16[4,288,128]{2,1,0:T(8,128)(2,1)S(1)}, u32[]{:S(2)}, u32[]{:S(2)}) %collective-permute-start.15) | collective-permute-done | bytes 294944 | tf_op jit(solution)/shard_map/ppermute | solution.py:367
  98.7 6.3 %collective-permute-done.16.refs_1_.refs_2_ = bf16[4,288,128]{2,1,0:T(8,128)(2,1)S(1)} collective-permute-done((bf16[4,288,128]{2,1,0:T(8,128)(2,1)S(1)}, bf16[4,288,128]{2,1,0:T(8,128)(2,1)S(1)}, u32[]{:S(2)}, u32[]{:S(2)}) %collective-permute-start.16) | collective-permute-done | bytes 294944 | tf_op jit(solution)/shard_map/ppermute | solution.py:367
  105.0 0.6 collective-permute-done.17.refs_2_.refs_3_
  105.6 0.0 collective-permute-done.13.before
  105.6 0.0 collective-permute-done.14.after
  105.6 3.9 %shard_map.74 = f32[4,8,288,128]{3,2,1,0:T(8,128)} custom-call(s32[3]{0:T(128)S(1)} %pad_add_fusion.ids, bf16[2,4,288,128]{3,2,1,0:T(8,128)(2,1)S(1)} %collective-permute-done.13.before, bf16[2,4,288,128]{3,2,1,0:T(8,128)(2,1)S(1)} %get-tuple-element.56.low, bf16[2,4,288,128]{3,2,1,0:T(8,128)(2,1)S(1)} %get-tuple-element.55.high, ...), custom_call_target="tpu_custom_call" | custom-call | tf_op jit(solution)/shard_map/pallas_call | solution.py:344
  (3 shorter events, 0.0 us)
Async XLA Ops:
  0.0 23.1 %copy-start = (bf16[4,8,288,128]{3,2,1,0:T(8,128)(2,1)S(1)}, bf16[4,8,288,128]{3,2,1,0:T(8,128)(2,1)}, u32[]{:S(2)}) copy-start(bf16[4,8,288,128]{3,2,1,0:T(8,128)(2,1)} %green) | copy-start | bytes 7077892
  0.0 6.4 %copy-start.4 = (bf16[16,16]{1,0:T(8,128)(2,1)S(1)}, bf16[16,16]{1,0:T(8,128)(2,1)}, u32[]{:S(2)}) copy-start(bf16[16,16]{1,0:T(8,128)(2,1)} %param.9) | copy-start | bytes 1540
  0.0 6.4 %copy-start.5 = (bf16[16,16]{1,0:T(8,128)(2,1)S(1)}, bf16[16,16]{1,0:T(8,128)(2,1)}, u32[]{:S(2)}) copy-start(bf16[16,16]{1,0:T(8,128)(2,1)} %param.10) | copy-start | bytes 1540
  0.0 6.5 %copy-start.2 = (s32[8,8]{1,0:T(8,128)S(1)}, s32[8,8]{1,0:T(8,128)}, u32[]{:S(2)}) copy-start(s32[8,8]{1,0:T(8,128)} %near_ref.3) | copy-start | bytes 772
  0.0 18.7 %copy-start.3 = (s32[16]{0:T(128)S(1)}, s32[16]{0:T(128)}, u32[]{:S(2)}) copy-start(s32[16]{0:T(128)} %off_ref.1) | copy-start | bytes 196
  1.7 23.5 %collective-permute-start.2 = (bf16[4,288,128]{2,1,0:T(8,128)(2,1)S(1)}, bf16[4,288,128]{2,1,0:T(8,128)(2,1)S(1)}, u32[]{:S(2)}, u32[]{:S(2)}) collective-permute-start(bf16[4,288,128]{2,1,0:T(8,128)(2,1)S(1)} %get-tuple-element.63), channel_id=1, source_target_pairs={{0,12},{4,0},{8,4},{12,8},{1,13},{5,1},{9,5},{13,9},{2,14},{6,2},{... | collective-permute-start | bytes 884744 | tf_op jit(solution)/shard_map/ppermute | solution.py:367
  1.8 24.5 %collective-permute-start.1 = (bf16[4,288,128]{2,1,0:T(8,128)(2,1)S(1)}, bf16[4,288,128]{2,1,0:T(8,128)(2,1)S(1)}, u32[]{:S(2)}, u32[]{:S(2)}) collective-permute-start(bf16[4,288,128]{2,1,0:T(8,128)(2,1)S(1)} %get-tuple-element.64), channel_id=1, source_target_pairs={{0,8},{4,12},{8,0},{12,4},{1,9},{5,13},{9,1},{13,5},{2,10},{6,14},... | collective-permute-start | bytes 884744 | tf_op jit(solution)/shard_map/ppermute | solution.py:367
  4.2 24.9 %collective-permute-start = (bf16[4,288,128]{2,1,0:T(8,128)(2,1)S(1)}, bf16[4,288,128]{2,1,0:T(8,128)(2,1)S(1)}, u32[]{:S(2)}, u32[]{:S(2)}) collective-permute-start(bf16[4,288,128]{2,1,0:T(8,128)(2,1)S(1)} %get-tuple-element.65), channel_id=1, source_target_pairs={{0,4},{4,8},{8,12},{12,0},{1,5},{5,9},{9,13},{13,1},{2,6},{6,10},{... | collective-permute-start | bytes 884744 | tf_op jit(solution)/shard_map/ppermute | solution.py:367
  6.5 0.9 copy-start.1
  23.8 24.3 %collective-permute-start.8 = (bf16[4,288,128]{2,1,0:T(8,128)(2,1)S(1)}, bf16[4,288,128]{2,1,0:T(8,128)(2,1)S(1)}, u32[]{:S(2)}, u32[]{:S(2)}) collective-permute-start(bf16[4,288,128]{2,1,0:T(8,128)(2,1)S(1)} %get-tuple-element.48), channel_id=1, source_target_pairs={{0,4},{4,8},{8,12},{12,0},{1,5},{5,9},{9,13},{13,1},{2,6},{6,10},{... | collective-permute-start | bytes 884744 | tf_op jit(solution)/shard_map/ppermute | solution.py:367
  23.9 36.8 %collective-permute-start.9 = (bf16[4,288,128]{2,1,0:T(8,128)(2,1)S(1)}, bf16[4,288,128]{2,1,0:T(8,128)(2,1)S(1)}, u32[]{:S(2)}, u32[]{:S(2)}) collective-permute-start(bf16[4,288,128]{2,1,0:T(8,128)(2,1)S(1)} %get-tuple-element.49), channel_id=1, source_target_pairs={{0,8},{4,12},{8,0},{12,4},{1,9},{5,13},{9,1},{13,5},{2,10},{6,14},... | collective-permute-start | bytes 884744 | tf_op jit(solution)/shard_map/ppermute | solution.py:367
  25.2 35.4 %collective-permute-start.10 = (bf16[4,288,128]{2,1,0:T(8,128)(2,1)S(1)}, bf16[4,288,128]{2,1,0:T(8,128)(2,1)S(1)}, u32[]{:S(2)}, u32[]{:S(2)}) collective-permute-start(bf16[4,288,128]{2,1,0:T(8,128)(2,1)S(1)} %get-tuple-element.50), channel_id=1, source_target_pairs={{0,12},{4,0},{8,4},{12,8},{1,13},{5,1},{9,5},{13,9},{2,14},{6,2},{... | collective-permute-start | bytes 884744 | tf_op jit(solution)/shard_map/ppermute | solution.py:367
  30.2 4.4 %collective-permute-start.3 = (bf16[2,288,128]{2,1,0:T(8,128)(2,1)S(1)}, bf16[2,288,128]{2,1,0:T(8,128)(2,1)S(1)}, u32[]{:S(2)}, u32[]{:S(2)}) collective-permute-start(bf16[2,288,128]{2,1,0:T(8,128)(2,1)S(1)} %get-tuple-element.39), channel_id=1, source_target_pairs={{0,16},{16,0},{1,17},{17,1},{2,18},{18,2},{3,19},{19,3},{4,20},{20... | collective-permute-start | bytes 442376 | tf_op jit(solution)/shard_map/ppermute | solution.py:398
  31.5 4.7 %collective-permute-start.4 = (bf16[2,288,128]{2,1,0:T(8,128)(2,1)S(1)}, bf16[2,288,128]{2,1,0:T(8,128)(2,1)S(1)}, u32[]{:S(2)}, u32[]{:S(2)}) collective-permute-start(bf16[2,288,128]{2,1,0:T(8,128)(2,1)S(1)} %get-tuple-element.40), channel_id=1, source_target_pairs={{0,16},{16,0},{1,17},{17,1},{2,18},{18,2},{3,19},{19,3},{4,20},{20... | collective-permute-start | bytes 442376 | tf_op jit(solution)/shard_map/ppermute | solution.py:398
  39.4 28.5 %collective-permute-start.6 = (bf16[4,288,128]{2,1,0:T(8,128)(2,1)S(1)}, bf16[4,288,128]{2,1,0:T(8,128)(2,1)S(1)}, u32[]{:S(2)}, u32[]{:S(2)}) collective-permute-start(bf16[4,288,128]{2,1,0:T(8,128)(2,1)S(1)} %get-tuple-element.45), channel_id=1, source_target_pairs={{0,8},{4,12},{8,0},{12,4},{1,9},{5,13},{9,1},{13,5},{2,10},{6,14},... | collective-permute-start | bytes 884744 | tf_op jit(solution)/shard_map/ppermute | solution.py:367
  61.7 4.1 %collective-permute-start.11 = (bf16[2,288,128]{2,1,0:T(8,128)(2,1)S(1)}, bf16[2,288,128]{2,1,0:T(8,128)(2,1)S(1)}, u32[]{:S(2)}, u32[]{:S(2)}) collective-permute-start(bf16[2,288,128]{2,1,0:T(8,128)(2,1)S(1)} %get-tuple-element.52), channel_id=1, source_target_pairs={{0,16},{16,0},{1,17},{17,1},{2,18},{18,2},{3,19},{19,3},{4,20},{20... | collective-permute-start | bytes 442376 | tf_op jit(solution)/shard_map/ppermute | solution.py:398
  63.0 5.0 %collective-permute-start.12 = (bf16[2,288,128]{2,1,0:T(8,128)(2,1)S(1)}, bf16[2,288,128]{2,1,0:T(8,128)(2,1)S(1)}, u32[]{:S(2)}, u32[]{:S(2)}) collective-permute-start(bf16[2,288,128]{2,1,0:T(8,128)(2,1)S(1)} %get-tuple-element.53), channel_id=1, source_target_pairs={{0,16},{16,0},{1,17},{17,1},{2,18},{18,2},{3,19},{19,3},{4,20},{20... | collective-permute-start | bytes 442376 | tf_op jit(solution)/shard_map/ppermute | solution.py:398
  63.2 14.9 %collective-permute-start.5 = (bf16[4,288,128]{2,1,0:T(8,128)(2,1)S(1)}, bf16[4,288,128]{2,1,0:T(8,128)(2,1)S(1)}, u32[]{:S(2)}, u32[]{:S(2)}) collective-permute-start(bf16[4,288,128]{2,1,0:T(8,128)(2,1)S(1)} %get-tuple-element.44), channel_id=1, source_target_pairs={{0,4},{4,8},{8,12},{12,0},{1,5},{5,9},{9,13},{13,1},{2,6},{6,10},{... | collective-permute-start | bytes 884744 | tf_op jit(solution)/shard_map/ppermute | solution.py:367
  63.2 19.9 %collective-permute-start.7 = (bf16[4,288,128]{2,1,0:T(8,128)(2,1)S(1)}, bf16[4,288,128]{2,1,0:T(8,128)(2,1)S(1)}, u32[]{:S(2)}, u32[]{:S(2)}) collective-permute-start(bf16[4,288,128]{2,1,0:T(8,128)(2,1)S(1)} %get-tuple-element.46), channel_id=1, source_target_pairs={{0,12},{4,0},{8,4},{12,8},{1,13},{5,1},{9,5},{13,9},{2,14},{6,2},{... | collective-permute-start | bytes 884744 | tf_op jit(solution)/shard_map/ppermute | solution.py:367
  71.2 27.5 %collective-permute-start.15 = (bf16[4,288,128]{2,1,0:T(8,128)(2,1)S(1)}, bf16[4,288,128]{2,1,0:T(8,128)(2,1)S(1)}, u32[]{:S(2)}, u32[]{:S(2)}) collective-permute-start(bf16[4,288,128]{2,1,0:T(8,128)(2,1)S(1)} %get-tuple-element.58), channel_id=1, source_target_pairs={{0,4},{4,8},{8,12},{12,0},{1,5},{5,9},{9,13},{13,1},{2,6},{6,10},{... | collective-permute-start | bytes 884744 | tf_op jit(solution)/shard_map/ppermute | solution.py:367
  71.3 33.8 %collective-permute-start.16 = (bf16[4,288,128]{2,1,0:T(8,128)(2,1)S(1)}, bf16[4,288,128]{2,1,0:T(8,128)(2,1)S(1)}, u32[]{:S(2)}, u32[]{:S(2)}) collective-permute-start(bf16[4,288,128]{2,1,0:T(8,128)(2,1)S(1)} %get-tuple-element.59), channel_id=1, source_target_pairs={{0,8},{4,12},{8,0},{12,4},{1,9},{5,13},{9,1},{13,5},{2,10},{6,14},... | collective-permute-start | bytes 884744 | tf_op jit(solution)/shard_map/ppermute | solution.py:367
  74.7 30.9 %collective-permute-start.17 = (bf16[4,288,128]{2,1,0:T(8,128)(2,1)S(1)}, bf16[4,288,128]{2,1,0:T(8,128)(2,1)S(1)}, u32[]{:S(2)}, u32[]{:S(2)}) collective-permute-start(bf16[4,288,128]{2,1,0:T(8,128)(2,1)S(1)} %get-tuple-element.60), channel_id=1, source_target_pairs={{0,12},{4,0},{8,4},{12,8},{1,13},{5,1},{9,5},{13,9},{2,14},{6,2},{... | collective-permute-start | bytes 884744 | tf_op jit(solution)/shard_map/ppermute | solution.py:367
  83.8 21.8 %collective-permute-start.13 = (bf16[2,4,288,128]{3,2,1,0:T(8,128)(2,1)S(1)}, bf16[2,4,288,128]{3,2,1,0:T(8,128)(2,1)S(1)}, u32[]{:S(2)}, u32[]{:S(2)}) collective-permute-start(bf16[2,4,288,128]{3,2,1,0:T(8,128)(2,1)S(1)} %get-tuple-element.55.high), channel_id=1, source_target_pairs={{0,1},{1,2},{2,3},{4,5},{5,6},{6,7},{8,9},{9,10},{10,11},{12,13},{... | collective-permute-start | bytes 1769480 | tf_op jit(solution)/shard_map/ppermute | solution.py:405
  87.5 18.1 %collective-permute-start.14 = (bf16[2,4,288,128]{3,2,1,0:T(8,128)(2,1)S(1)}, bf16[2,4,288,128]{3,2,1,0:T(8,128)(2,1)S(1)}, u32[]{:S(2)}, u32[]{:S(2)}) collective-permute-start(bf16[2,4,288,128]{3,2,1,0:T(8,128)(2,1)S(1)} %get-tuple-element.56.low), channel_id=1, source_target_pairs={{1,0},{2,1},{3,2},{5,4},{6,5},{7,6},{9,8},{10,9},{11,10},{13,12},{... | collective-permute-start | bytes 1769480 | tf_op jit(solution)/shard_map/ppermute | solution.py:404

commit v4 on v3

--- a/solution.py
+++ b/solution.py
@@ -164,12 +164,12 @@
     )(offsets, emit.astype(F32), absorb.astype(F32), ids, wait)
 
 
-def sum_kernel(nz, sides, *refs):
+def sum_kernel(nz, sides, parts, *refs):
     pieces, refs = refs[:nz], refs[nz:]
     halos, refs = refs[:2 * sides], refs[2 * sides:]
     main, refs = refs[0], refs[1:]
     edges, refs = refs[:sides], refs[sides:]
-    outs, done, wide = refs[-nz - 2:-2], refs[-2], refs[-1]
+    outs, done, wide = refs[-nz * parts - 2:-2], refs[-2], refs[-1]
     done[...] = jnp.zeros_like(done)
     k, rows, energies = pieces[0].shape
     total = nz * k
@@ -193,20 +193,22 @@
             start = (nz - 1 - pair // per) * strip
             value += jnp.dot(wide[:, at:at + nz * strip], edges[side][pair % per, start:start + nz * strip, :], preferred_element_type=F32)
         value = value.astype(BF)
-        for b in range(2):
-            outs[pair // per][2 * (pair % per) + b] = value[:, b * energies:(b + 1) * energies]
-
-
-def phonon_sum(pieces, halos, main, edges, waits):
+        size = rows // parts
+        for i in range(parts):
+            for b in range(2):
+                outs[pair // per * parts + i][2 * (pair % per) + b] = value[i * size:(i + 1) * size, b * energies:(b + 1) * energies]
+
+
+def phonon_sum(pieces, halos, main, edges, parts, waits):
     nz, sides = len(pieces), len(halos) // 2
     k, rows, energies = pieces[0].shape
-    out = jax.ShapeDtypeStruct((k, rows, energies), BF)
+    out = jax.ShapeDtypeStruct((k, rows // parts, energies), BF)
     depth = nz * k * energies + sides * nz * k * SMAX
     return pl.pallas_call(
-        functools.partial(sum_kernel, nz, sides),
-        out_shape=(out,) * nz + (token(),),
+        functools.partial(sum_kernel, nz, sides, parts),
+        out_shape=(out,) * (nz * parts) + (token(),),
         in_specs=[vmem()] * (nz + 2 * sides + 1 + sides) + [anywhere()] * len(waits),
-        out_specs=(vmem(),) * (nz + 1),
+        out_specs=(vmem(),) * (nz * parts + 1),
         scratch_shapes=[pltpu.VMEM((rows, depth), BF)],
         compiler_params=params(),
         cost_estimate=cost(2 * rows * depth * nz * k * energies, main.size * 2),
@@ -303,54 +305,54 @@
         in_specs=[anywhere()] * len(pieces),
         out_specs=vmem(),
         compiler_params=params(),
-        cost_estimate=pl.CostEstimate(flops=40 * 10**9, bytes_accessed=0, transcendentals=0),
+        cost_estimate=pl.CostEstimate(flops=55 * 10**8, bytes_accessed=0, transcendentals=0),
     )(*pieces)
 
 
-def apply_kernel(nz, ids, before, low, high, after, *refs):
+def apply_kernel(nz, c, ids, before, low, high, after, *refs):
     pieces, (below, above, _, out, held, ready, sems) = refs[:-7], refs[-7:]
     k, atoms, comps, energies = out.shape
     comp = comps // 2
     deep = below.shape[1]
     half = atoms // 2
     copies = []
-    for c in range(2):
-        rows = pl.ds(c * comp, comp)
-        for kk in range(0, k, 2):
+    rows = pl.ds(c * comp, comp)
+    for kk in range(0, k, 2):
+        for b in range(2):
+            cols = pl.ds(b * energies, energies)
+            for j in range(REACH):
+                for ref, at in ((before, j), (low, REACH + j), (high, atoms + j), (after, atoms + REACH + j)):
+                    held[at * comp:(at + 1) * comp, cols] = ref[j, kk + b, rows, :]
+            for i, piece in enumerate(pieces):
+                at = (2 * REACH + i // nz * nz + lax.rem(ids[0] + nz - i % nz, nz)) * comp
+                held[pl.ds(pl.multiple_of(at, 16), comp), cols] = piece[kk + b]
+        for atom in range(atoms):
+            matrix, at = (below, atom) if atom < half else (above, atom - half)
+            value = jnp.dot(matrix[at * comp:(at + 1) * comp, :], held[atom * comp:atom * comp + deep, :], preferred_element_type=F32)
             for b in range(2):
-                cols = pl.ds(b * energies, energies)
-                for j in range(REACH):
-                    for ref, at in ((before, j), (low, REACH + j), (high, atoms + j), (after, atoms + REACH + j)):
-                        held[at * comp:(at + 1) * comp, cols] = ref[j, kk + b, rows, :]
-                for i, piece in enumerate(pieces):
-                    at = (2 * REACH + i // nz * nz + lax.rem(ids[0] + nz - i % nz, nz)) * comp
-                    held[pl.ds(pl.multiple_of(at, 16), comp), cols] = piece[kk + b, rows, :]
-            for atom in range(atoms):
-                matrix, at = (below, atom) if atom < half else (above, atom - half)
-                value = jnp.dot(matrix[at * comp:(at + 1) * comp, :], held[atom * comp:atom * comp + deep, :], preferred_element_type=F32)
-                for b in range(2):
-                    ready[kk + b, atom, rows, :] = value[:, b * energies:(b + 1) * energies]
-                block = (pl.ds(kk, 2), atom, rows)
-                copies.append(pltpu.make_async_copy(ready.at[block], out.at[block], sems.at[len(copies)]))
-                copies[-1].start()
+                ready[kk + b, atom] = value[:, b * energies:(b + 1) * energies]
+            block = (pl.ds(kk, 2), atom)
+            copies.append(pltpu.make_async_copy(ready.at[block], out.at[(*block, rows)], sems.at[len(copies)]))
+            copies[-1].start()
     for copy in copies:
         copy.wait()
 
 
-def apply_couplings(ids, nz, before, low, high, after, pieces, below, above, wait, shape):
+def apply_couplings(ids, nz, c, before, low, high, after, pieces, below, above, wait, shape):
     k, atoms, comps, energies = shape
     comp = comps // 2
     matrices = [m.reshape(-1, m.shape[2]) for m in (below, above)]
     return pl.pallas_call(
-        functools.partial(apply_kernel, nz),
+        functools.partial(apply_kernel, nz, c),
         out_shape=jax.ShapeDtypeStruct(shape, F32),
         in_specs=[smem()] + [vmem()] * (4 + len(pieces) + len(matrices)) + [anywhere()],
         out_specs=anywhere(),
         scratch_shapes=[
             pltpu.VMEM(((atoms + 2 * REACH) * comp, 2 * energies), BF),
-            pltpu.VMEM(shape, F32),
-            pltpu.SemaphoreType.DMA((k * atoms,)),
+            pltpu.VMEM((k, atoms, comp, energies), F32),
+            pltpu.SemaphoreType.DMA((k * atoms // 2,)),
         ],
+        input_output_aliases={5 + len(pieces) + len(matrices): 0} if wait.shape == shape else {},
         compiler_params=params(),
         cost_estimate=cost(0, 0),
     )(ids, before, low, high, after, *pieces, *matrices, wait)
@@ -377,7 +379,7 @@
             sent = [lax.dynamic_index_in_dim(green, atom_of(group * nz + lax.rem(ids[0] + r, nz), atoms), 1, keepdims=False) for r in range(nz)]
         else:
             sent = pack(ids, green, nz, group, waits)
-        return spread(sent, ([[1, 2, 3], [1, 2, 3], [1, 2, 3], [1, 2, 3]])[group])
+        return spread(sent, range(1, nz))
 
     def spread(sent, order):
         there = {r: around(sent[r], r) for r in order}
@@ -396,15 +398,19 @@
     for group in range(groups):
         halos = halo_pack(ids, got[group], sides, waits)
         halos = [lax.ppermute(h, "energy", routes[i // 2]) for i, h in enumerate(halos)]
-        *sums, sum_done = phonon_sum(got[group], halos, main, edges, [back[-1][r] for r in [2]] if back else [])
+        parts = 1 if group == 0 else 2
+        *sums, sum_done = phonon_sum(got[group], halos, main, edges, parts, [back[-1][0][r] for r in [2]] if back else [])
         waits = [sum_done]
-        back.append(spread(sums, ([[1, 2, 3], [1, 2, 3], [1, 2, 3], [1, 2, 3]])[2 + group]))
-
-    low, high = edge_pack(ids, back[0], waits)
+        back.append([spread(sums[i::parts], range(1, nz)) for i in range(parts)])
+
+    low, high = edge_pack(ids, back[0][0], waits)
     after = lax.ppermute(low, "atom", [(i + 1, i) for i in range(ny - 1)])
     before = lax.ppermute(high, "atom", [(i, i + 1) for i in range(ny - 1)])
-    pieces = [piece for group in back[1:] for piece in group]
-    return apply_couplings(ids, nz, before, low, high, after, pieces, below, above, arrive([p for group in back[1:] for p in group[1:]]), green.shape)
+    out = arrive([p for parts in back[1:] for p in parts[0][1:]])
+    for c in range(2):
+        pieces = [piece for parts in back[1:] for piece in parts[c]]
+        out = apply_couplings(ids, nz, c, before, low, high, after, pieces, below, above, out, green.shape)
+    return out
 
 
 def solution(mesh):

time: 111 us -> 110 us (level)
  waiting for transfers between devices: 54.8 us -> 34.5 us
  starting transfers between devices: 22.4 us -> 40.6 us
  Pallas kernels: 29.5 us -> 30.9 us
    ppermute x12 -> x15, waiting for transfers between devices: 47.1 us -> 23.4 us  [around(): lax.ppermute(array, 'momentum', [(i, (i + r) % nz) for i in range(nz)])]
    ppermute x12 -> x15, starting transfers between devices: 13.6 us -> 29.6 us  [around(): lax.ppermute(array, 'momentum', [(i, (i + r) % nz) for i in range(nz)])]
    ppermute x1, waiting for transfers between devices: 0.01 us -> 2.57 us  [shards(): after = lax.ppermute(low, 'atom', [(i + 1, i) for i in range(ny - 1)])]
    ppermute x1, starting transfers between devices: 3.69 us -> 6.03 us  [shards(): before = lax.ppermute(high, 'atom', [(i, i + 1) for i in range(ny - 1)])]
    pallas_call x3 -> x4, Pallas kernels: 10.4 us -> 11.9 us  [the longest x2 6.5 us: phonon_sum(): pl.pallas_call(functools.partial(sum_kernel, nz, sides, parts), out_shape...]
  transfers between devices with their start and end apart: 18 -> 21, of which waited for: 12 -> 13; matrix products, arithmetic and copies ran while one was open for 0% -> 0% of each run, Pallas kernels for 23% -> 26%
where the time goes in v4:
time: 110 us; the launch traced here: 109 us
  starting transfers between devices  40.6 us (37%)
  waiting for transfers between devices  34.5 us (31%)
  Pallas kernels  30.9 us (28%)
  local copies, waits for them, and re-layouts  2.26 us (2%)
    ppermute x15, starting transfers between devices, around(): lax.ppermute(array, 'momentum', [(i, (i + r) % nz) for i in range(nz)])  29.6 us
    ppermute x15, waiting for transfers between devices, around(): lax.ppermute(array, 'momentum', [(i, (i + r) % nz) for i in range(nz)])  23.4 us
    pallas_call x2, Pallas kernels, coupling_matrices(): pl.pallas_call(functools.partial(coupling_kernel, slots, skip), grid=(cou...  11.3 us
    ppermute x4, waiting for transfers between devices, shards(): lax.ppermute(h, 'energy', routes[i // 2])  8.51 us
    pallas_call x2, Pallas kernels, phonon_sum(): pl.pallas_call(functools.partial(sum_kernel, nz, sides, parts), out_shape...  6.5 us
    ppermute x1, starting transfers between devices, shards(): before = lax.ppermute(high, 'atom', [(i, i + 1) for i in range(ny - 1)])  6.03 us
    pallas_call x2, Pallas kernels, apply_couplings(): pl.pallas_call(functools.partial(apply_kernel, nz, c), out_shape=jax.Shap...  5.36 us
    pallas_call x1, Pallas kernels, tables(): pl.pallas_call(functools.partial(table_kernel, nz, k, energies, sides), o...  4.37 us
  transfers between devices with their start and end apart: 21, of which 13 were waited for; matrix products, arithmetic and copies ran while one was open for 0% of the time, Pallas kernels for 26%

profile of v4, /device:TPU:9, one launch (start us, length us, event | category | flops | bytes accessed | tf_op | source)
XLA Modules:
  0.0 109.1 jit_solution(8954904845698602036)
XLA Ops:
  0.0 0.0 copy-start.2
  0.0 0.0 copy-start.3
  0.0 0.1 pad_add_fusion.ids
  0.4 1.3 %dynamic-slice_bitcast_fusion = (bf16[4,288,128]{2,1,0:T(8,128)(2,1)S(1)}, bf16[4,288,128]{2,1,0:T(8,128)(2,1)S(1)}, bf16[4,288,128]{2,1,0:T(8,128)(2,1)S(1)}, bf16[4,288,128]{2,1,0:T(8,128)(2,1)S(1)}) fusion(bf16[4,8,288,128]{3,2,1,0:T(8,128)(2,1)} %green, s32[]{:T(128)S(6)} %select_n.49, s32[]{:T(128)S(6)} %select_n.46, s32[]{:T(128)S(6)} %select_n.43, ...), kind=kLoop, calls=%fused_computation | loop fusion | bytes 2359312 | tf_op jit(solution)/shard_map/jit(dynamic_index_in_dim)/squeeze | solution.py:379
  1.7 0.1 collective-permute-start.2
  1.8 2.5 %collective-permute-start.1 = (bf16[4,288,128]{2,1,0:T(8,128)(2,1)S(1)}, bf16[4,288,128]{2,1,0:T(8,128)(2,1)S(1)}, u32[]{:S(2)}, u32[]{:S(2)}) collective-permute-start(bf16[4,288,128]{2,1,0:T(8,128)(2,1)S(1)} %get-tuple-element.72), channel_id=1, source_target_pairs={{0,8},{4,12},{8,0},{12,4},{1,9},{5,13},{9,1},{13,5},{2,10},{6,14},... | collective-permute-start | bytes 884744 | tf_op jit(solution)/shard_map/ppermute | solution.py:369
  4.2 2.2 %collective-permute-start = (bf16[4,288,128]{2,1,0:T(8,128)(2,1)S(1)}, bf16[4,288,128]{2,1,0:T(8,128)(2,1)S(1)}, u32[]{:S(2)}, u32[]{:S(2)}) collective-permute-start(bf16[4,288,128]{2,1,0:T(8,128)(2,1)S(1)} %get-tuple-element.73), channel_id=1, source_target_pairs={{0,4},{4,8},{8,12},{12,0},{1,5},{5,9},{9,13},{13,1},{2,6},{6,10},{... | collective-permute-start | bytes 884744 | tf_op jit(solution)/shard_map/ppermute | solution.py:369
  6.4 0.0 copy-done.4
  6.5 0.0 copy-done.5
  6.5 0.0 copy-done.2
  6.5 0.0 copy-start.1
  6.5 0.9 copy-done.1
  7.4 5.6 %shard_map.64 = (bf16[4,144,720]{2,1,0:T(8,128)(2,1)S(1)}, f32[8,128]{1,0:T(8,128)S(1)}) custom-call(s32[3]{0:T(128)S(1)} %pad_add_fusion.ids, s32[8,8]{1,0:T(8,128)S(1)} %copy-done.2, bf16[8,96,12]{2,1,0:T(8,128)(2,1)S(1)} %bitcast.22, bf16[4,288,128]{2,1,0:T(8,128)(2,1)S(1)} %get-tuple-element.74.wait.refs_0_), custom_call_target="tpu_custom_call" | custom-call | tf_op jit(solution)/shard_map/pallas_call | solution.py:260
  13.0 5.7 %shard_map.65 = (bf16[4,144,720]{2,1,0:T(8,128)(2,1)S(1)}, f32[8,128]{1,0:T(8,128)S(1)}) custom-call(s32[3]{0:T(128)S(1)} %pad_add_fusion.ids, s32[8,8]{1,0:T(8,128)S(1)} %copy-done.2, bf16[8,96,12]{2,1,0:T(8,128)(2,1)S(1)} %bitcast.23, f32[8,128]{1,0:T(8,128)S(1)} %get-tuple-element.40.wait), custom_call_target="tpu_custom_call" | custom-call | tf_op jit(solution)/shard_map/pallas_call | solution.py:260
  18.7 0.0 copy-done.3
  18.7 4.4 %shard_map.66 = (bf16[3840,256]{1,0:T(8,128)(2,1)S(1)}, bf16[2,896,256]{2,1,0:T(8,128)(2,1)S(1)}, f32[8,128]{1,0:T(8,128)S(1)}) custom-call(s32[16]{0:T(128)S(1)} %copy-done.3, f32[16,16]{1,0:T(8,128)S(1)} %convert_element_type.6.emit_ref, f32[16,16]{1,0:T(8,128)S(1)} %convert_element_type.7.absorb_ref, s32[3]{0:T(128)S(1)} %pad_add_fusion.ids, ...), custom_call_target="tpu_custom_call" | custom-call | tf_op jit(solution)/shard_map/pallas_call | solution.py:156
  23.1 0.0 copy-done
  23.1 0.7 shard_map.69
  23.8 0.1 collective-permute-start.8
  23.9 1.3 %collective-permute-start.9 = (bf16[4,288,128]{2,1,0:T(8,128)(2,1)S(1)}, bf16[4,288,128]{2,1,0:T(8,128)(2,1)S(1)}, u32[]{:S(2)}, u32[]{:S(2)}) collective-permute-start(bf16[4,288,128]{2,1,0:T(8,128)(2,1)S(1)} %get-tuple-element.53), channel_id=1, source_target_pairs={{0,8},{4,12},{8,0},{12,4},{1,9},{5,13},{9,1},{13,5},{2,10},{6,14},... | collective-permute-start | bytes 884744 | tf_op jit(solution)/shard_map/ppermute | solution.py:369
  25.2 0.0 collective-permute-done.2.refs_3_
  25.2 1.0 collective-permute-start.10
  26.2 0.0 collective-permute-done.1.refs_2_
  26.2 3.0 %collective-permute-done.refs_1_ = bf16[4,288,128]{2,1,0:T(8,128)(2,1)S(1)} collective-permute-done((bf16[4,288,128]{2,1,0:T(8,128)(2,1)S(1)}, bf16[4,288,128]{2,1,0:T(8,128)(2,1)S(1)}, u32[]{:S(2)}, u32[]{:S(2)}) %collective-permute-start) | collective-permute-done | bytes 294944 | tf_op jit(solution)/shard_map/ppermute | solution.py:369
  29.2 1.0 shard_map.67
  30.2 1.3 %collective-permute-start.3 = (bf16[2,288,128]{2,1,0:T(8,128)(2,1)S(1)}, bf16[2,288,128]{2,1,0:T(8,128)(2,1)S(1)}, u32[]{:S(2)}, u32[]{:S(2)}) collective-permute-start(bf16[2,288,128]{2,1,0:T(8,128)(2,1)S(1)} %get-tuple-element.43), channel_id=1, source_target_pairs={{0,16},{16,0},{1,17},{17,1},{2,18},{18,2},{3,19},{19,3},{4,20},{20... | collective-permute-start | bytes 442376 | tf_op jit(solution)/shard_map/ppermute | solution.py:400
  31.5 0.3 collective-permute-start.4
  31.8 2.8 %collective-permute-done.3.refs_4_ = bf16[2,288,128]{2,1,0:T(8,128)(2,1)S(1)} collective-permute-done((bf16[2,288,128]{2,1,0:T(8,128)(2,1)S(1)}, bf16[2,288,128]{2,1,0:T(8,128)(2,1)S(1)}, u32[]{:S(2)}, u32[]{:S(2)}) %collective-permute-start.3) | collective-permute-done | bytes 147488 | tf_op jit(solution)/shard_map/ppermute | solution.py:400
  34.6 1.6 %collective-permute-done.4.refs_5_ = bf16[2,288,128]{2,1,0:T(8,128)(2,1)S(1)} collective-permute-done((bf16[2,288,128]{2,1,0:T(8,128)(2,1)S(1)}, bf16[2,288,128]{2,1,0:T(8,128)(2,1)S(1)}, u32[]{:S(2)}, u32[]{:S(2)}) %collective-permute-start.4) | collective-permute-done | bytes 147488 | tf_op jit(solution)/shard_map/ppermute | solution.py:400
  36.2 3.2 %shard_map.68 = (bf16[4,288,128]{2,1,0:T(8,128)(2,1)S(1)}, bf16[4,288,128]{2,1,0:T(8,128)(2,1)S(1)}, bf16[4,288,128]{2,1,0:T(8,128)(2,1)S(1)}, bf16[4,288,128]{2,1,0:T(8,128)(2,1)S(1)}, f32[8,128]{1,0:T(8,128)S(1)}) custom-call(bf16[4,288,128]{2,1,0:T(8,128)(2,1)S(1)} %get-tuple-element.74.wait.refs_0_, ...), custom_call_target="tpu_custom_call" | custom-call | tf_op jit(solution)/shard_map/pallas_call | solution.py:207
  39.4 0.1 collective-permute-start.6
  39.5 14.4 %collective-permute-start.5 = (bf16[4,288,128]{2,1,0:T(8,128)(2,1)S(1)}, bf16[4,288,128]{2,1,0:T(8,128)(2,1)S(1)}, u32[]{:S(2)}, u32[]{:S(2)}) collective-permute-start(bf16[4,288,128]{2,1,0:T(8,128)(2,1)S(1)} %get-tuple-element.48), channel_id=1, source_target_pairs={{0,4},{4,8},{8,12},{12,0},{1,5},{5,9},{9,13},{13,1},{2,6},{6,10},{... | collective-permute-start | bytes 884744 | tf_op jit(solution)/shard_map/ppermute | solution.py:369
  53.9 0.0 collective-permute-done.8.refs_1_
  53.9 0.0 collective-permute-start.7
  53.9 4.0 %collective-permute-done.9.refs_2_ = bf16[4,288,128]{2,1,0:T(8,128)(2,1)S(1)} collective-permute-done((bf16[4,288,128]{2,1,0:T(8,128)(2,1)S(1)}, bf16[4,288,128]{2,1,0:T(8,128)(2,1)S(1)}, u32[]{:S(2)}, u32[]{:S(2)}) %collective-permute-start.9) | collective-permute-done | bytes 294944 | tf_op jit(solution)/shard_map/ppermute | solution.py:369
  58.0 8.6 %collective-permute-done.10.refs_3_ = bf16[4,288,128]{2,1,0:T(8,128)(2,1)S(1)} collective-permute-done((bf16[4,288,128]{2,1,0:T(8,128)(2,1)S(1)}, bf16[4,288,128]{2,1,0:T(8,128)(2,1)S(1)}, u32[]{:S(2)}, u32[]{:S(2)}) %collective-permute-start.10) | collective-permute-done | bytes 294944 | tf_op jit(solution)/shard_map/ppermute | solution.py:369
  66.6 1.0 shard_map.70
  67.6 1.3 %collective-permute-start.11 = (bf16[2,288,128]{2,1,0:T(8,128)(2,1)S(1)}, bf16[2,288,128]{2,1,0:T(8,128)(2,1)S(1)}, u32[]{:S(2)}, u32[]{:S(2)}) collective-permute-start(bf16[2,288,128]{2,1,0:T(8,128)(2,1)S(1)} %get-tuple-element.56), channel_id=1, source_target_pairs={{0,16},{16,0},{1,17},{17,1},{2,18},{18,2},{3,19},{19,3},{4,20},{20... | collective-permute-start | bytes 442376 | tf_op jit(solution)/shard_map/ppermute | solution.py:400
  68.9 0.3 collective-permute-start.12
  69.1 2.5 %collective-permute-done.11.refs_4_ = bf16[2,288,128]{2,1,0:T(8,128)(2,1)S(1)} collective-permute-done((bf16[2,288,128]{2,1,0:T(8,128)(2,1)S(1)}, bf16[2,288,128]{2,1,0:T(8,128)(2,1)S(1)}, u32[]{:S(2)}, u32[]{:S(2)}) %collective-permute-start.11) | collective-permute-done | bytes 147488 | tf_op jit(solution)/shard_map/ppermute | solution.py:400
  71.6 1.6 %collective-permute-done.12.refs_5_ = bf16[2,288,128]{2,1,0:T(8,128)(2,1)S(1)} collective-permute-done((bf16[2,288,128]{2,1,0:T(8,128)(2,1)S(1)}, bf16[2,288,128]{2,1,0:T(8,128)(2,1)S(1)}, u32[]{:S(2)}, u32[]{:S(2)}) %collective-permute-start.12) | collective-permute-done | bytes 147488 | tf_op jit(solution)/shard_map/ppermute | solution.py:400
  73.2 0.2 collective-permute-done.6.refs_8_.refs_2_
  73.4 3.2 %shard_map.71 = (bf16[4,144,128]{2,1,0:T(8,128)(2,1)S(1)}, bf16[4,144,128]{2,1,0:T(8,128)(2,1)S(1)}, bf16[4,144,128]{2,1,0:T(8,128)(2,1)S(1)}, bf16[4,144,128]{2...) custom-call(bf16[4,288,128]{2,1,0:T(8,128)(2,1)S(1)} %get-tuple-elem, ...), custom_call_target="tpu_custom_call" | custom-call | tf_op jit(solution)/shard_map/pallas_call | solution.py:207
  76.7 0.1 collective-permute-start.18
  76.8 3.2 %collective-permute-start.19 = (bf16[4,144,128]{2,1,0:T(8,128)(2,1)S(1)}, bf16[4,144,128]{2,1,0:T(8,128)(2,1)S(1)}, u32[]{:S(2)}, u32[]{:S(2)}) collective-permute-start(bf16[4,144,128]{2,1,0:T(8,128)(2,1)S(1)} %get-tuple-element.69), channel_id=1, source_target_pairs={{0,8},{4,12},{8,0},{12,4},{1,9},{5,13},{9,1},{13,5},{2,10},{6,14},... | collective-permute-start | bytes 442376 | tf_op jit(solution)/shard_map/ppermute | solution.py:369
  79.9 1.4 %collective-permute-start.20 = (bf16[4,144,128]{2,1,0:T(8,128)(2,1)S(1)}, bf16[4,144,128]{2,1,0:T(8,128)(2,1)S(1)}, u32[]{:S(2)}, u32[]{:S(2)}) collective-permute-start(bf16[4,144,128]{2,1,0:T(8,128)(2,1)S(1)} %get-tuple-element.70), channel_id=1, source_target_pairs={{0,12},{4,0},{8,4},{12,8},{1,13},{5,1},{9,5},{13,9},{2,14},{6,2},{... | collective-permute-start | bytes 442376 | tf_op jit(solution)/shard_map/ppermute | solution.py:369
  81.3 0.0 collective-permute-done.5.refs_1_
  81.3 0.0 collective-permute-done.7.refs_3_
  81.3 0.7 shard_map.72
  82.0 6.0 %collective-permute-start.13 = (bf16[2,4,288,128]{3,2,1,0:T(8,128)(2,1)S(1)}, bf16[2,4,288,128]{3,2,1,0:T(8,128)(2,1)S(1)}, u32[]{:S(2)}, u32[]{:S(2)}) collective-permute-start(bf16[2,4,288,128]{3,2,1,0:T(8,128)(2,1)S(1)} %get-tuple-element.59.high), channel_id=1, source_target_pairs={{0,1},{1,2},{2,3},{4,5},{5,6},{6,7},{8,9},{9,10},{10,11},{12,13},{... | collective-permute-start | bytes 1769480 | tf_op jit(solution)/shard_map/ppermute | solution.py:408
  88.1 1.9 %collective-permute-start.14 = (bf16[2,4,288,128]{3,2,1,0:T(8,128)(2,1)S(1)}, bf16[2,4,288,128]{3,2,1,0:T(8,128)(2,1)S(1)}, u32[]{:S(2)}, u32[]{:S(2)}) collective-permute-start(bf16[2,4,288,128]{3,2,1,0:T(8,128)(2,1)S(1)} %get-tuple-element.60.low), channel_id=1, source_target_pairs={{1,0},{2,1},{3,2},{5,4},{6,5},{7,6},{9,8},{10,9},{11,10},{13,12},{... | collective-permute-start | bytes 1769480 | tf_op jit(solution)/shard_map/ppermute | solution.py:407
  90.0 0.0 collective-permute-done.18.refs_0_.refs_1_
  90.0 0.3 collective-permute-start.15
  90.3 2.2 %collective-permute-done.19.refs_1_.refs_2_ = bf16[4,144,128]{2,1,0:T(8,128)(2,1)S(1)} collective-permute-done((bf16[4,144,128]{2,1,0:T(8,128)(2,1)S(1)}, bf16[4,144,128]{2,1,0:T(8,128)(2,1)S(1)}, u32[]{:S(2)}, u32[]{:S(2)}) %collective-permute-start.19) | collective-permute-done | bytes 147488 | tf_op jit(solution)/shard_map/ppermute | solution.py:369
  92.4 3.1 %collective-permute-start.16 = (bf16[4,144,128]{2,1,0:T(8,128)(2,1)S(1)}, bf16[4,144,128]{2,1,0:T(8,128)(2,1)S(1)}, u32[]{:S(2)}, u32[]{:S(2)}) collective-permute-start(bf16[4,144,128]{2,1,0:T(8,128)(2,1)S(1)} %get-tuple-element.63), channel_id=1, source_target_pairs={{0,8},{4,12},{8,0},{12,4},{1,9},{5,13},{9,1},{13,5},{2,10},{6,14},... | collective-permute-start | bytes 442376 | tf_op jit(solution)/shard_map/ppermute | solution.py:369
  95.5 1.1 %collective-permute-done.20.refs_2_.refs_3_ = bf16[4,144,128]{2,1,0:T(8,128)(2,1)S(1)} collective-permute-done((bf16[4,144,128]{2,1,0:T(8,128)(2,1)S(1)}, bf16[4,144,128]{2,1,0:T(8,128)(2,1)S(1)}, u32[]{:S(2)}, u32[]{:S(2)}) %collective-permute-start.20) | collective-permute-done | bytes 147488 | tf_op jit(solution)/shard_map/ppermute | solution.py:369
  96.7 0.0 collective-permute-start.17
  96.7 0.0 collective-permute-done.13.before
  96.7 2.6 %collective-permute-done.14.after = bf16[2,4,288,128]{3,2,1,0:T(8,128)(2,1)S(1)} collective-permute-done((bf16[2,4,288,128]{3,2,1,0:T(8,128)(2,1)S(1)}, bf16[2,4,288,128]{3,2,1,0:T(8,128)(2,1)S(1)}, u32[]{:S(2)}, u32[]{:S(2)}) %collective-permute-start.14) | collective-permute-done | bytes 589856 | tf_op jit(solution)/shard_map/ppermute | solution.py:407
  99.3 2.7 %shard_map.74.refs_6_ = f32[4,8,288,128]{3,2,1,0:T(8,128)} custom-call(s32[3]{0:T(128)S(1)} %pad_add_fusion.ids, bf16[2,4,288,128]{3,2,1,0:T(8,128)(2,1)S(1)} %collective-permute-done.13.before, bf16[2,4,288,128]{3,2,1,0:T(8,128)(2,1)S(1)} %get-tuple-element.60.low, bf16[2,4,288,128]{3,2,1,0:T(8,128)(2,1)S(1)} %get-tuple-element.59.high, ...), custom_call_target="tpu_custom_call" | custom-call | tf_op jit(solution)/shard_map/pallas_call | solution.py:345
  102.0 0.0 collective-permute-done.15.refs_1_
  102.0 3.1 %collective-permute-done.16.refs_2_ = bf16[4,144,128]{2,1,0:T(8,128)(2,1)S(1)} collective-permute-done((bf16[4,144,128]{2,1,0:T(8,128)(2,1)S(1)}, bf16[4,144,128]{2,1,0:T(8,128)(2,1)S(1)}, u32[]{:S(2)}, u32[]{:S(2)}) %collective-permute-start.16) | collective-permute-done | bytes 147488 | tf_op jit(solution)/shard_map/ppermute | solution.py:369
  105.1 1.2 %collective-permute-done.17.refs_3_ = bf16[4,144,128]{2,1,0:T(8,128)(2,1)S(1)} collective-permute-done((bf16[4,144,128]{2,1,0:T(8,128)(2,1)S(1)}, bf16[4,144,128]{2,1,0:T(8,128)(2,1)S(1)}, u32[]{:S(2)}, u32[]{:S(2)}) %collective-permute-start.17) | collective-permute-done | bytes 147488 | tf_op jit(solution)/shard_map/ppermute | solution.py:369
  106.3 2.7 %shard_map.75 = f32[4,8,288,128]{3,2,1,0:T(8,128)} custom-call(s32[3]{0:T(128)S(1)} %pad_add_fusion.ids, bf16[2,4,288,128]{3,2,1,0:T(8,128)(2,1)S(1)} %collective-permute-done.13.before, bf16[2,4,288,128]{3,2,1,0:T(8,128)(2,1)S(1)} %get-tuple-element.60.low, bf16[2,4,288,128]{3,2,1,0:T(8,128)(2,1)S(1)} %get-tuple-element.59.high, ...), custom_call_target="tpu_custom_call", output_to_operand_aliasing={{}: (11, {})} | custom-call | tf_op jit(solution)/shard_map/pallas_call | solution.py:345
  (6 shorter events, 0.0 us)
Async XLA Ops:
  0.0 23.1 %copy-start = (bf16[4,8,288,128]{3,2,1,0:T(8,128)(2,1)S(1)}, bf16[4,8,288,128]{3,2,1,0:T(8,128)(2,1)}, u32[]{:S(2)}) copy-start(bf16[4,8,288,128]{3,2,1,0:T(8,128)(2,1)} %green) | copy-start | bytes 7077892
  0.0 6.4 %copy-start.4 = (bf16[16,16]{1,0:T(8,128)(2,1)S(1)}, bf16[16,16]{1,0:T(8,128)(2,1)}, u32[]{:S(2)}) copy-start(bf16[16,16]{1,0:T(8,128)(2,1)} %param.9) | copy-start | bytes 1540
  0.0 6.4 %copy-start.5 = (bf16[16,16]{1,0:T(8,128)(2,1)S(1)}, bf16[16,16]{1,0:T(8,128)(2,1)}, u32[]{:S(2)}) copy-start(bf16[16,16]{1,0:T(8,128)(2,1)} %param.10) | copy-start | bytes 1540
  0.0 6.5 %copy-start.2 = (s32[8,8]{1,0:T(8,128)S(1)}, s32[8,8]{1,0:T(8,128)}, u32[]{:S(2)}) copy-start(s32[8,8]{1,0:T(8,128)} %near_ref.3) | copy-start | bytes 772
  0.0 18.7 %copy-start.3 = (s32[16]{0:T(128)S(1)}, s32[16]{0:T(128)}, u32[]{:S(2)}) copy-start(s32[16]{0:T(128)} %off_ref.1) | copy-start | bytes 196
  1.7 23.5 %collective-permute-start.2 = (bf16[4,288,128]{2,1,0:T(8,128)(2,1)S(1)}, bf16[4,288,128]{2,1,0:T(8,128)(2,1)S(1)}, u32[]{:S(2)}, u32[]{:S(2)}) collective-permute-start(bf16[4,288,128]{2,1,0:T(8,128)(2,1)S(1)} %get-tuple-element.71), channel_id=1, source_target_pairs={{0,12},{4,0},{8,4},{12,8},{1,13},{5,1},{9,5},{13,9},{2,14},{6,2},{... | collective-permute-start | bytes 884744 | tf_op jit(solution)/shard_map/ppermute | solution.py:369
  1.8 24.5 %collective-permute-start.1 = (bf16[4,288,128]{2,1,0:T(8,128)(2,1)S(1)}, bf16[4,288,128]{2,1,0:T(8,128)(2,1)S(1)}, u32[]{:S(2)}, u32[]{:S(2)}) collective-permute-start(bf16[4,288,128]{2,1,0:T(8,128)(2,1)S(1)} %get-tuple-element.72), channel_id=1, source_target_pairs={{0,8},{4,12},{8,0},{12,4},{1,9},{5,13},{9,1},{13,5},{2,10},{6,14},... | collective-permute-start | bytes 884744 | tf_op jit(solution)/shard_map/ppermute | solution.py:369
  4.2 24.9 %collective-permute-start = (bf16[4,288,128]{2,1,0:T(8,128)(2,1)S(1)}, bf16[4,288,128]{2,1,0:T(8,128)(2,1)S(1)}, u32[]{:S(2)}, u32[]{:S(2)}) collective-permute-start(bf16[4,288,128]{2,1,0:T(8,128)(2,1)S(1)} %get-tuple-element.73), channel_id=1, source_target_pairs={{0,4},{4,8},{8,12},{12,0},{1,5},{5,9},{9,13},{13,1},{2,6},{6,10},{... | collective-permute-start | bytes 884744 | tf_op jit(solution)/shard_map/ppermute | solution.py:369
  6.5 0.9 copy-start.1
  23.8 30.1 %collective-permute-start.8 = (bf16[4,288,128]{2,1,0:T(8,128)(2,1)S(1)}, bf16[4,288,128]{2,1,0:T(8,128)(2,1)S(1)}, u32[]{:S(2)}, u32[]{:S(2)}) collective-permute-start(bf16[4,288,128]{2,1,0:T(8,128)(2,1)S(1)} %get-tuple-element.52), channel_id=1, source_target_pairs={{0,4},{4,8},{8,12},{12,0},{1,5},{5,9},{9,13},{13,1},{2,6},{6,10},{... | collective-permute-start | bytes 884744 | tf_op jit(solution)/shard_map/ppermute | solution.py:369
  23.9 34.1 %collective-permute-start.9 = (bf16[4,288,128]{2,1,0:T(8,128)(2,1)S(1)}, bf16[4,288,128]{2,1,0:T(8,128)(2,1)S(1)}, u32[]{:S(2)}, u32[]{:S(2)}) collective-permute-start(bf16[4,288,128]{2,1,0:T(8,128)(2,1)S(1)} %get-tuple-element.53), channel_id=1, source_target_pairs={{0,8},{4,12},{8,0},{12,4},{1,9},{5,13},{9,1},{13,5},{2,10},{6,14},... | collective-permute-start | bytes 884744 | tf_op jit(solution)/shard_map/ppermute | solution.py:369
  25.2 41.3 %collective-permute-start.10 = (bf16[4,288,128]{2,1,0:T(8,128)(2,1)S(1)}, bf16[4,288,128]{2,1,0:T(8,128)(2,1)S(1)}, u32[]{:S(2)}, u32[]{:S(2)}) collective-permute-start(bf16[4,288,128]{2,1,0:T(8,128)(2,1)S(1)} %get-tuple-element.54), channel_id=1, source_target_pairs={{0,12},{4,0},{8,4},{12,8},{1,13},{5,1},{9,5},{13,9},{2,14},{6,2},{... | collective-permute-start | bytes 884744 | tf_op jit(solution)/shard_map/ppermute | solution.py:369
  30.2 4.4 %collective-permute-start.3 = (bf16[2,288,128]{2,1,0:T(8,128)(2,1)S(1)}, bf16[2,288,128]{2,1,0:T(8,128)(2,1)S(1)}, u32[]{:S(2)}, u32[]{:S(2)}) collective-permute-start(bf16[2,288,128]{2,1,0:T(8,128)(2,1)S(1)} %get-tuple-element.43), channel_id=1, source_target_pairs={{0,16},{16,0},{1,17},{17,1},{2,18},{18,2},{3,19},{19,3},{4,20},{20... | collective-permute-start | bytes 442376 | tf_op jit(solution)/shard_map/ppermute | solution.py:400
  31.5 4.7 %collective-permute-start.4 = (bf16[2,288,128]{2,1,0:T(8,128)(2,1)S(1)}, bf16[2,288,128]{2,1,0:T(8,128)(2,1)S(1)}, u32[]{:S(2)}, u32[]{:S(2)}) collective-permute-start(bf16[2,288,128]{2,1,0:T(8,128)(2,1)S(1)} %get-tuple-element.44), channel_id=1, source_target_pairs={{0,16},{16,0},{1,17},{17,1},{2,18},{18,2},{3,19},{19,3},{4,20},{20... | collective-permute-start | bytes 442376 | tf_op jit(solution)/shard_map/ppermute | solution.py:400
  39.4 34.0 %collective-permute-start.6 = (bf16[4,288,128]{2,1,0:T(8,128)(2,1)S(1)}, bf16[4,288,128]{2,1,0:T(8,128)(2,1)S(1)}, u32[]{:S(2)}, u32[]{:S(2)}) collective-permute-start(bf16[4,288,128]{2,1,0:T(8,128)(2,1)S(1)} %get-tuple-element.49), channel_id=1, source_target_pairs={{0,8},{4,12},{8,0},{12,4},{1,9},{5,13},{9,1},{13,5},{2,10},{6,14},... | collective-permute-start | bytes 884744 | tf_op jit(solution)/shard_map/ppermute | solution.py:369
  39.5 41.8 %collective-permute-start.5 = (bf16[4,288,128]{2,1,0:T(8,128)(2,1)S(1)}, bf16[4,288,128]{2,1,0:T(8,128)(2,1)S(1)}, u32[]{:S(2)}, u32[]{:S(2)}) collective-permute-start(bf16[4,288,128]{2,1,0:T(8,128)(2,1)S(1)} %get-tuple-element.48), channel_id=1, source_target_pairs={{0,4},{4,8},{8,12},{12,0},{1,5},{5,9},{9,13},{13,1},{2,6},{6,10},{... | collective-permute-start | bytes 884744 | tf_op jit(solution)/shard_map/ppermute | solution.py:369
  53.9 27.4 %collective-permute-start.7 = (bf16[4,288,128]{2,1,0:T(8,128)(2,1)S(1)}, bf16[4,288,128]{2,1,0:T(8,128)(2,1)S(1)}, u32[]{:S(2)}, u32[]{:S(2)}) collective-permute-start(bf16[4,288,128]{2,1,0:T(8,128)(2,1)S(1)} %get-tuple-element.50), channel_id=1, source_target_pairs={{0,12},{4,0},{8,4},{12,8},{1,13},{5,1},{9,5},{13,9},{2,14},{6,2},{... | collective-permute-start | bytes 884744 | tf_op jit(solution)/shard_map/ppermute | solution.py:369
  67.6 4.1 %collective-permute-start.11 = (bf16[2,288,128]{2,1,0:T(8,128)(2,1)S(1)}, bf16[2,288,128]{2,1,0:T(8,128)(2,1)S(1)}, u32[]{:S(2)}, u32[]{:S(2)}) collective-permute-start(bf16[2,288,128]{2,1,0:T(8,128)(2,1)S(1)} %get-tuple-element.56), channel_id=1, source_target_pairs={{0,16},{16,0},{1,17},{17,1},{2,18},{18,2},{3,19},{19,3},{4,20},{20... | collective-permute-start | bytes 442376 | tf_op jit(solution)/shard_map/ppermute | solution.py:400
  68.9 4.4 %collective-permute-start.12 = (bf16[2,288,128]{2,1,0:T(8,128)(2,1)S(1)}, bf16[2,288,128]{2,1,0:T(8,128)(2,1)S(1)}, u32[]{:S(2)}, u32[]{:S(2)}) collective-permute-start(bf16[2,288,128]{2,1,0:T(8,128)(2,1)S(1)} %get-tuple-element.57), channel_id=1, source_target_pairs={{0,16},{16,0},{1,17},{17,1},{2,18},{18,2},{3,19},{19,3},{4,20},{20... | collective-permute-start | bytes 442376 | tf_op jit(solution)/shard_map/ppermute | solution.py:400
  76.7 13.3 %collective-permute-start.18 = (bf16[4,144,128]{2,1,0:T(8,128)(2,1)S(1)}, bf16[4,144,128]{2,1,0:T(8,128)(2,1)S(1)}, u32[]{:S(2)}, u32[]{:S(2)}) collective-permute-start(bf16[4,144,128]{2,1,0:T(8,128)(2,1)S(1)} %get-tuple-element.68), channel_id=1, source_target_pairs={{0,4},{4,8},{8,12},{12,0},{1,5},{5,9},{9,13},{13,1},{2,6},{6,10},{... | collective-permute-start | bytes 442376 | tf_op jit(solution)/shard_map/ppermute | solution.py:369
  76.8 15.7 %collective-permute-start.19 = (bf16[4,144,128]{2,1,0:T(8,128)(2,1)S(1)}, bf16[4,144,128]{2,1,0:T(8,128)(2,1)S(1)}, u32[]{:S(2)}, u32[]{:S(2)}) collective-permute-start(bf16[4,144,128]{2,1,0:T(8,128)(2,1)S(1)} %get-tuple-element.69), channel_id=1, source_target_pairs={{0,8},{4,12},{8,0},{12,4},{1,9},{5,13},{9,1},{13,5},{2,10},{6,14},... | collective-permute-start | bytes 442376 | tf_op jit(solution)/shard_map/ppermute | solution.py:369
  79.9 16.8 %collective-permute-start.20 = (bf16[4,144,128]{2,1,0:T(8,128)(2,1)S(1)}, bf16[4,144,128]{2,1,0:T(8,128)(2,1)S(1)}, u32[]{:S(2)}, u32[]{:S(2)}) collective-permute-start(bf16[4,144,128]{2,1,0:T(8,128)(2,1)S(1)} %get-tuple-element.70), channel_id=1, source_target_pairs={{0,12},{4,0},{8,4},{12,8},{1,13},{5,1},{9,5},{13,9},{2,14},{6,2},{... | collective-permute-start | bytes 442376 | tf_op jit(solution)/shard_map/ppermute | solution.py:369
  82.0 14.7 %collective-permute-start.13 = (bf16[2,4,288,128]{3,2,1,0:T(8,128)(2,1)S(1)}, bf16[2,4,288,128]{3,2,1,0:T(8,128)(2,1)S(1)}, u32[]{:S(2)}, u32[]{:S(2)}) collective-permute-start(bf16[2,4,288,128]{3,2,1,0:T(8,128)(2,1)S(1)} %get-tuple-element.59.high), channel_id=1, source_target_pairs={{0,1},{1,2},{2,3},{4,5},{5,6},{6,7},{8,9},{9,10},{10,11},{12,13},{... | collective-permute-start | bytes 1769480 | tf_op jit(solution)/shard_map/ppermute | solution.py:408
  88.1 11.2 %collective-permute-start.14 = (bf16[2,4,288,128]{3,2,1,0:T(8,128)(2,1)S(1)}, bf16[2,4,288,128]{3,2,1,0:T(8,128)(2,1)S(1)}, u32[]{:S(2)}, u32[]{:S(2)}) collective-permute-start(bf16[2,4,288,128]{3,2,1,0:T(8,128)(2,1)S(1)} %get-tuple-element.60.low), channel_id=1, source_target_pairs={{1,0},{2,1},{3,2},{5,4},{6,5},{7,6},{9,8},{10,9},{11,10},{13,12},{... | collective-permute-start | bytes 1769480 | tf_op jit(solution)/shard_map/ppermute | solution.py:407
  90.0 12.0 %collective-permute-start.15 = (bf16[4,144,128]{2,1,0:T(8,128)(2,1)S(1)}, bf16[4,144,128]{2,1,0:T(8,128)(2,1)S(1)}, u32[]{:S(2)}, u32[]{:S(2)}) collective-permute-start(bf16[4,144,128]{2,1,0:T(8,128)(2,1)S(1)} %get-tuple-element.62), channel_id=1, source_target_pairs={{0,4},{4,8},{8,12},{12,0},{1,5},{5,9},{9,13},{13,1},{2,6},{6,10},{... | collective-permute-start | bytes 442376 | tf_op jit(solution)/shard_map/ppermute | solution.py:369
  92.4 12.6 %collective-permute-start.16 = (bf16[4,144,128]{2,1,0:T(8,128)(2,1)S(1)}, bf16[4,144,128]{2,1,0:T(8,128)(2,1)S(1)}, u32[]{:S(2)}, u32[]{:S(2)}) collective-permute-start(bf16[4,144,128]{2,1,0:T(8,128)(2,1)S(1)} %get-tuple-element.63), channel_id=1, source_target_pairs={{0,8},{4,12},{8,0},{12,4},{1,9},{5,13},{9,1},{13,5},{2,10},{6,14},... | collective-permute-start | bytes 442376 | tf_op jit(solution)/shard_map/ppermute | solution.py:369
  96.7 9.6 %collective-permute-start.17 = (bf16[4,144,128]{2,1,0:T(8,128)(2,1)S(1)}, bf16[4,144,128]{2,1,0:T(8,128)(2,1)S(1)}, u32[]{:S(2)}, u32[]{:S(2)}) collective-permute-start(bf16[4,144,128]{2,1,0:T(8,128)(2,1)S(1)} %get-tuple-element.64), channel_id=1, source_target_pairs={{0,12},{4,0},{8,4},{12,8},{1,13},{5,1},{9,5},{13,9},{2,14},{6,2},{... | collective-permute-start | bytes 442376 | tf_op jit(solution)/shard_map/ppermute | solution.py:369

commit v5 on v4

--- a/solution.py
+++ b/solution.py
@@ -399,7 +399,7 @@
         halos = halo_pack(ids, got[group], sides, waits)
         halos = [lax.ppermute(h, "energy", routes[i // 2]) for i, h in enumerate(halos)]
         parts = 1 if group == 0 else 2
-        *sums, sum_done = phonon_sum(got[group], halos, main, edges, parts, [back[-1][0][r] for r in [2]] if back else [])
+        *sums, sum_done = phonon_sum(got[group], halos, main, edges, parts, [back[-1][0][r] for r in [nz // 2]] if back else [got[1][nz - 1]])
         waits = [sum_done]
         back.append([spread(sums[i::parts], range(1, nz)) for i in range(parts)])
 

time: 110 us -> 110 us (level)
  waiting for transfers between devices: 34.5 us -> 44.6 us
  starting transfers between devices: 40.6 us -> 30.7 us
    ppermute x15, waiting for transfers between devices: 23.4 us -> 37.8 us  [around(): lax.ppermute(array, 'momentum', [(i, (i + r) % nz) for i in range(nz)])]
    ppermute x15, starting transfers between devices: 29.6 us -> 19.7 us  [around(): lax.ppermute(array, 'momentum', [(i, (i + r) % nz) for i in range(nz)])]
    ppermute x4, waiting for transfers between devices: 8.51 us -> 4.41 us  [shards(): lax.ppermute(h, 'energy', routes[i // 2])]
  transfers between devices with their start and end apart: 21 -> 21, of which waited for: 13 -> 11; matrix products, arithmetic and copies ran while one was open for 0% -> 0% of each run, Pallas kernels for 26% -> 26%
where the time goes in v5:
time: 110 us; the launch traced here: 109 us
  waiting for transfers between devices  44.6 us (41%)
  Pallas kernels  30.9 us (28%)
  starting transfers between devices  30.7 us (28%)
  local copies, waits for them, and re-layouts  2.26 us (2%)
    ppermute x15, waiting for transfers between devices, around(): lax.ppermute(array, 'momentum', [(i, (i + r) % nz) for i in range(nz)])  37.8 us
    ppermute x15, starting transfers between devices, around(): lax.ppermute(array, 'momentum', [(i, (i + r) % nz) for i in range(nz)])  19.7 us
    pallas_call x2, Pallas kernels, coupling_matrices(): pl.pallas_call(functools.partial(coupling_kernel, slots, skip), grid=(cou...  11.3 us
    pallas_call x2, Pallas kernels, phonon_sum(): pl.pallas_call(functools.partial(sum_kernel, nz, sides, parts), out_shape...  6.5 us
    ppermute x1, starting transfers between devices, shards(): before = lax.ppermute(high, 'atom', [(i, i + 1) for i in range(ny - 1)])  6.03 us
    pallas_call x2, Pallas kernels, apply_couplings(): pl.pallas_call(functools.partial(apply_kernel, nz, c), out_shape=jax.Shap...  5.36 us
    ppermute x4, waiting for transfers between devices, shards(): lax.ppermute(h, 'energy', routes[i // 2])  4.41 us
    pallas_call x1, Pallas kernels, tables(): pl.pallas_call(functools.partial(table_kernel, nz, k, energies, sides), o...  4.37 us
  transfers between devices with their start and end apart: 21, of which 11 were waited for; matrix products, arithmetic and copies ran while one was open for 0% of the time, Pallas kernels for 26%

profile of v5, /device:TPU:9, one launch (start us, length us, event | category | flops | bytes accessed | tf_op | source)
XLA Modules:
  0.0 109.3 jit_solution(16003733552431116955)
XLA Ops:
  0.0 0.0 copy-start.2
  0.0 0.0 copy-start.3
  0.0 0.1 pad_add_fusion.ids
  0.4 1.3 %dynamic-slice_bitcast_fusion = (bf16[4,288,128]{2,1,0:T(8,128)(2,1)S(1)}, bf16[4,288,128]{2,1,0:T(8,128)(2,1)S(1)}, bf16[4,288,128]{2,1,0:T(8,128)(2,1)S(1)}, bf16[4,288,128]{2,1,0:T(8,128)(2,1)S(1)}) fusion(bf16[4,8,288,128]{3,2,1,0:T(8,128)(2,1)} %green, s32[]{:T(128)S(6)} %select_n.49, s32[]{:T(128)S(6)} %select_n.46, s32[]{:T(128)S(6)} %select_n.43, ...), kind=kLoop, calls=%fused_computation | loop fusion | bytes 2359312 | tf_op jit(solution)/shard_map/jit(dynamic_index_in_dim)/squeeze | solution.py:379
  1.7 0.1 collective-permute-start.2
  1.8 2.5 %collective-permute-start.1 = (bf16[4,288,128]{2,1,0:T(8,128)(2,1)S(1)}, bf16[4,288,128]{2,1,0:T(8,128)(2,1)S(1)}, u32[]{:S(2)}, u32[]{:S(2)}) collective-permute-start(bf16[4,288,128]{2,1,0:T(8,128)(2,1)S(1)} %get-tuple-element.72), channel_id=1, source_target_pairs={{0,8},{4,12},{8,0},{12,4},{1,9},{5,13},{9,1},{13,5},{2,10},{6,14},... | collective-permute-start | bytes 884744 | tf_op jit(solution)/shard_map/ppermute | solution.py:369
  4.2 2.2 %collective-permute-start = (bf16[4,288,128]{2,1,0:T(8,128)(2,1)S(1)}, bf16[4,288,128]{2,1,0:T(8,128)(2,1)S(1)}, u32[]{:S(2)}, u32[]{:S(2)}) collective-permute-start(bf16[4,288,128]{2,1,0:T(8,128)(2,1)S(1)} %get-tuple-element.73), channel_id=1, source_target_pairs={{0,4},{4,8},{8,12},{12,0},{1,5},{5,9},{9,13},{13,1},{2,6},{6,10},{... | collective-permute-start | bytes 884744 | tf_op jit(solution)/shard_map/ppermute | solution.py:369
  6.4 0.0 copy-done.4
  6.5 0.0 copy-done.5
  6.5 0.0 copy-done.2
  6.5 0.0 copy-start.1
  6.5 0.9 copy-done.1
  7.4 5.6 %shard_map.64 = (bf16[4,144,720]{2,1,0:T(8,128)(2,1)S(1)}, f32[8,128]{1,0:T(8,128)S(1)}) custom-call(s32[3]{0:T(128)S(1)} %pad_add_fusion.ids, s32[8,8]{1,0:T(8,128)S(1)} %copy-done.2, bf16[8,96,12]{2,1,0:T(8,128)(2,1)S(1)} %bitcast.22, bf16[4,288,128]{2,1,0:T(8,128)(2,1)S(1)} %get-tuple-element.74.wait.refs_0_), custom_call_target="tpu_custom_call" | custom-call | tf_op jit(solution)/shard_map/pallas_call | solution.py:260
  13.0 5.7 %shard_map.65 = (bf16[4,144,720]{2,1,0:T(8,128)(2,1)S(1)}, f32[8,128]{1,0:T(8,128)S(1)}) custom-call(s32[3]{0:T(128)S(1)} %pad_add_fusion.ids, s32[8,8]{1,0:T(8,128)S(1)} %copy-done.2, bf16[8,96,12]{2,1,0:T(8,128)(2,1)S(1)} %bitcast.23, f32[8,128]{1,0:T(8,128)S(1)} %get-tuple-element.40.wait), custom_call_target="tpu_custom_call" | custom-call | tf_op jit(solution)/shard_map/pallas_call | solution.py:260
  18.7 0.0 copy-done.3
  18.7 4.4 %shard_map.66 = (bf16[3840,256]{1,0:T(8,128)(2,1)S(1)}, bf16[2,896,256]{2,1,0:T(8,128)(2,1)S(1)}, f32[8,128]{1,0:T(8,128)S(1)}) custom-call(s32[16]{0:T(128)S(1)} %copy-done.3, f32[16,16]{1,0:T(8,128)S(1)} %convert_element_type.6.emit_ref, f32[16,16]{1,0:T(8,128)S(1)} %convert_element_type.7.absorb_ref, s32[3]{0:T(128)S(1)} %pad_add_fusion.ids, ...), custom_call_target="tpu_custom_call" | custom-call | tf_op jit(solution)/shard_map/pallas_call | solution.py:156
  23.1 0.0 copy-done
  23.1 0.7 shard_map.68
  23.8 0.1 collective-permute-start.5
  23.9 1.5 %collective-permute-start.9 = (bf16[4,288,128]{2,1,0:T(8,128)(2,1)S(1)}, bf16[4,288,128]{2,1,0:T(8,128)(2,1)S(1)}, u32[]{:S(2)}, u32[]{:S(2)}) collective-permute-start(bf16[4,288,128]{2,1,0:T(8,128)(2,1)S(1)} %get-tuple-element.53), channel_id=1, source_target_pairs={{0,4},{4,8},{8,12},{12,0},{1,5},{5,9},{9,13},{13,1},{2,6},{6,10},{... | collective-permute-start | bytes 884744 | tf_op jit(solution)/shard_map/ppermute | solution.py:369
  25.3 0.0 collective-permute-done.2.refs_3_
  25.3 2.7 %collective-permute-start.10 = (bf16[4,288,128]{2,1,0:T(8,128)(2,1)S(1)}, bf16[4,288,128]{2,1,0:T(8,128)(2,1)S(1)}, u32[]{:S(2)}, u32[]{:S(2)}) collective-permute-start(bf16[4,288,128]{2,1,0:T(8,128)(2,1)S(1)} %get-tuple-element.54), channel_id=1, source_target_pairs={{0,8},{4,12},{8,0},{12,4},{1,9},{5,13},{9,1},{13,5},{2,10},{6,14},... | collective-permute-start | bytes 884744 | tf_op jit(solution)/shard_map/ppermute | solution.py:369
  28.0 0.0 collective-permute-done.1.refs_2_
  28.0 7.5 %collective-permute-done.refs_1_ = bf16[4,288,128]{2,1,0:T(8,128)(2,1)S(1)} collective-permute-done((bf16[4,288,128]{2,1,0:T(8,128)(2,1)S(1)}, bf16[4,288,128]{2,1,0:T(8,128)(2,1)S(1)}, u32[]{:S(2)}, u32[]{:S(2)}) %collective-permute-start) | collective-permute-done | bytes 294944 | tf_op jit(solution)/shard_map/ppermute | solution.py:369
  35.5 1.0 shard_map.67
  36.5 1.3 %collective-permute-start.3 = (bf16[2,288,128]{2,1,0:T(8,128)(2,1)S(1)}, bf16[2,288,128]{2,1,0:T(8,128)(2,1)S(1)}, u32[]{:S(2)}, u32[]{:S(2)}) collective-permute-start(bf16[2,288,128]{2,1,0:T(8,128)(2,1)S(1)} %get-tuple-element.43), channel_id=1, source_target_pairs={{0,16},{16,0},{1,17},{17,1},{2,18},{18,2},{3,19},{19,3},{4,20},{20... | collective-permute-start | bytes 442376 | tf_op jit(solution)/shard_map/ppermute | solution.py:400
  37.8 0.3 collective-permute-start.4
  38.1 9.5 %collective-permute-done.5.refs_8_.refs_3_ = bf16[4,288,128]{2,1,0:T(8,128)(2,1)S(1)} collective-permute-done((bf16[4,288,128]{2,1,0:T(8,128)(2,1)S(1)}, bf16[4,288,128]{2,1,0:T(8,128)(2,1)S(1)}, u32[]{:S(2)}, u32[]{:S(2)}) %collective-permute-start.5) | collective-permute-done | bytes 294944 | tf_op jit(solution)/shard_map/ppermute | solution.py:369
  47.6 0.0 collective-permute-done.3.refs_4_
  47.6 0.0 collective-permute-done.4.refs_5_
  47.6 3.2 %shard_map.69 = (bf16[4,288,128]{2,1,0:T(8,128)(2,1)S(1)}, bf16[4,288,128]{2,1,0:T(8,128)(2,1)S(1)}, bf16[4,288,128]{2,1,0:T(8,128)(2,1)S(1)}, bf16[4,288,128]{2,1,0:T(8,128)(2,1)S(1)}, f32[8,128]{1,0:T(8,128)S(1)}) custom-call(bf16[4,288,128]{2,1,0:T(8,128)(2,1)S(1)} %get-tuple-element.74.wait.refs_0_, ...), custom_call_target="tpu_custom_call" | custom-call | tf_op jit(solution)/shard_map/pallas_call | solution.py:207
  50.9 0.1 collective-permute-start.7
  51.0 0.1 collective-permute-start.6
  51.0 1.5 %collective-permute-start.8 = (bf16[4,288,128]{2,1,0:T(8,128)(2,1)S(1)}, bf16[4,288,128]{2,1,0:T(8,128)(2,1)S(1)}, u32[]{:S(2)}, u32[]{:S(2)}) collective-permute-start(bf16[4,288,128]{2,1,0:T(8,128)(2,1)S(1)} %get-tuple-element.51), channel_id=1, source_target_pairs={{0,12},{4,0},{8,4},{12,8},{1,13},{5,1},{9,5},{13,9},{2,14},{6,2},{... | collective-permute-start | bytes 884744 | tf_op jit(solution)/shard_map/ppermute | solution.py:369
  52.5 0.0 collective-permute-done.9.refs_1_
  52.5 7.5 %collective-permute-done.10.refs_2_ = bf16[4,288,128]{2,1,0:T(8,128)(2,1)S(1)} collective-permute-done((bf16[4,288,128]{2,1,0:T(8,128)(2,1)S(1)}, bf16[4,288,128]{2,1,0:T(8,128)(2,1)S(1)}, u32[]{:S(2)}, u32[]{:S(2)}) %collective-permute-start.10) | collective-permute-done | bytes 294944 | tf_op jit(solution)/shard_map/ppermute | solution.py:369
  60.0 1.0 shard_map.70
  61.0 1.3 %collective-permute-start.11 = (bf16[2,288,128]{2,1,0:T(8,128)(2,1)S(1)}, bf16[2,288,128]{2,1,0:T(8,128)(2,1)S(1)}, u32[]{:S(2)}, u32[]{:S(2)}) collective-permute-start(bf16[2,288,128]{2,1,0:T(8,128)(2,1)S(1)} %get-tuple-element.56), channel_id=1, source_target_pairs={{0,16},{16,0},{1,17},{17,1},{2,18},{18,2},{3,19},{19,3},{4,20},{20... | collective-permute-start | bytes 442376 | tf_op jit(solution)/shard_map/ppermute | solution.py:400
  62.2 0.3 collective-permute-start.12
  62.5 2.8 %collective-permute-done.11.refs_4_ = bf16[2,288,128]{2,1,0:T(8,128)(2,1)S(1)} collective-permute-done((bf16[2,288,128]{2,1,0:T(8,128)(2,1)S(1)}, bf16[2,288,128]{2,1,0:T(8,128)(2,1)S(1)}, u32[]{:S(2)}, u32[]{:S(2)}) %collective-permute-start.11) | collective-permute-done | bytes 147488 | tf_op jit(solution)/shard_map/ppermute | solution.py:400
  65.3 1.6 %collective-permute-done.12.refs_5_ = bf16[2,288,128]{2,1,0:T(8,128)(2,1)S(1)} collective-permute-done((bf16[2,288,128]{2,1,0:T(8,128)(2,1)S(1)}, bf16[2,288,128]{2,1,0:T(8,128)(2,1)S(1)}, u32[]{:S(2)}, u32[]{:S(2)}) %collective-permute-start.12) | collective-permute-done | bytes 147488 | tf_op jit(solution)/shard_map/ppermute | solution.py:400
  66.9 6.6 %collective-permute-done.7.refs_8_.refs_2_ = bf16[4,288,128]{2,1,0:T(8,128)(2,1)S(1)} collective-permute-done((bf16[4,288,128]{2,1,0:T(8,128)(2,1)S(1)}, bf16[4,288,128]{2,1,0:T(8,128)(2,1)S(1)}, u32[]{:S(2)}, u32[]{:S(2)}) %collective-permute-start.7) | collective-permute-done | bytes 294944 | tf_op jit(solution)/shard_map/ppermute | solution.py:369
  73.5 3.2 %shard_map.71 = (bf16[4,144,128]{2,1,0:T(8,128)(2,1)S(1)}, bf16[4,144,128]{2,1,0:T(8,128)(2,1)S(1)}, bf16[4,144,128]{2,1,0:T(8,128)(2,1)S(1)}, bf16[4,144,128]{2...) custom-call(bf16[4,288,128]{2,1,0:T(8,128)(2,1)S(1)} %get-tuple-elem, ...), custom_call_target="tpu_custom_call" | custom-call | tf_op jit(solution)/shard_map/pallas_call | solution.py:207
  76.7 0.1 collective-permute-start.18
  76.8 3.2 %collective-permute-start.19 = (bf16[4,144,128]{2,1,0:T(8,128)(2,1)S(1)}, bf16[4,144,128]{2,1,0:T(8,128)(2,1)S(1)}, u32[]{:S(2)}, u32[]{:S(2)}) collective-permute-start(bf16[4,144,128]{2,1,0:T(8,128)(2,1)S(1)} %get-tuple-element.69), channel_id=1, source_target_pairs={{0,8},{4,12},{8,0},{12,4},{1,9},{5,13},{9,1},{13,5},{2,10},{6,14},... | collective-permute-start | bytes 442376 | tf_op jit(solution)/shard_map/ppermute | solution.py:369
  80.0 1.4 %collective-permute-start.20 = (bf16[4,144,128]{2,1,0:T(8,128)(2,1)S(1)}, bf16[4,144,128]{2,1,0:T(8,128)(2,1)S(1)}, u32[]{:S(2)}, u32[]{:S(2)}) collective-permute-start(bf16[4,144,128]{2,1,0:T(8,128)(2,1)S(1)} %get-tuple-element.70), channel_id=1, source_target_pairs={{0,12},{4,0},{8,4},{12,8},{1,13},{5,1},{9,5},{13,9},{2,14},{6,2},{... | collective-permute-start | bytes 442376 | tf_op jit(solution)/shard_map/ppermute | solution.py:369
  81.4 0.0 collective-permute-done.6.refs_1_
  81.4 0.0 collective-permute-done.8.refs_3_
  81.4 0.7 shard_map.72
  82.1 6.0 %collective-permute-start.13 = (bf16[2,4,288,128]{3,2,1,0:T(8,128)(2,1)S(1)}, bf16[2,4,288,128]{3,2,1,0:T(8,128)(2,1)S(1)}, u32[]{:S(2)}, u32[]{:S(2)}) collective-permute-start(bf16[2,4,288,128]{3,2,1,0:T(8,128)(2,1)S(1)} %get-tuple-element.59.high), channel_id=1, source_target_pairs={{0,1},{1,2},{2,3},{4,5},{5,6},{6,7},{8,9},{9,10},{10,11},{12,13},{... | collective-permute-start | bytes 1769480 | tf_op jit(solution)/shard_map/ppermute | solution.py:408
  88.1 1.9 %collective-permute-start.14 = (bf16[2,4,288,128]{3,2,1,0:T(8,128)(2,1)S(1)}, bf16[2,4,288,128]{3,2,1,0:T(8,128)(2,1)S(1)}, u32[]{:S(2)}, u32[]{:S(2)}) collective-permute-start(bf16[2,4,288,128]{3,2,1,0:T(8,128)(2,1)S(1)} %get-tuple-element.60.low), channel_id=1, source_target_pairs={{1,0},{2,1},{3,2},{5,4},{6,5},{7,6},{9,8},{10,9},{11,10},{13,12},{... | collective-permute-start | bytes 1769480 | tf_op jit(solution)/shard_map/ppermute | solution.py:407
  90.0 0.0 collective-permute-done.18.refs_0_.refs_1_
  90.0 1.4 %collective-permute-start.15 = (bf16[4,144,128]{2,1,0:T(8,128)(2,1)S(1)}, bf16[4,144,128]{2,1,0:T(8,128)(2,1)S(1)}, u32[]{:S(2)}, u32[]{:S(2)}) collective-permute-start(bf16[4,144,128]{2,1,0:T(8,128)(2,1)S(1)} %get-tuple-element.62), channel_id=1, source_target_pairs={{0,4},{4,8},{8,12},{12,0},{1,5},{5,9},{9,13},{13,1},{2,6},{6,10},{... | collective-permute-start | bytes 442376 | tf_op jit(solution)/shard_map/ppermute | solution.py:369
  91.5 1.0 collective-permute-done.19.refs_1_.refs_2_
  92.5 3.1 %collective-permute-start.16 = (bf16[4,144,128]{2,1,0:T(8,128)(2,1)S(1)}, bf16[4,144,128]{2,1,0:T(8,128)(2,1)S(1)}, u32[]{:S(2)}, u32[]{:S(2)}) collective-permute-start(bf16[4,144,128]{2,1,0:T(8,128)(2,1)S(1)} %get-tuple-element.63), channel_id=1, source_target_pairs={{0,8},{4,12},{8,0},{12,4},{1,9},{5,13},{9,1},{13,5},{2,10},{6,14},... | collective-permute-start | bytes 442376 | tf_op jit(solution)/shard_map/ppermute | solution.py:369
  95.6 1.3 %collective-permute-done.20.refs_2_.refs_3_ = bf16[4,144,128]{2,1,0:T(8,128)(2,1)S(1)} collective-permute-done((bf16[4,144,128]{2,1,0:T(8,128)(2,1)S(1)}, bf16[4,144,128]{2,1,0:T(8,128)(2,1)S(1)}, u32[]{:S(2)}, u32[]{:S(2)}) %collective-permute-start.20) | collective-permute-done | bytes 147488 | tf_op jit(solution)/shard_map/ppermute | solution.py:369
  96.9 0.0 collective-permute-start.17
  96.9 0.0 collective-permute-done.13.before
  96.9 2.4 %collective-permute-done.14.after = bf16[2,4,288,128]{3,2,1,0:T(8,128)(2,1)S(1)} collective-permute-done((bf16[2,4,288,128]{3,2,1,0:T(8,128)(2,1)S(1)}, bf16[2,4,288,128]{3,2,1,0:T(8,128)(2,1)S(1)}, u32[]{:S(2)}, u32[]{:S(2)}) %collective-permute-start.14) | collective-permute-done | bytes 589856 | tf_op jit(solution)/shard_map/ppermute | solution.py:407
  99.3 2.7 %shard_map.74.refs_6_ = f32[4,8,288,128]{3,2,1,0:T(8,128)} custom-call(s32[3]{0:T(128)S(1)} %pad_add_fusion.ids, bf16[2,4,288,128]{3,2,1,0:T(8,128)(2,1)S(1)} %collective-permute-done.13.before, bf16[2,4,288,128]{3,2,1,0:T(8,128)(2,1)S(1)} %get-tuple-element.60.low, bf16[2,4,288,128]{3,2,1,0:T(8,128)(2,1)S(1)} %get-tuple-element.59.high, ...), custom_call_target="tpu_custom_call" | custom-call | tf_op jit(solution)/shard_map/pallas_call | solution.py:345
  102.0 0.0 collective-permute-done.15.refs_1_
  102.0 3.1 %collective-permute-done.16.refs_2_ = bf16[4,144,128]{2,1,0:T(8,128)(2,1)S(1)} collective-permute-done((bf16[4,144,128]{2,1,0:T(8,128)(2,1)S(1)}, bf16[4,144,128]{2,1,0:T(8,128)(2,1)S(1)}, u32[]{:S(2)}, u32[]{:S(2)}) %collective-permute-start.16) | collective-permute-done | bytes 147488 | tf_op jit(solution)/shard_map/ppermute | solution.py:369
  105.1 1.3 %collective-permute-done.17.refs_3_ = bf16[4,144,128]{2,1,0:T(8,128)(2,1)S(1)} collective-permute-done((bf16[4,144,128]{2,1,0:T(8,128)(2,1)S(1)}, bf16[4,144,128]{2,1,0:T(8,128)(2,1)S(1)}, u32[]{:S(2)}, u32[]{:S(2)}) %collective-permute-start.17) | collective-permute-done | bytes 147488 | tf_op jit(solution)/shard_map/ppermute | solution.py:369
  106.4 2.7 %shard_map.75 = f32[4,8,288,128]{3,2,1,0:T(8,128)} custom-call(s32[3]{0:T(128)S(1)} %pad_add_fusion.ids, bf16[2,4,288,128]{3,2,1,0:T(8,128)(2,1)S(1)} %collective-permute-done.13.before, bf16[2,4,288,128]{3,2,1,0:T(8,128)(2,1)S(1)} %get-tuple-element.60.low, bf16[2,4,288,128]{3,2,1,0:T(8,128)(2,1)S(1)} %get-tuple-element.59.high, ...), custom_call_target="tpu_custom_call", output_to_operand_aliasing={{}: (11, {})} | custom-call | tf_op jit(solution)/shard_map/pallas_call | solution.py:345
  (6 shorter events, 0.0 us)
Async XLA Ops:
  0.0 23.1 %copy-start = (bf16[4,8,288,128]{3,2,1,0:T(8,128)(2,1)S(1)}, bf16[4,8,288,128]{3,2,1,0:T(8,128)(2,1)}, u32[]{:S(2)}) copy-start(bf16[4,8,288,128]{3,2,1,0:T(8,128)(2,1)} %green) | copy-start | bytes 7077892
  0.0 6.4 %copy-start.4 = (bf16[16,16]{1,0:T(8,128)(2,1)S(1)}, bf16[16,16]{1,0:T(8,128)(2,1)}, u32[]{:S(2)}) copy-start(bf16[16,16]{1,0:T(8,128)(2,1)} %param.9) | copy-start | bytes 1540
  0.0 6.4 %copy-start.5 = (bf16[16,16]{1,0:T(8,128)(2,1)S(1)}, bf16[16,16]{1,0:T(8,128)(2,1)}, u32[]{:S(2)}) copy-start(bf16[16,16]{1,0:T(8,128)(2,1)} %param.10) | copy-start | bytes 1540
  0.0 6.5 %copy-start.2 = (s32[8,8]{1,0:T(8,128)S(1)}, s32[8,8]{1,0:T(8,128)}, u32[]{:S(2)}) copy-start(s32[8,8]{1,0:T(8,128)} %near_ref.3) | copy-start | bytes 772
  0.0 18.7 %copy-start.3 = (s32[16]{0:T(128)S(1)}, s32[16]{0:T(128)}, u32[]{:S(2)}) copy-start(s32[16]{0:T(128)} %off_ref.1) | copy-start | bytes 196
  1.7 23.6 %collective-permute-start.2 = (bf16[4,288,128]{2,1,0:T(8,128)(2,1)S(1)}, bf16[4,288,128]{2,1,0:T(8,128)(2,1)S(1)}, u32[]{:S(2)}, u32[]{:S(2)}) collective-permute-start(bf16[4,288,128]{2,1,0:T(8,128)(2,1)S(1)} %get-tuple-element.71), channel_id=1, source_target_pairs={{0,12},{4,0},{8,4},{12,8},{1,13},{5,1},{9,5},{13,9},{2,14},{6,2},{... | collective-permute-start | bytes 884744 | tf_op jit(solution)/shard_map/ppermute | solution.py:369
  1.8 26.3 %collective-permute-start.1 = (bf16[4,288,128]{2,1,0:T(8,128)(2,1)S(1)}, bf16[4,288,128]{2,1,0:T(8,128)(2,1)S(1)}, u32[]{:S(2)}, u32[]{:S(2)}) collective-permute-start(bf16[4,288,128]{2,1,0:T(8,128)(2,1)S(1)} %get-tuple-element.72), channel_id=1, source_target_pairs={{0,8},{4,12},{8,0},{12,4},{1,9},{5,13},{9,1},{13,5},{2,10},{6,14},... | collective-permute-start | bytes 884744 | tf_op jit(solution)/shard_map/ppermute | solution.py:369
  4.2 31.3 %collective-permute-start = (bf16[4,288,128]{2,1,0:T(8,128)(2,1)S(1)}, bf16[4,288,128]{2,1,0:T(8,128)(2,1)S(1)}, u32[]{:S(2)}, u32[]{:S(2)}) collective-permute-start(bf16[4,288,128]{2,1,0:T(8,128)(2,1)S(1)} %get-tuple-element.73), channel_id=1, source_target_pairs={{0,4},{4,8},{8,12},{12,0},{1,5},{5,9},{9,13},{13,1},{2,6},{6,10},{... | collective-permute-start | bytes 884744 | tf_op jit(solution)/shard_map/ppermute | solution.py:369
  6.5 0.9 copy-start.1
  23.8 23.8 %collective-permute-start.5 = (bf16[4,288,128]{2,1,0:T(8,128)(2,1)S(1)}, bf16[4,288,128]{2,1,0:T(8,128)(2,1)S(1)}, u32[]{:S(2)}, u32[]{:S(2)}) collective-permute-start(bf16[4,288,128]{2,1,0:T(8,128)(2,1)S(1)} %get-tuple-element.47), channel_id=1, source_target_pairs={{0,12},{4,0},{8,4},{12,8},{1,13},{5,1},{9,5},{13,9},{2,14},{6,2},{... | collective-permute-start | bytes 884744 | tf_op jit(solution)/shard_map/ppermute | solution.py:369
  23.9 28.6 %collective-permute-start.9 = (bf16[4,288,128]{2,1,0:T(8,128)(2,1)S(1)}, bf16[4,288,128]{2,1,0:T(8,128)(2,1)S(1)}, u32[]{:S(2)}, u32[]{:S(2)}) collective-permute-start(bf16[4,288,128]{2,1,0:T(8,128)(2,1)S(1)} %get-tuple-element.53), channel_id=1, source_target_pairs={{0,4},{4,8},{8,12},{12,0},{1,5},{5,9},{9,13},{13,1},{2,6},{6,10},{... | collective-permute-start | bytes 884744 | tf_op jit(solution)/shard_map/ppermute | solution.py:369
  25.3 34.6 %collective-permute-start.10 = (bf16[4,288,128]{2,1,0:T(8,128)(2,1)S(1)}, bf16[4,288,128]{2,1,0:T(8,128)(2,1)S(1)}, u32[]{:S(2)}, u32[]{:S(2)}) collective-permute-start(bf16[4,288,128]{2,1,0:T(8,128)(2,1)S(1)} %get-tuple-element.54), channel_id=1, source_target_pairs={{0,8},{4,12},{8,0},{12,4},{1,9},{5,13},{9,1},{13,5},{2,10},{6,14},... | collective-permute-start | bytes 884744 | tf_op jit(solution)/shard_map/ppermute | solution.py:369
  36.5 11.1 %collective-permute-start.3 = (bf16[2,288,128]{2,1,0:T(8,128)(2,1)S(1)}, bf16[2,288,128]{2,1,0:T(8,128)(2,1)S(1)}, u32[]{:S(2)}, u32[]{:S(2)}) collective-permute-start(bf16[2,288,128]{2,1,0:T(8,128)(2,1)S(1)} %get-tuple-element.43), channel_id=1, source_target_pairs={{0,16},{16,0},{1,17},{17,1},{2,18},{18,2},{3,19},{19,3},{4,20},{20... | collective-permute-start | bytes 442376 | tf_op jit(solution)/shard_map/ppermute | solution.py:400
  37.8 9.8 %collective-permute-start.4 = (bf16[2,288,128]{2,1,0:T(8,128)(2,1)S(1)}, bf16[2,288,128]{2,1,0:T(8,128)(2,1)S(1)}, u32[]{:S(2)}, u32[]{:S(2)}) collective-permute-start(bf16[2,288,128]{2,1,0:T(8,128)(2,1)S(1)} %get-tuple-element.44), channel_id=1, source_target_pairs={{0,16},{16,0},{1,17},{17,1},{2,18},{18,2},{3,19},{19,3},{4,20},{20... | collective-permute-start | bytes 442376 | tf_op jit(solution)/shard_map/ppermute | solution.py:400
  50.9 22.6 %collective-permute-start.7 = (bf16[4,288,128]{2,1,0:T(8,128)(2,1)S(1)}, bf16[4,288,128]{2,1,0:T(8,128)(2,1)S(1)}, u32[]{:S(2)}, u32[]{:S(2)}) collective-permute-start(bf16[4,288,128]{2,1,0:T(8,128)(2,1)S(1)} %get-tuple-element.50), channel_id=1, source_target_pairs={{0,8},{4,12},{8,0},{12,4},{1,9},{5,13},{9,1},{13,5},{2,10},{6,14},... | collective-permute-start | bytes 884744 | tf_op jit(solution)/shard_map/ppermute | solution.py:369
  51.0 30.4 %collective-permute-start.6 = (bf16[4,288,128]{2,1,0:T(8,128)(2,1)S(1)}, bf16[4,288,128]{2,1,0:T(8,128)(2,1)S(1)}, u32[]{:S(2)}, u32[]{:S(2)}) collective-permute-start(bf16[4,288,128]{2,1,0:T(8,128)(2,1)S(1)} %get-tuple-element.49), channel_id=1, source_target_pairs={{0,4},{4,8},{8,12},{12,0},{1,5},{5,9},{9,13},{13,1},{2,6},{6,10},{... | collective-permute-start | bytes 884744 | tf_op jit(solution)/shard_map/ppermute | solution.py:369
  51.0 30.3 %collective-permute-start.8 = (bf16[4,288,128]{2,1,0:T(8,128)(2,1)S(1)}, bf16[4,288,128]{2,1,0:T(8,128)(2,1)S(1)}, u32[]{:S(2)}, u32[]{:S(2)}) collective-permute-start(bf16[4,288,128]{2,1,0:T(8,128)(2,1)S(1)} %get-tuple-element.51), channel_id=1, source_target_pairs={{0,12},{4,0},{8,4},{12,8},{1,13},{5,1},{9,5},{13,9},{2,14},{6,2},{... | collective-permute-start | bytes 884744 | tf_op jit(solution)/shard_map/ppermute | solution.py:369
  61.0 4.4 %collective-permute-start.11 = (bf16[2,288,128]{2,1,0:T(8,128)(2,1)S(1)}, bf16[2,288,128]{2,1,0:T(8,128)(2,1)S(1)}, u32[]{:S(2)}, u32[]{:S(2)}) collective-permute-start(bf16[2,288,128]{2,1,0:T(8,128)(2,1)S(1)} %get-tuple-element.56), channel_id=1, source_target_pairs={{0,16},{16,0},{1,17},{17,1},{2,18},{18,2},{3,19},{19,3},{4,20},{20... | collective-permute-start | bytes 442376 | tf_op jit(solution)/shard_map/ppermute | solution.py:400
  62.2 4.7 %collective-permute-start.12 = (bf16[2,288,128]{2,1,0:T(8,128)(2,1)S(1)}, bf16[2,288,128]{2,1,0:T(8,128)(2,1)S(1)}, u32[]{:S(2)}, u32[]{:S(2)}) collective-permute-start(bf16[2,288,128]{2,1,0:T(8,128)(2,1)S(1)} %get-tuple-element.57), channel_id=1, source_target_pairs={{0,16},{16,0},{1,17},{17,1},{2,18},{18,2},{3,19},{19,3},{4,20},{20... | collective-permute-start | bytes 442376 | tf_op jit(solution)/shard_map/ppermute | solution.py:400
  76.7 13.3 %collective-permute-start.18 = (bf16[4,144,128]{2,1,0:T(8,128)(2,1)S(1)}, bf16[4,144,128]{2,1,0:T(8,128)(2,1)S(1)}, u32[]{:S(2)}, u32[]{:S(2)}) collective-permute-start(bf16[4,144,128]{2,1,0:T(8,128)(2,1)S(1)} %get-tuple-element.68), channel_id=1, source_target_pairs={{0,4},{4,8},{8,12},{12,0},{1,5},{5,9},{9,13},{13,1},{2,6},{6,10},{... | collective-permute-start | bytes 442376 | tf_op jit(solution)/shard_map/ppermute | solution.py:369
  76.8 15.7 %collective-permute-start.19 = (bf16[4,144,128]{2,1,0:T(8,128)(2,1)S(1)}, bf16[4,144,128]{2,1,0:T(8,128)(2,1)S(1)}, u32[]{:S(2)}, u32[]{:S(2)}) collective-permute-start(bf16[4,144,128]{2,1,0:T(8,128)(2,1)S(1)} %get-tuple-element.69), channel_id=1, source_target_pairs={{0,8},{4,12},{8,0},{12,4},{1,9},{5,13},{9,1},{13,5},{2,10},{6,14},... | collective-permute-start | bytes 442376 | tf_op jit(solution)/shard_map/ppermute | solution.py:369
  80.0 16.9 %collective-permute-start.20 = (bf16[4,144,128]{2,1,0:T(8,128)(2,1)S(1)}, bf16[4,144,128]{2,1,0:T(8,128)(2,1)S(1)}, u32[]{:S(2)}, u32[]{:S(2)}) collective-permute-start(bf16[4,144,128]{2,1,0:T(8,128)(2,1)S(1)} %get-tuple-element.70), channel_id=1, source_target_pairs={{0,12},{4,0},{8,4},{12,8},{1,13},{5,1},{9,5},{13,9},{2,14},{6,2},{... | collective-permute-start | bytes 442376 | tf_op jit(solution)/shard_map/ppermute | solution.py:369
  82.1 14.8 %collective-permute-start.13 = (bf16[2,4,288,128]{3,2,1,0:T(8,128)(2,1)S(1)}, bf16[2,4,288,128]{3,2,1,0:T(8,128)(2,1)S(1)}, u32[]{:S(2)}, u32[]{:S(2)}) collective-permute-start(bf16[2,4,288,128]{3,2,1,0:T(8,128)(2,1)S(1)} %get-tuple-element.59.high), channel_id=1, source_target_pairs={{0,1},{1,2},{2,3},{4,5},{5,6},{6,7},{8,9},{9,10},{10,11},{12,13},{... | collective-permute-start | bytes 1769480 | tf_op jit(solution)/shard_map/ppermute | solution.py:408
  88.1 11.2 %collective-permute-start.14 = (bf16[2,4,288,128]{3,2,1,0:T(8,128)(2,1)S(1)}, bf16[2,4,288,128]{3,2,1,0:T(8,128)(2,1)S(1)}, u32[]{:S(2)}, u32[]{:S(2)}) collective-permute-start(bf16[2,4,288,128]{3,2,1,0:T(8,128)(2,1)S(1)} %get-tuple-element.60.low), channel_id=1, source_target_pairs={{1,0},{2,1},{3,2},{5,4},{6,5},{7,6},{9,8},{10,9},{11,10},{13,12},{... | collective-permute-start | bytes 1769480 | tf_op jit(solution)/shard_map/ppermute | solution.py:407
  90.0 12.0 %collective-permute-start.15 = (bf16[4,144,128]{2,1,0:T(8,128)(2,1)S(1)}, bf16[4,144,128]{2,1,0:T(8,128)(2,1)S(1)}, u32[]{:S(2)}, u32[]{:S(2)}) collective-permute-start(bf16[4,144,128]{2,1,0:T(8,128)(2,1)S(1)} %get-tuple-element.62), channel_id=1, source_target_pairs={{0,4},{4,8},{8,12},{12,0},{1,5},{5,9},{9,13},{13,1},{2,6},{6,10},{... | collective-permute-start | bytes 442376 | tf_op jit(solution)/shard_map/ppermute | solution.py:369
  92.5 12.6 %collective-permute-start.16 = (bf16[4,144,128]{2,1,0:T(8,128)(2,1)S(1)}, bf16[4,144,128]{2,1,0:T(8,128)(2,1)S(1)}, u32[]{:S(2)}, u32[]{:S(2)}) collective-permute-start(bf16[4,144,128]{2,1,0:T(8,128)(2,1)S(1)} %get-tuple-element.63), channel_id=1, source_target_pairs={{0,8},{4,12},{8,0},{12,4},{1,9},{5,13},{9,1},{13,5},{2,10},{6,14},... | collective-permute-start | bytes 442376 | tf_op jit(solution)/shard_map/ppermute | solution.py:369
  96.9 9.6 %collective-permute-start.17 = (bf16[4,144,128]{2,1,0:T(8,128)(2,1)S(1)}, bf16[4,144,128]{2,1,0:T(8,128)(2,1)S(1)}, u32[]{:S(2)}, u32[]{:S(2)}) collective-permute-start(bf16[4,144,128]{2,1,0:T(8,128)(2,1)S(1)} %get-tuple-element.64), channel_id=1, source_target_pairs={{0,12},{4,0},{8,4},{12,8},{1,13},{5,1},{9,5},{13,9},{2,14},{6,2},{... | collective-permute-start | bytes 442376 | tf_op jit(solution)/shard_map/ppermute | solution.py:369

commit v6 on v5

--- a/solution.py
+++ b/solution.py
@@ -390,9 +390,9 @@
     below, done = coupling_matrices(ids, neighbours, coupling, 0, half, got[0][0])
     above, done = coupling_matrices(ids, neighbours, coupling, half, half, done)
 
-    main, *edges, done = tables(offsets, emit_weight, absorb_weight, ids, sides, nz, k, energies, done)
     for group in range(1, groups):
         got.append(send(group, done))
+    main, *edges, done = tables(offsets, emit_weight, absorb_weight, ids, sides, nz, k, energies, done)
     waits = [done]
     back = []
     for group in range(groups):

time: 110 us -> 110 us (level)
  no operation moved by 1% of the time
where the time goes in v6:
time: 110 us
  waiting for transfers between devices  44.7 us (41%)
  Pallas kernels  30.9 us (28%)
  starting transfers between devices  30.7 us (28%)
  local copies, waits for them, and re-layouts  2.49 us (2%)
    ppermute x15, waiting for transfers between devices, around(): lax.ppermute(array, 'momentum', [(i, (i + r) % nz) for i in range(nz)])  38.1 us
    ppermute x15, starting transfers between devices, around(): lax.ppermute(array, 'momentum', [(i, (i + r) % nz) for i in range(nz)])  19.7 us
    pallas_call x2, Pallas kernels, coupling_matrices(): pl.pallas_call(functools.partial(coupling_kernel, slots, skip), grid=(cou...  11.3 us
    pallas_call x2, Pallas kernels, phonon_sum(): pl.pallas_call(functools.partial(sum_kernel, nz, sides, parts), out_shape...  6.5 us
    ppermute x1, starting transfers between devices, shards(): before = lax.ppermute(high, 'atom', [(i, i + 1) for i in range(ny - 1)])  6.03 us
    pallas_call x2, Pallas kernels, apply_couplings(): pl.pallas_call(functools.partial(apply_kernel, nz, c), out_shape=jax.Shap...  5.36 us
    pallas_call x1, Pallas kernels, tables(): pl.pallas_call(functools.partial(table_kernel, nz, k, energies, sides), o...  4.37 us
    ppermute x4, waiting for transfers between devices, shards(): lax.ppermute(h, 'energy', routes[i // 2])  4.11 us
  transfers between devices with their start and end apart: 21, of which 11 were waited for; matrix products, arithmetic and copies ran while one was open for 0% of the time, Pallas kernels for 26%

profile of v6, /device:TPU:9, one launch (start us, length us, event | category | flops | bytes accessed | tf_op | source)
XLA Modules:
  0.0 109.6 jit_solution(1297413516490022825)
XLA Ops:
  0.0 0.1 pad_add_fusion.ids
  0.4 0.0 copy-start.4
  0.4 0.0 copy-start.5
  0.4 0.0 copy-start.3
  0.4 1.5 %dynamic-slice_bitcast_fusion = (bf16[4,288,128]{2,1,0:T(8,128)(2,1)S(1)}, bf16[4,288,128]{2,1,0:T(8,128)(2,1)S(1)}, bf16[4,288,128]{2,1,0:T(8,128)(2,1)S(1)}, bf16[4,288,128]{2,1,0:T(8,128)(2,1)S(1)}) fusion(bf16[4,8,288,128]{3,2,1,0:T(8,128)(2,1)} %green, s32[]{:T(128)S(6)} %select_n.49, s32[]{:T(128)S(6)} %select_n.46, s32[]{:T(128)S(6)} %select_n.43, ...), kind=kLoop, calls=%fused_computation | loop fusion | bytes 2359312 | tf_op jit(solution)/shard_map/jit(dynamic_index_in_dim)/squeeze | solution.py:379
  1.9 0.1 collective-permute-start.2
  2.0 2.5 %collective-permute-start.1 = (bf16[4,288,128]{2,1,0:T(8,128)(2,1)S(1)}, bf16[4,288,128]{2,1,0:T(8,128)(2,1)S(1)}, u32[]{:S(2)}, u32[]{:S(2)}) collective-permute-start(bf16[4,288,128]{2,1,0:T(8,128)(2,1)S(1)} %get-tuple-element.72), channel_id=1, source_target_pairs={{0,8},{4,12},{8,0},{12,4},{1,9},{5,13},{9,1},{13,5},{2,10},{6,14},... | collective-permute-start | bytes 884744 | tf_op jit(solution)/shard_map/ppermute | solution.py:369
  4.5 2.2 %collective-permute-start = (bf16[4,288,128]{2,1,0:T(8,128)(2,1)S(1)}, bf16[4,288,128]{2,1,0:T(8,128)(2,1)S(1)}, u32[]{:S(2)}, u32[]{:S(2)}) collective-permute-start(bf16[4,288,128]{2,1,0:T(8,128)(2,1)S(1)} %get-tuple-element.73), channel_id=1, source_target_pairs={{0,4},{4,8},{8,12},{12,0},{1,5},{5,9},{9,13},{13,1},{2,6},{6,10},{... | collective-permute-start | bytes 884744 | tf_op jit(solution)/shard_map/ppermute | solution.py:369
  6.7 0.0 copy-done.2
  6.7 0.9 copy-done.1
  7.6 5.6 %shard_map.64 = (bf16[4,144,720]{2,1,0:T(8,128)(2,1)S(1)}, f32[8,128]{1,0:T(8,128)S(1)}) custom-call(s32[3]{0:T(128)S(1)} %pad_add_fusion.ids, s32[8,8]{1,0:T(8,128)S(1)} %copy-done.2, bf16[8,96,12]{2,1,0:T(8,128)(2,1)S(1)} %bitcast.22, bf16[4,288,128]{2,1,0:T(8,128)(2,1)S(1)} %get-tuple-element.74.wait.refs_0_), custom_call_target="tpu_custom_call" | custom-call | tf_op jit(solution)/shard_map/pallas_call | solution.py:260
  13.2 5.7 %shard_map.65 = (bf16[4,144,720]{2,1,0:T(8,128)(2,1)S(1)}, f32[8,128]{1,0:T(8,128)S(1)}) custom-call(s32[3]{0:T(128)S(1)} %pad_add_fusion.ids, s32[8,8]{1,0:T(8,128)S(1)} %copy-done.2, bf16[8,96,12]{2,1,0:T(8,128)(2,1)S(1)} %bitcast.23, f32[8,128]{1,0:T(8,128)S(1)} %get-tuple-element.40.wait), custom_call_target="tpu_custom_call" | custom-call | tf_op jit(solution)/shard_map/pallas_call | solution.py:260
  18.9 0.0 copy-done
  18.9 0.7 shard_map.68
  19.6 0.1 collective-permute-start.5
  19.7 1.5 %collective-permute-start.9 = (bf16[4,288,128]{2,1,0:T(8,128)(2,1)S(1)}, bf16[4,288,128]{2,1,0:T(8,128)(2,1)S(1)}, u32[]{:S(2)}, u32[]{:S(2)}) collective-permute-start(bf16[4,288,128]{2,1,0:T(8,128)(2,1)S(1)} %get-tuple-element.53), channel_id=1, source_target_pairs={{0,4},{4,8},{8,12},{12,0},{1,5},{5,9},{9,13},{13,1},{2,6},{6,10},{... | collective-permute-start | bytes 884744 | tf_op jit(solution)/shard_map/ppermute | solution.py:369
  21.1 0.0 copy-done.4
  21.1 0.0 copy-done.5
  21.2 0.0 copy-done.3
  21.2 4.4 %shard_map.66 = (bf16[3840,256]{1,0:T(8,128)(2,1)S(1)}, bf16[2,896,256]{2,1,0:T(8,128)(2,1)S(1)}, f32[8,128]{1,0:T(8,128)S(1)}) custom-call(s32[16]{0:T(128)S(1)} %copy-done.3, f32[16,16]{1,0:T(8,128)S(1)} %convert_element_type.6.emit_ref, f32[16,16]{1,0:T(8,128)S(1)} %convert_element_type.7.absorb_ref, s32[3]{0:T(128)S(1)} %pad_add_fusion.ids, ...), custom_call_target="tpu_custom_call" | custom-call | tf_op jit(solution)/shard_map/pallas_call | solution.py:156
  25.5 0.0 collective-permute-done.2.refs_3_
  25.5 2.8 %collective-permute-start.10 = (bf16[4,288,128]{2,1,0:T(8,128)(2,1)S(1)}, bf16[4,288,128]{2,1,0:T(8,128)(2,1)S(1)}, u32[]{:S(2)}, u32[]{:S(2)}) collective-permute-start(bf16[4,288,128]{2,1,0:T(8,128)(2,1)S(1)} %get-tuple-element.54), channel_id=1, source_target_pairs={{0,8},{4,12},{8,0},{12,4},{1,9},{5,13},{9,1},{13,5},{2,10},{6,14},... | collective-permute-start | bytes 884744 | tf_op jit(solution)/shard_map/ppermute | solution.py:369
  28.3 0.0 collective-permute-done.1.refs_2_
  28.3 7.4 %collective-permute-done.refs_1_ = bf16[4,288,128]{2,1,0:T(8,128)(2,1)S(1)} collective-permute-done((bf16[4,288,128]{2,1,0:T(8,128)(2,1)S(1)}, bf16[4,288,128]{2,1,0:T(8,128)(2,1)S(1)}, u32[]{:S(2)}, u32[]{:S(2)}) %collective-permute-start) | collective-permute-done | bytes 294944 | tf_op jit(solution)/shard_map/ppermute | solution.py:369
  35.8 1.0 shard_map.67
  36.8 1.3 %collective-permute-start.3 = (bf16[2,288,128]{2,1,0:T(8,128)(2,1)S(1)}, bf16[2,288,128]{2,1,0:T(8,128)(2,1)S(1)}, u32[]{:S(2)}, u32[]{:S(2)}) collective-permute-start(bf16[2,288,128]{2,1,0:T(8,128)(2,1)S(1)} %get-tuple-element.43), channel_id=1, source_target_pairs={{0,16},{16,0},{1,17},{17,1},{2,18},{18,2},{3,19},{19,3},{4,20},{20... | collective-permute-start | bytes 442376 | tf_op jit(solution)/shard_map/ppermute | solution.py:400
  38.1 0.3 collective-permute-start.4
  38.3 9.5 %collective-permute-done.5.refs_8_.refs_3_ = bf16[4,288,128]{2,1,0:T(8,128)(2,1)S(1)} collective-permute-done((bf16[4,288,128]{2,1,0:T(8,128)(2,1)S(1)}, bf16[4,288,128]{2,1,0:T(8,128)(2,1)S(1)}, u32[]{:S(2)}, u32[]{:S(2)}) %collective-permute-start.5) | collective-permute-done | bytes 294944 | tf_op jit(solution)/shard_map/ppermute | solution.py:369
  47.8 0.0 collective-permute-done.3.refs_4_
  47.8 0.0 collective-permute-done.4.refs_5_
  47.8 3.2 %shard_map.69 = (bf16[4,288,128]{2,1,0:T(8,128)(2,1)S(1)}, bf16[4,288,128]{2,1,0:T(8,128)(2,1)S(1)}, bf16[4,288,128]{2,1,0:T(8,128)(2,1)S(1)}, bf16[4,288,128]{2,1,0:T(8,128)(2,1)S(1)}, f32[8,128]{1,0:T(8,128)S(1)}) custom-call(bf16[4,288,128]{2,1,0:T(8,128)(2,1)S(1)} %get-tuple-element.74.wait.refs_0_, ...), custom_call_target="tpu_custom_call" | custom-call | tf_op jit(solution)/shard_map/pallas_call | solution.py:207
  51.1 0.1 collective-permute-start.7
  51.2 0.1 collective-permute-start.6
  51.2 1.5 %collective-permute-start.8 = (bf16[4,288,128]{2,1,0:T(8,128)(2,1)S(1)}, bf16[4,288,128]{2,1,0:T(8,128)(2,1)S(1)}, u32[]{:S(2)}, u32[]{:S(2)}) collective-permute-start(bf16[4,288,128]{2,1,0:T(8,128)(2,1)S(1)} %get-tuple-element.51), channel_id=1, source_target_pairs={{0,12},{4,0},{8,4},{12,8},{1,13},{5,1},{9,5},{13,9},{2,14},{6,2},{... | collective-permute-start | bytes 884744 | tf_op jit(solution)/shard_map/ppermute | solution.py:369
  52.7 0.0 collective-permute-done.9.refs_1_
  52.7 5.3 %collective-permute-done.10.refs_2_ = bf16[4,288,128]{2,1,0:T(8,128)(2,1)S(1)} collective-permute-done((bf16[4,288,128]{2,1,0:T(8,128)(2,1)S(1)}, bf16[4,288,128]{2,1,0:T(8,128)(2,1)S(1)}, u32[]{:S(2)}, u32[]{:S(2)}) %collective-permute-start.10) | collective-permute-done | bytes 294944 | tf_op jit(solution)/shard_map/ppermute | solution.py:369
  57.9 1.0 shard_map.70
  59.0 1.3 %collective-permute-start.11 = (bf16[2,288,128]{2,1,0:T(8,128)(2,1)S(1)}, bf16[2,288,128]{2,1,0:T(8,128)(2,1)S(1)}, u32[]{:S(2)}, u32[]{:S(2)}) collective-permute-start(bf16[2,288,128]{2,1,0:T(8,128)(2,1)S(1)} %get-tuple-element.56), channel_id=1, source_target_pairs={{0,16},{16,0},{1,17},{17,1},{2,18},{18,2},{3,19},{19,3},{4,20},{20... | collective-permute-start | bytes 442376 | tf_op jit(solution)/shard_map/ppermute | solution.py:400
  60.2 0.3 collective-permute-start.12
  60.5 2.8 %collective-permute-done.11.refs_4_ = bf16[2,288,128]{2,1,0:T(8,128)(2,1)S(1)} collective-permute-done((bf16[2,288,128]{2,1,0:T(8,128)(2,1)S(1)}, bf16[2,288,128]{2,1,0:T(8,128)(2,1)S(1)}, u32[]{:S(2)}, u32[]{:S(2)}) %collective-permute-start.11) | collective-permute-done | bytes 147488 | tf_op jit(solution)/shard_map/ppermute | solution.py:400
  63.3 1.3 %collective-permute-done.12.refs_5_ = bf16[2,288,128]{2,1,0:T(8,128)(2,1)S(1)} collective-permute-done((bf16[2,288,128]{2,1,0:T(8,128)(2,1)S(1)}, bf16[2,288,128]{2,1,0:T(8,128)(2,1)S(1)}, u32[]{:S(2)}, u32[]{:S(2)}) %collective-permute-start.12) | collective-permute-done | bytes 147488 | tf_op jit(solution)/shard_map/ppermute | solution.py:400
  64.6 9.2 %collective-permute-done.7.refs_8_.refs_2_ = bf16[4,288,128]{2,1,0:T(8,128)(2,1)S(1)} collective-permute-done((bf16[4,288,128]{2,1,0:T(8,128)(2,1)S(1)}, bf16[4,288,128]{2,1,0:T(8,128)(2,1)S(1)}, u32[]{:S(2)}, u32[]{:S(2)}) %collective-permute-start.7) | collective-permute-done | bytes 294944 | tf_op jit(solution)/shard_map/ppermute | solution.py:369
  73.8 3.2 %shard_map.71 = (bf16[4,144,128]{2,1,0:T(8,128)(2,1)S(1)}, bf16[4,144,128]{2,1,0:T(8,128)(2,1)S(1)}, bf16[4,144,128]{2,1,0:T(8,128)(2,1)S(1)}, bf16[4,144,128]{2...) custom-call(bf16[4,288,128]{2,1,0:T(8,128)(2,1)S(1)} %get-tuple-elem, ...), custom_call_target="tpu_custom_call" | custom-call | tf_op jit(solution)/shard_map/pallas_call | solution.py:207
  77.0 0.1 collective-permute-start.18
  77.1 3.2 %collective-permute-start.19 = (bf16[4,144,128]{2,1,0:T(8,128)(2,1)S(1)}, bf16[4,144,128]{2,1,0:T(8,128)(2,1)S(1)}, u32[]{:S(2)}, u32[]{:S(2)}) collective-permute-start(bf16[4,144,128]{2,1,0:T(8,128)(2,1)S(1)} %get-tuple-element.69), channel_id=1, source_target_pairs={{0,8},{4,12},{8,0},{12,4},{1,9},{5,13},{9,1},{13,5},{2,10},{6,14},... | collective-permute-start | bytes 442376 | tf_op jit(solution)/shard_map/ppermute | solution.py:369
  80.3 1.4 %collective-permute-start.20 = (bf16[4,144,128]{2,1,0:T(8,128)(2,1)S(1)}, bf16[4,144,128]{2,1,0:T(8,128)(2,1)S(1)}, u32[]{:S(2)}, u32[]{:S(2)}) collective-permute-start(bf16[4,144,128]{2,1,0:T(8,128)(2,1)S(1)} %get-tuple-element.70), channel_id=1, source_target_pairs={{0,12},{4,0},{8,4},{12,8},{1,13},{5,1},{9,5},{13,9},{2,14},{6,2},{... | collective-permute-start | bytes 442376 | tf_op jit(solution)/shard_map/ppermute | solution.py:369
  81.7 0.0 collective-permute-done.6.refs_1_
  81.7 0.0 collective-permute-done.8.refs_3_
  81.7 0.7 shard_map.72
  82.4 6.0 %collective-permute-start.13 = (bf16[2,4,288,128]{3,2,1,0:T(8,128)(2,1)S(1)}, bf16[2,4,288,128]{3,2,1,0:T(8,128)(2,1)S(1)}, u32[]{:S(2)}, u32[]{:S(2)}) collective-permute-start(bf16[2,4,288,128]{3,2,1,0:T(8,128)(2,1)S(1)} %get-tuple-element.59.high), channel_id=1, source_target_pairs={{0,1},{1,2},{2,3},{4,5},{5,6},{6,7},{8,9},{9,10},{10,11},{12,13},{... | collective-permute-start | bytes 1769480 | tf_op jit(solution)/shard_map/ppermute | solution.py:408
  88.4 1.9 %collective-permute-start.14 = (bf16[2,4,288,128]{3,2,1,0:T(8,128)(2,1)S(1)}, bf16[2,4,288,128]{3,2,1,0:T(8,128)(2,1)S(1)}, u32[]{:S(2)}, u32[]{:S(2)}) collective-permute-start(bf16[2,4,288,128]{3,2,1,0:T(8,128)(2,1)S(1)} %get-tuple-element.60.low), channel_id=1, source_target_pairs={{1,0},{2,1},{3,2},{5,4},{6,5},{7,6},{9,8},{10,9},{11,10},{13,12},{... | collective-permute-start | bytes 1769480 | tf_op jit(solution)/shard_map/ppermute | solution.py:407
  90.4 0.0 collective-permute-done.18.refs_0_.refs_1_
  90.4 1.4 %collective-permute-start.15 = (bf16[4,144,128]{2,1,0:T(8,128)(2,1)S(1)}, bf16[4,144,128]{2,1,0:T(8,128)(2,1)S(1)}, u32[]{:S(2)}, u32[]{:S(2)}) collective-permute-start(bf16[4,144,128]{2,1,0:T(8,128)(2,1)S(1)} %get-tuple-element.62), channel_id=1, source_target_pairs={{0,4},{4,8},{8,12},{12,0},{1,5},{5,9},{9,13},{13,1},{2,6},{6,10},{... | collective-permute-start | bytes 442376 | tf_op jit(solution)/shard_map/ppermute | solution.py:369
  91.8 1.0 collective-permute-done.19.refs_1_.refs_2_
  92.8 3.1 %collective-permute-start.16 = (bf16[4,144,128]{2,1,0:T(8,128)(2,1)S(1)}, bf16[4,144,128]{2,1,0:T(8,128)(2,1)S(1)}, u32[]{:S(2)}, u32[]{:S(2)}) collective-permute-start(bf16[4,144,128]{2,1,0:T(8,128)(2,1)S(1)} %get-tuple-element.63), channel_id=1, source_target_pairs={{0,8},{4,12},{8,0},{12,4},{1,9},{5,13},{9,1},{13,5},{2,10},{6,14},... | collective-permute-start | bytes 442376 | tf_op jit(solution)/shard_map/ppermute | solution.py:369
  95.9 1.3 %collective-permute-done.20.refs_2_.refs_3_ = bf16[4,144,128]{2,1,0:T(8,128)(2,1)S(1)} collective-permute-done((bf16[4,144,128]{2,1,0:T(8,128)(2,1)S(1)}, bf16[4,144,128]{2,1,0:T(8,128)(2,1)S(1)}, u32[]{:S(2)}, u32[]{:S(2)}) %collective-permute-start.20) | collective-permute-done | bytes 147488 | tf_op jit(solution)/shard_map/ppermute | solution.py:369
  97.2 0.0 collective-permute-start.17
  97.2 0.0 collective-permute-done.13.before
  97.2 2.4 %collective-permute-done.14.after = bf16[2,4,288,128]{3,2,1,0:T(8,128)(2,1)S(1)} collective-permute-done((bf16[2,4,288,128]{3,2,1,0:T(8,128)(2,1)S(1)}, bf16[2,4,288,128]{3,2,1,0:T(8,128)(2,1)S(1)}, u32[]{:S(2)}, u32[]{:S(2)}) %collective-permute-start.14) | collective-permute-done | bytes 589856 | tf_op jit(solution)/shard_map/ppermute | solution.py:407
  99.6 2.7 %shard_map.74.refs_6_ = f32[4,8,288,128]{3,2,1,0:T(8,128)} custom-call(s32[3]{0:T(128)S(1)} %pad_add_fusion.ids, bf16[2,4,288,128]{3,2,1,0:T(8,128)(2,1)S(1)} %collective-permute-done.13.before, bf16[2,4,288,128]{3,2,1,0:T(8,128)(2,1)S(1)} %get-tuple-element.60.low, bf16[2,4,288,128]{3,2,1,0:T(8,128)(2,1)S(1)} %get-tuple-element.59.high, ...), custom_call_target="tpu_custom_call" | custom-call | tf_op jit(solution)/shard_map/pallas_call | solution.py:345
  102.3 0.0 collective-permute-done.15.refs_1_
  102.3 3.1 %collective-permute-done.16.refs_2_ = bf16[4,144,128]{2,1,0:T(8,128)(2,1)S(1)} collective-permute-done((bf16[4,144,128]{2,1,0:T(8,128)(2,1)S(1)}, bf16[4,144,128]{2,1,0:T(8,128)(2,1)S(1)}, u32[]{:S(2)}, u32[]{:S(2)}) %collective-permute-start.16) | collective-permute-done | bytes 147488 | tf_op jit(solution)/shard_map/ppermute | solution.py:369
  105.4 1.3 %collective-permute-done.17.refs_3_ = bf16[4,144,128]{2,1,0:T(8,128)(2,1)S(1)} collective-permute-done((bf16[4,144,128]{2,1,0:T(8,128)(2,1)S(1)}, bf16[4,144,128]{2,1,0:T(8,128)(2,1)S(1)}, u32[]{:S(2)}, u32[]{:S(2)}) %collective-permute-start.17) | collective-permute-done | bytes 147488 | tf_op jit(solution)/shard_map/ppermute | solution.py:369
  106.7 2.7 %shard_map.75 = f32[4,8,288,128]{3,2,1,0:T(8,128)} custom-call(s32[3]{0:T(128)S(1)} %pad_add_fusion.ids, bf16[2,4,288,128]{3,2,1,0:T(8,128)(2,1)S(1)} %collective-permute-done.13.before, bf16[2,4,288,128]{3,2,1,0:T(8,128)(2,1)S(1)} %get-tuple-element.60.low, bf16[2,4,288,128]{3,2,1,0:T(8,128)(2,1)S(1)} %get-tuple-element.59.high, ...), custom_call_target="tpu_custom_call", output_to_operand_aliasing={{}: (11, {})} | custom-call | tf_op jit(solution)/shard_map/pallas_call | solution.py:345
  (6 shorter events, 0.0 us)
Async XLA Ops:
  0.0 18.9 %copy-start = (bf16[4,8,288,128]{3,2,1,0:T(8,128)(2,1)S(1)}, bf16[4,8,288,128]{3,2,1,0:T(8,128)(2,1)}, u32[]{:S(2)}) copy-start(bf16[4,8,288,128]{3,2,1,0:T(8,128)(2,1)} %green) | copy-start | bytes 7077892
  0.0 6.7 %copy-start.2 = (s32[8,8]{1,0:T(8,128)S(1)}, s32[8,8]{1,0:T(8,128)}, u32[]{:S(2)}) copy-start(s32[8,8]{1,0:T(8,128)} %near_ref.3) | copy-start | bytes 772
  0.4 20.8 %copy-start.4 = (bf16[16,16]{1,0:T(8,128)(2,1)S(1)}, bf16[16,16]{1,0:T(8,128)(2,1)}, u32[]{:S(2)}) copy-start(bf16[16,16]{1,0:T(8,128)(2,1)} %param.9) | copy-start | bytes 1540
  0.4 20.8 %copy-start.5 = (bf16[16,16]{1,0:T(8,128)(2,1)S(1)}, bf16[16,16]{1,0:T(8,128)(2,1)}, u32[]{:S(2)}) copy-start(bf16[16,16]{1,0:T(8,128)(2,1)} %param.10) | copy-start | bytes 1540
  0.4 20.8 %copy-start.3 = (s32[16]{0:T(128)S(1)}, s32[16]{0:T(128)}, u32[]{:S(2)}) copy-start(s32[16]{0:T(128)} %off_ref.1) | copy-start | bytes 196
  1.9 23.6 %collective-permute-start.2 = (bf16[4,288,128]{2,1,0:T(8,128)(2,1)S(1)}, bf16[4,288,128]{2,1,0:T(8,128)(2,1)S(1)}, u32[]{:S(2)}, u32[]{:S(2)}) collective-permute-start(bf16[4,288,128]{2,1,0:T(8,128)(2,1)S(1)} %get-tuple-element.71), channel_id=1, source_target_pairs={{0,12},{4,0},{8,4},{12,8},{1,13},{5,1},{9,5},{13,9},{2,14},{6,2},{... | collective-permute-start | bytes 884744 | tf_op jit(solution)/shard_map/ppermute | solution.py:369
  2.0 26.3 %collective-permute-start.1 = (bf16[4,288,128]{2,1,0:T(8,128)(2,1)S(1)}, bf16[4,288,128]{2,1,0:T(8,128)(2,1)S(1)}, u32[]{:S(2)}, u32[]{:S(2)}) collective-permute-start(bf16[4,288,128]{2,1,0:T(8,128)(2,1)S(1)} %get-tuple-element.72), channel_id=1, source_target_pairs={{0,8},{4,12},{8,0},{12,4},{1,9},{5,13},{9,1},{13,5},{2,10},{6,14},... | collective-permute-start | bytes 884744 | tf_op jit(solution)/shard_map/ppermute | solution.py:369
  4.5 31.3 %collective-permute-start = (bf16[4,288,128]{2,1,0:T(8,128)(2,1)S(1)}, bf16[4,288,128]{2,1,0:T(8,128)(2,1)S(1)}, u32[]{:S(2)}, u32[]{:S(2)}) collective-permute-start(bf16[4,288,128]{2,1,0:T(8,128)(2,1)S(1)} %get-tuple-element.73), channel_id=1, source_target_pairs={{0,4},{4,8},{8,12},{12,0},{1,5},{5,9},{9,13},{13,1},{2,6},{6,10},{... | collective-permute-start | bytes 884744 | tf_op jit(solution)/shard_map/ppermute | solution.py:369
  6.7 0.9 copy-start.1
  19.6 28.2 %collective-permute-start.5 = (bf16[4,288,128]{2,1,0:T(8,128)(2,1)S(1)}, bf16[4,288,128]{2,1,0:T(8,128)(2,1)S(1)}, u32[]{:S(2)}, u32[]{:S(2)}) collective-permute-start(bf16[4,288,128]{2,1,0:T(8,128)(2,1)S(1)} %get-tuple-element.47), channel_id=1, source_target_pairs={{0,12},{4,0},{8,4},{12,8},{1,13},{5,1},{9,5},{13,9},{2,14},{6,2},{... | collective-permute-start | bytes 884744 | tf_op jit(solution)/shard_map/ppermute | solution.py:369
  19.7 33.0 %collective-permute-start.9 = (bf16[4,288,128]{2,1,0:T(8,128)(2,1)S(1)}, bf16[4,288,128]{2,1,0:T(8,128)(2,1)S(1)}, u32[]{:S(2)}, u32[]{:S(2)}) collective-permute-start(bf16[4,288,128]{2,1,0:T(8,128)(2,1)S(1)} %get-tuple-element.53), channel_id=1, source_target_pairs={{0,4},{4,8},{8,12},{12,0},{1,5},{5,9},{9,13},{13,1},{2,6},{6,10},{... | collective-permute-start | bytes 884744 | tf_op jit(solution)/shard_map/ppermute | solution.py:369
  25.5 32.4 %collective-permute-start.10 = (bf16[4,288,128]{2,1,0:T(8,128)(2,1)S(1)}, bf16[4,288,128]{2,1,0:T(8,128)(2,1)S(1)}, u32[]{:S(2)}, u32[]{:S(2)}) collective-permute-start(bf16[4,288,128]{2,1,0:T(8,128)(2,1)S(1)} %get-tuple-element.54), channel_id=1, source_target_pairs={{0,8},{4,12},{8,0},{12,4},{1,9},{5,13},{9,1},{13,5},{2,10},{6,14},... | collective-permute-start | bytes 884744 | tf_op jit(solution)/shard_map/ppermute | solution.py:369
  36.8 11.0 %collective-permute-start.3 = (bf16[2,288,128]{2,1,0:T(8,128)(2,1)S(1)}, bf16[2,288,128]{2,1,0:T(8,128)(2,1)S(1)}, u32[]{:S(2)}, u32[]{:S(2)}) collective-permute-start(bf16[2,288,128]{2,1,0:T(8,128)(2,1)S(1)} %get-tuple-element.43), channel_id=1, source_target_pairs={{0,16},{16,0},{1,17},{17,1},{2,18},{18,2},{3,19},{19,3},{4,20},{20... | collective-permute-start | bytes 442376 | tf_op jit(solution)/shard_map/ppermute | solution.py:400
  38.1 9.8 %collective-permute-start.4 = (bf16[2,288,128]{2,1,0:T(8,128)(2,1)S(1)}, bf16[2,288,128]{2,1,0:T(8,128)(2,1)S(1)}, u32[]{:S(2)}, u32[]{:S(2)}) collective-permute-start(bf16[2,288,128]{2,1,0:T(8,128)(2,1)S(1)} %get-tuple-element.44), channel_id=1, source_target_pairs={{0,16},{16,0},{1,17},{17,1},{2,18},{18,2},{3,19},{19,3},{4,20},{20... | collective-permute-start | bytes 442376 | tf_op jit(solution)/shard_map/ppermute | solution.py:400
  51.1 22.7 %collective-permute-start.7 = (bf16[4,288,128]{2,1,0:T(8,128)(2,1)S(1)}, bf16[4,288,128]{2,1,0:T(8,128)(2,1)S(1)}, u32[]{:S(2)}, u32[]{:S(2)}) collective-permute-start(bf16[4,288,128]{2,1,0:T(8,128)(2,1)S(1)} %get-tuple-element.50), channel_id=1, source_target_pairs={{0,8},{4,12},{8,0},{12,4},{1,9},{5,13},{9,1},{13,5},{2,10},{6,14},... | collective-permute-start | bytes 884744 | tf_op jit(solution)/shard_map/ppermute | solution.py:369
  51.2 30.5 %collective-permute-start.6 = (bf16[4,288,128]{2,1,0:T(8,128)(2,1)S(1)}, bf16[4,288,128]{2,1,0:T(8,128)(2,1)S(1)}, u32[]{:S(2)}, u32[]{:S(2)}) collective-permute-start(bf16[4,288,128]{2,1,0:T(8,128)(2,1)S(1)} %get-tuple-element.49), channel_id=1, source_target_pairs={{0,4},{4,8},{8,12},{12,0},{1,5},{5,9},{9,13},{13,1},{2,6},{6,10},{... | collective-permute-start | bytes 884744 | tf_op jit(solution)/shard_map/ppermute | solution.py:369
  51.2 30.4 %collective-permute-start.8 = (bf16[4,288,128]{2,1,0:T(8,128)(2,1)S(1)}, bf16[4,288,128]{2,1,0:T(8,128)(2,1)S(1)}, u32[]{:S(2)}, u32[]{:S(2)}) collective-permute-start(bf16[4,288,128]{2,1,0:T(8,128)(2,1)S(1)} %get-tuple-element.51), channel_id=1, source_target_pairs={{0,12},{4,0},{8,4},{12,8},{1,13},{5,1},{9,5},{13,9},{2,14},{6,2},{... | collective-permute-start | bytes 884744 | tf_op jit(solution)/shard_map/ppermute | solution.py:369
  59.0 4.4 %collective-permute-start.11 = (bf16[2,288,128]{2,1,0:T(8,128)(2,1)S(1)}, bf16[2,288,128]{2,1,0:T(8,128)(2,1)S(1)}, u32[]{:S(2)}, u32[]{:S(2)}) collective-permute-start(bf16[2,288,128]{2,1,0:T(8,128)(2,1)S(1)} %get-tuple-element.56), channel_id=1, source_target_pairs={{0,16},{16,0},{1,17},{17,1},{2,18},{18,2},{3,19},{19,3},{4,20},{20... | collective-permute-start | bytes 442376 | tf_op jit(solution)/shard_map/ppermute | solution.py:400
  60.2 4.4 %collective-permute-start.12 = (bf16[2,288,128]{2,1,0:T(8,128)(2,1)S(1)}, bf16[2,288,128]{2,1,0:T(8,128)(2,1)S(1)}, u32[]{:S(2)}, u32[]{:S(2)}) collective-permute-start(bf16[2,288,128]{2,1,0:T(8,128)(2,1)S(1)} %get-tuple-element.57), channel_id=1, source_target_pairs={{0,16},{16,0},{1,17},{17,1},{2,18},{18,2},{3,19},{19,3},{4,20},{20... | collective-permute-start | bytes 442376 | tf_op jit(solution)/shard_map/ppermute | solution.py:400
  77.0 13.3 %collective-permute-start.18 = (bf16[4,144,128]{2,1,0:T(8,128)(2,1)S(1)}, bf16[4,144,128]{2,1,0:T(8,128)(2,1)S(1)}, u32[]{:S(2)}, u32[]{:S(2)}) collective-permute-start(bf16[4,144,128]{2,1,0:T(8,128)(2,1)S(1)} %get-tuple-element.68), channel_id=1, source_target_pairs={{0,4},{4,8},{8,12},{12,0},{1,5},{5,9},{9,13},{13,1},{2,6},{6,10},{... | collective-permute-start | bytes 442376 | tf_op jit(solution)/shard_map/ppermute | solution.py:369
  77.1 15.7 %collective-permute-start.19 = (bf16[4,144,128]{2,1,0:T(8,128)(2,1)S(1)}, bf16[4,144,128]{2,1,0:T(8,128)(2,1)S(1)}, u32[]{:S(2)}, u32[]{:S(2)}) collective-permute-start(bf16[4,144,128]{2,1,0:T(8,128)(2,1)S(1)} %get-tuple-element.69), channel_id=1, source_target_pairs={{0,8},{4,12},{8,0},{12,4},{1,9},{5,13},{9,1},{13,5},{2,10},{6,14},... | collective-permute-start | bytes 442376 | tf_op jit(solution)/shard_map/ppermute | solution.py:369
  80.3 16.9 %collective-permute-start.20 = (bf16[4,144,128]{2,1,0:T(8,128)(2,1)S(1)}, bf16[4,144,128]{2,1,0:T(8,128)(2,1)S(1)}, u32[]{:S(2)}, u32[]{:S(2)}) collective-permute-start(bf16[4,144,128]{2,1,0:T(8,128)(2,1)S(1)} %get-tuple-element.70), channel_id=1, source_target_pairs={{0,12},{4,0},{8,4},{12,8},{1,13},{5,1},{9,5},{13,9},{2,14},{6,2},{... | collective-permute-start | bytes 442376 | tf_op jit(solution)/shard_map/ppermute | solution.py:369
  82.4 14.8 %collective-permute-start.13 = (bf16[2,4,288,128]{3,2,1,0:T(8,128)(2,1)S(1)}, bf16[2,4,288,128]{3,2,1,0:T(8,128)(2,1)S(1)}, u32[]{:S(2)}, u32[]{:S(2)}) collective-permute-start(bf16[2,4,288,128]{3,2,1,0:T(8,128)(2,1)S(1)} %get-tuple-element.59.high), channel_id=1, source_target_pairs={{0,1},{1,2},{2,3},{4,5},{5,6},{6,7},{8,9},{9,10},{10,11},{12,13},{... | collective-permute-start | bytes 1769480 | tf_op jit(solution)/shard_map/ppermute | solution.py:408
  88.4 11.2 %collective-permute-start.14 = (bf16[2,4,288,128]{3,2,1,0:T(8,128)(2,1)S(1)}, bf16[2,4,288,128]{3,2,1,0:T(8,128)(2,1)S(1)}, u32[]{:S(2)}, u32[]{:S(2)}) collective-permute-start(bf16[2,4,288,128]{3,2,1,0:T(8,128)(2,1)S(1)} %get-tuple-element.60.low), channel_id=1, source_target_pairs={{1,0},{2,1},{3,2},{5,4},{6,5},{7,6},{9,8},{10,9},{11,10},{13,12},{... | collective-permute-start | bytes 1769480 | tf_op jit(solution)/shard_map/ppermute | solution.py:407
  90.4 12.0 %collective-permute-start.15 = (bf16[4,144,128]{2,1,0:T(8,128)(2,1)S(1)}, bf16[4,144,128]{2,1,0:T(8,128)(2,1)S(1)}, u32[]{:S(2)}, u32[]{:S(2)}) collective-permute-start(bf16[4,144,128]{2,1,0:T(8,128)(2,1)S(1)} %get-tuple-element.62), channel_id=1, source_target_pairs={{0,4},{4,8},{8,12},{12,0},{1,5},{5,9},{9,13},{13,1},{2,6},{6,10},{... | collective-permute-start | bytes 442376 | tf_op jit(solution)/shard_map/ppermute | solution.py:369
  92.8 12.6 %collective-permute-start.16 = (bf16[4,144,128]{2,1,0:T(8,128)(2,1)S(1)}, bf16[4,144,128]{2,1,0:T(8,128)(2,1)S(1)}, u32[]{:S(2)}, u32[]{:S(2)}) collective-permute-start(bf16[4,144,128]{2,1,0:T(8,128)(2,1)S(1)} %get-tuple-element.63), channel_id=1, source_target_pairs={{0,8},{4,12},{8,0},{12,4},{1,9},{5,13},{9,1},{13,5},{2,10},{6,14},... | collective-permute-start | bytes 442376 | tf_op jit(solution)/shard_map/ppermute | solution.py:369
  97.2 9.6 %collective-permute-start.17 = (bf16[4,144,128]{2,1,0:T(8,128)(2,1)S(1)}, bf16[4,144,128]{2,1,0:T(8,128)(2,1)S(1)}, u32[]{:S(2)}, u32[]{:S(2)}) collective-permute-start(bf16[4,144,128]{2,1,0:T(8,128)(2,1)S(1)} %get-tuple-element.64), channel_id=1, source_target_pairs={{0,12},{4,0},{8,4},{12,8},{1,13},{5,1},{9,5},{13,9},{2,14},{6,2},{... | collective-permute-start | bytes 442376 | tf_op jit(solution)/shard_map/ppermute | solution.py:369
